TPU v7x, 32 devices: a whole 2x2x4 slice. The times are simulated.
32 devices in a mesh: fsdp: 8 (over z, core), seq: 4 (over y, x).
Axes of the slice: x: 2, y: 2, z: 4, core: 2. Of those that a mesh axis runs over, the one named last changes fastest.
Arguments:
- inputs: bfloat16 [16, 1024, 1152], P('fsdp', 'seq'), may hold values from -24 to 24
- key_mask: int32 [16, 1024], P('fsdp'), may hold values from 0 to 1, as said below
- w_qkv: bfloat16 [1152, 3456], P('fsdp'), may hold values from -1 to 1
- w_out: bfloat16 [1152, 1152], P('fsdp'), may hold values from -2 to 2
- w_up: bfloat16 [1152, 4304], P('fsdp'), may hold values from -0.1875 to 0.1875
- w_down: bfloat16 [4304, 1152], P(None, 'fsdp'), may hold values from -0.09375 to 0.09375
- norm_gains: bfloat16 [2, 1152], P(None, 'fsdp'), may hold values from 0.099609375 to 1.8984375
- biases: bfloat16 [6, 1152], P(None, 'fsdp'), may hold values from -3 to 3
- up_bias: bfloat16 [4304], P('fsdp'), may hold values from -3 to 3
- cotangent: bfloat16 [16, 1024, 1152], P('fsdp', 'seq'), may hold values from -6 to 6
Outputs:
- layer_out: bfloat16 [16, 1024, 1152], P('fsdp', 'seq')
- grad_in: bfloat16 [16, 1024, 1152], P('fsdp', 'seq')
- grad_qkv: float32 [1152, 3456], P('fsdp')
- grad_proj: float32 [1152, 1152], P('fsdp')
- grad_up: float32 [1152, 4304], P('fsdp')
- grad_down: float32 [4304, 1152], P(None, 'fsdp')
- grad_gains: float32 [2, 1152], P(None, 'fsdp')
- grad_biases: float32 [6, 1152], P(None, 'fsdp')
- grad_upbias: float32 [4304], P('fsdp')
Inputs may be any that keep to these rules, and one draw needn't show every extreme that they name: `key_mask`: in each image the live keys are its first L tokens, with L between 512 and 1024; image 0 has L = 512.
All inputs are finite; a program needn't handle non-finite values.
Results may differ from a plain program's by a relative error of at most 0.012.
Values may be sent and summed in bfloat16 or wider, within the bound.
No kernel may reach another device: no remote copies, remote signals or barrier semaphores. Data moves between devices by JAX's collectives and lax.ppermute only.
A program may use at most 256 MiB of HBM per device.

v0:
```python
import functools
import math

import jax
import jax.numpy as jnp
from jax import lax
from jax.experimental import pallas as pl
from jax.experimental.pallas import tpu as pltpu
from jax.sharding import PartitionSpec as P

HEAD_DIM = 72
QBLOCK = 512
EPSILON = 1e-06
NEG_FILL = -1e30
GELU_CUBE = 0.044715
GELU_SCALE = math.sqrt(2.0 / math.pi)
LOG2E = math.log2(math.e)
LANES = 128
F32 = jnp.float32
BF16 = jnp.bfloat16
MIB = 2**20


def attention_forward_kernel(block, heads, qkv_ref, bias_ref, out_ref, probs_ref, inv_ref, by_row, out_rows):
    head = pl.program_id(0)
    width = heads * HEAD_DIM
    seq = qkv_ref.shape[0]

    @pl.when(head == 0)
    def _():
        by_row[...] = qkv_ref[...].astype(F32).T

    def rows(which):
        return pl.ds(pl.multiple_of(which * width + head * HEAD_DIM, 8), HEAD_DIM)

    query = by_row[rows(0), :].astype(BF16)
    keys = by_row[rows(1), :].T.astype(BF16)
    values = by_row[rows(2), :].astype(BF16)
    bias = bias_ref[...]
    for start in range(0, seq, block):
        part = slice(start, start + block)
        scores = jnp.dot(keys, query[:, part], preferred_element_type=F32) * (LOG2E / math.sqrt(HEAD_DIM)) + bias
        top = jnp.max(scores, axis=0, keepdims=True)
        raised = jnp.exp2(scores - top)
        inv = 1.0 / jnp.sum(raised, axis=0, keepdims=True)
        raised_low = raised.astype(BF16)
        probs_ref[0, :, part] = raised_low
        inv_ref[0, :, part] = inv
        out_rows[rows(0), part] = jnp.dot(values, raised_low, preferred_element_type=F32) * inv

    @pl.when(head == heads - 1)
    def _():
        out_ref[:, :width] = out_rows[...].T.astype(BF16)


def attention_forward(qkv, bias, block=QBLOCK):
    seq, triple = qkv.shape
    width = triple // 3
    heads = width // HEAD_DIM
    whole_tiles = -(-width // LANES) * LANES
    return pl.pallas_call(
        functools.partial(attention_forward_kernel, block, heads),
        grid=(heads,),
        in_specs=[pl.BlockSpec((seq, triple), lambda h: (0, 0)), pl.BlockSpec((seq, 1), lambda h: (0, 0))],
        out_specs=[
            pl.BlockSpec((seq, whole_tiles), lambda h: (0, 0)),
            pl.BlockSpec((1, seq, seq), lambda h: (h, 0, 0)),
            pl.BlockSpec((1, 1, seq), lambda h: (h, 0, 0)),
        ],
        out_shape=[
            jax.ShapeDtypeStruct((seq, whole_tiles), BF16),
            jax.ShapeDtypeStruct((heads, seq, seq), BF16),
            jax.ShapeDtypeStruct((heads, 1, seq), F32),
        ],
        scratch_shapes=[pltpu.VMEM((triple, seq), F32), pltpu.VMEM((width, seq), F32)],
        compiler_params=pltpu.CompilerParams(vmem_limit_bytes=48 * MIB),
        cost_estimate=pl.CostEstimate(
            flops=heads * seq * seq, bytes_accessed=seq * triple, transcendentals=0
        ),
    )(qkv, bias)


def attention_backward_kernel(
    block, heads, qkv_ref, d_out_ref, out_ref, probs_ref, inv_ref, grad_ref, by_row, d_rows, o_rows, grad_rows
):
    head = pl.program_id(0)
    width = heads * HEAD_DIM
    seq = qkv_ref.shape[0]
    scale = 1.0 / math.sqrt(HEAD_DIM)

    @pl.when(head == 0)
    def _():
        by_row[...] = qkv_ref[...].astype(F32).T
        d_rows[...] = d_out_ref[...].astype(F32).T
        o_rows[...] = out_ref[:, :width].astype(F32).T

    def rows(which):
        return pl.ds(pl.multiple_of(which * width + head * HEAD_DIM, 8), HEAD_DIM)

    query = by_row[rows(0), :].T.astype(BF16)
    keys = by_row[rows(1), :].astype(BF16)
    values = by_row[rows(2), :].T.astype(BF16)
    d_out = d_rows[rows(0), :]
    inv = inv_ref[0]
    row_dot = jnp.sum(d_out * o_rows[rows(0), :], axis=0, keepdims=True) * inv
    d_scaled = d_out * inv
    d_tokens = d_scaled.T.astype(BF16)
    d_scaled = d_scaled.astype(BF16)
    d_keys = jnp.zeros((seq, HEAD_DIM), F32)
    d_values = jnp.zeros((seq, HEAD_DIM), F32)
    for start in range(0, seq, block):
        part = slice(start, start + block)
        raised = probs_ref[0, :, part]
        d_probs = jnp.dot(values, d_scaled[:, part], preferred_element_type=F32)
        d_scores = (raised.astype(F32) * (d_probs - row_dot[:, part])).astype(BF16)
        d_values += jnp.dot(raised, d_tokens[part, :], preferred_element_type=F32)
        d_keys += jnp.dot(d_scores, query[part, :], preferred_element_type=F32)
        grad_rows[rows(0), part] = jnp.dot(keys, d_scores, preferred_element_type=F32) * scale
    grad_rows[rows(1), :] = d_keys.T * scale
    grad_rows[rows(2), :] = d_values.T

    @pl.when(head == heads - 1)
    def _():
        grad_ref[...] = grad_rows[...].T.astype(BF16)


def attention_backward(qkv, d_out, out, probs, inv, block=QBLOCK):
    seq, triple = qkv.shape
    width = triple // 3
    heads = width // HEAD_DIM
    whole = lambda h: (0, 0)
    return pl.pallas_call(
        functools.partial(attention_backward_kernel, block, heads),
        grid=(heads,),
        in_specs=[
            pl.BlockSpec((seq, triple), whole),
            pl.BlockSpec((seq, width), whole),
            pl.BlockSpec(out.shape, whole),
            pl.BlockSpec((1, seq, seq), lambda h: (h, 0, 0)),
            pl.BlockSpec((1, 1, seq), lambda h: (h, 0, 0)),
        ],
        out_specs=pl.BlockSpec((seq, triple), whole),
        out_shape=jax.ShapeDtypeStruct((seq, triple), BF16),
        scratch_shapes=[
            pltpu.VMEM((triple, seq), F32),
            pltpu.VMEM((width, seq), F32),
            pltpu.VMEM((width, seq), F32),
            pltpu.VMEM((triple, seq), F32),
        ],
        compiler_params=pltpu.CompilerParams(vmem_limit_bytes=56 * MIB),
        cost_estimate=pl.CostEstimate(
            flops=heads * seq * seq, bytes_accessed=seq * triple, transcendentals=0
        ),
    )(qkv, d_out, out, probs, inv)


class Place:
    def __init__(self):
        self.planes = lax.axis_size("fsdp") // 2
        f = lax.axis_index("fsdp")
        k = lax.axis_index("seq")
        self.z, self.c = f // 2, f % 2
        self.k, self.y, self.x = k, k // 2, k % 2
        self.z_lines = [[2 * z + c for z in range(self.planes)] for c in range(2)]
        self.spot = jnp.stack([self.c, self.z, self.y, self.x, self.k]).astype(jnp.int32)

    def send(self, value, to):
        pairs = []
        for z in range(self.planes):
            for c in range(2):
                for y in range(2):
                    for x in range(2):
                        tz, tc, ty, tx = to(z, c, y, x)
                        here, there = ((z * 2 + c) * 2 + y) * 2 + x, ((tz * 2 + tc) * 2 + ty) * 2 + tx
                        if here != there:
                            pairs.append((here, there))
        return lax.ppermute(value, ("fsdp", "seq"), pairs)

    def core(self, value):
        return self.send(value, lambda z, c, y, x: (z, 1 - c, y, x))

    def along_x(self, value):
        return self.send(value, lambda z, c, y, x: (z, c, y, 1 - x))

    def along_y(self, value):
        return self.send(value, lambda z, c, y, x: (z, c, 1 - y, x))

    def across(self, value):
        return self.send(value, lambda z, c, y, x: (z, c, 1 - y, 1 - x))

    def along_z(self, value, step):
        return self.send(value, lambda z, c, y, x: (z ^ step, c, y, x))

    def over_z(self, value):
        return lax.all_to_all(value, "fsdp", 0, 0, axis_index_groups=self.z_lines, tiled=True)

    def turn(self, value, step):
        return self.send(value, lambda z, c, y, x: (z, y, c, x ^ step))


def pick(stack, index):
    return lax.dynamic_index_in_dim(stack, index, 0, keepdims=False)


def in_order(flag, mine, other):
    return jnp.where(flag == 0, jnp.concatenate([mine, other]), jnp.concatenate([other, mine]))


def to_image(place, here, there):
    near, far = place.turn(here, 0), place.turn(there, 1)
    here, near, far = yield here, near, far
    half = jnp.concatenate([jnp.where(place.c == place.y, here, near), far])
    half, other = yield half, place.core(half)
    return half, other


def image_order(place, row):
    blocks = row.reshape(4, -1)
    first = 2 * place.c + place.x
    return jnp.concatenate([pick(blocks, first ^ i) for i in range(4)])


def from_image(place, half):
    size = half.shape[0] // 2
    here = half[:size]
    near, far = place.turn(here, 0), place.turn(half[size:], 1)
    here, near, far = yield here, near, far
    return in_order(place.x, jnp.where(place.c == place.y, here, near)[None], far[None])


def other_order(value):
    size = value.shape[0] // 2
    return jnp.concatenate([value[size:], value[:size]])


def lane_cut(columns):
    return columns // 2 // LANES * LANES


class Transfer:
    def __init__(self, steps):
        self.steps = steps
        self.arrays = next(steps)
        self.result = None


def close_round(*transfers, rest=(), hold=()):
    every = (*transfers, *rest)
    arrays, held = lax.optimization_barrier(([transfer.arrays for transfer in every], list(hold)))
    for transfer, arrived in zip(every, arrays):
        if transfer in rest:
            transfer.arrays = arrived
            continue
        try:
            transfer.arrays = transfer.steps.send(arrived)
        except StopIteration as end:
            transfer.result = end.value
    return held


def spread(place, give, keep, corner=False):
    arrived = place.core(give)
    keep, arrived = yield keep, arrived
    block = in_order(place.c, keep, arrived)
    rows, columns = block.shape[0] // 4, block.shape[1]
    quarters = block.reshape(4, rows, columns)
    wide = jnp.broadcast_to(pick(quarters, place.k)[None], (place.planes, rows, columns))
    quarters, wide = yield quarters, wide
    quarters, planes = yield quarters, place.over_z(wide)
    own = jnp.stack([pick(planes, place.z ^ step) for step in range(1, place.planes)])
    x_part, y_part = place.along_x(own), place.along_y(own)
    quarters, own, x_part, y_part = yield quarters, own, x_part, y_part
    cut = lane_cut(columns)
    if corner:
        far = [place.across(own)]
    else:
        far = [place.along_x(y_part[:, :, :cut]), place.along_y(x_part[:, :, cut:])]
    pieces = yield quarters, own, x_part, y_part, *far
    return pieces


def assemble_kernel(planes, start, size, where, block, own, x_part, y_part, *refs):
    *far, out, sems = refs
    z, k = where[1], where[4]
    here = pl.ds(start, size)
    copies = [(block.at[:, :, here], out.at[pl.ds(z * 4, 4)])]
    for step in range(1, planes):
        at = (z ^ step) * 4
        for turn, part in enumerate((own, x_part, y_part)):
            copies.append((part.at[step - 1, :, here], out.at[at + (k ^ turn)]))
        first = 0
        for part in far:
            low, high = max(start, first), min(start + size, first + part.shape[2])
            if low < high:
                source = part.at[step - 1, :, pl.ds(low - first, high - low)]
                copies.append((source, out.at[at + (k ^ 3), :, pl.ds(low - start, high - low)]))
            first += part.shape[2]
    started = [pltpu.make_async_copy(source, target, sems.at[i]) for i, (source, target) in enumerate(copies)]
    for copy in started:
        copy.start()
    for copy in started:
        copy.wait()


def assemble(place, pieces, start, size):
    planes = place.planes
    rows = pieces[0].shape[1]
    out = pl.pallas_call(
        functools.partial(assemble_kernel, planes, start, size),
        in_specs=[scalar_spec()] + [pl.BlockSpec(memory_space=pltpu.HBM)] * len(pieces),
        out_specs=whole_spec(),
        out_shape=jax.ShapeDtypeStruct((planes * 4, rows, size), BF16),
        scratch_shapes=[pltpu.SemaphoreType.DMA((1 + 5 * (planes - 1),))],
        compiler_params=vmem(12),
        cost_estimate=pl.CostEstimate(flops=0, bytes_accessed=planes * 4 * rows * size, transcendentals=0),
    )(place.spot, *pieces)
    return out.reshape(planes * 4 * rows, size)


def whole_spec():
    return pl.BlockSpec(memory_space=pltpu.VMEM)


def scalar_spec():
    return pl.BlockSpec(memory_space=pltpu.SMEM)


def vmem(mib):
    return pltpu.CompilerParams(vmem_limit_bytes=mib * MIB)


def weight_grad_kernel(cut, group, rows, pair_count, with_riders, with_sums, where, *refs):
    lefts, rights, refs = refs[:pair_count], refs[pair_count : 2 * pair_count], refs[2 * pair_count :]
    riders, refs = (refs[0], refs[1:]) if with_riders else (None, refs)
    low_keep, low_send, high_keep, high_send, *refs = refs
    sums, refs = (refs[0], refs[1:]) if with_sums else (None, refs)
    total, *turned = refs
    step = pl.program_id(0)
    y, x = where[2], where[3]
    block = group * 4 * rows

    @pl.when(step == 0)
    def _():
        for left, by_row in zip(lefts, turned):
            by_row[...] = left[...].astype(F32).T.astype(BF16)
        if with_sums:
            sums[...] = jnp.broadcast_to(jnp.sum(rights[0][...].astype(F32), axis=0, keepdims=True), sums.shape)

    at = 0
    for right, by_row in zip(rights, turned):
        left = by_row[pl.ds(pl.multiple_of(step * block, 16), block), :]
        columns = right.shape[1]
        for start in range(0, columns, 4 * LANES):
            end = min(start + 4 * LANES, columns)
            total[:, at + start : at + end] = jnp.dot(left, right[:, start:end], preferred_element_type=F32)
        at += columns
    if with_riders:
        total[:, at:] = riders[...]
    for plane in range(group):
        for dy in range(2):
            for dx in range(2):
                row = (plane * 4 + (y ^ dy) * 2 + (x ^ dx)) * rows
                part = total[pl.ds(pl.multiple_of(row, 8), rows), :].astype(BF16)
                (low_send if dx else low_keep)[dy, plane] = part[:, :cut]
                (high_send if dy else high_keep)[dx, plane] = part[:, cut:]


def weight_grad(place, pairs, riders=None, with_sums=False):
    planes = place.planes
    tokens, width = pairs[0][0].shape
    rows = width // planes // 4
    group = planes
    columns = sum(right.shape[1] for _, right in pairs) + (0 if riders is None else riders.shape[1])
    rider_list = [] if riders is None else [riders]
    cut = lane_cut(columns)
    still = lambda shape: pl.BlockSpec(shape, lambda i: (0, 0), pipeline_mode=pl.Buffered(1))
    low = jax.ShapeDtypeStruct((2, planes, rows, cut), BF16)
    high = jax.ShapeDtypeStruct((2, planes, rows, columns - cut), BF16)
    low_spec = pl.BlockSpec((2, group, rows, cut), lambda i: (0, i, 0, 0))
    high_spec = pl.BlockSpec((2, group, rows, columns - cut), lambda i: (0, i, 0, 0))
    sum_shapes = [jax.ShapeDtypeStruct((8, pairs[0][1].shape[1]), F32)] if with_sums else []
    return pl.pallas_call(
        functools.partial(weight_grad_kernel, cut, group, rows, len(pairs), riders is not None, with_sums),
        grid=(planes // group,),
        in_specs=[scalar_spec()]
        + [still(left.shape) for left, _ in pairs]
        + [still(right.shape) for _, right in pairs]
        + [pl.BlockSpec((group * 4 * rows, extra.shape[1]), lambda i: (i, 0)) for extra in rider_list],
        out_specs=[low_spec, low_spec, high_spec, high_spec] + [pl.BlockSpec(s.shape, lambda i: (0, 0)) for s in sum_shapes],
        out_shape=[low, low, high, high] + sum_shapes,
        scratch_shapes=[pltpu.VMEM((group * 4 * rows, columns), F32)] + [pltpu.VMEM((width, tokens), BF16) for _ in pairs],
        compiler_params=vmem(56),
        cost_estimate=pl.CostEstimate(flops=tokens * width, bytes_accessed=width * columns, transcendentals=0),
    )(place.spot, *[left for left, _ in pairs], *[right for _, right in pairs], *rider_list)


def add_first_kernel(low, from_x, high, from_y, low_keep, low_send, high_keep, high_send):
    for kept, arrived, outs in ((low, from_x, (low_keep, low_send)), (high, from_y, (high_keep, high_send))):
        for i, out in enumerate(outs):
            out[...] = (kept[i].astype(F32) + arrived[i].astype(F32)).astype(BF16)


def add_first(low, from_x, high, from_y):
    planes = low.shape[1]
    ins = lambda a: pl.BlockSpec((2, 1, *a.shape[2:]), lambda i: (0, i, 0, 0))
    out = lambda a: pl.BlockSpec((1, *a.shape[2:]), lambda i: (i, 0, 0))
    shape = lambda a: jax.ShapeDtypeStruct(a.shape[1:], BF16)
    return pl.pallas_call(
        add_first_kernel,
        grid=(planes,),
        in_specs=[ins(low), ins(from_x), ins(high), ins(from_y)],
        out_specs=[out(low), out(low), out(high), out(high)],
        out_shape=[shape(low), shape(low), shape(high), shape(high)],
        compiler_params=vmem(24),
    )(low, from_x, high, from_y)


def add_second_kernel(low, from_y, high, from_x, out):
    cut = low.shape[2]
    out[:, :, :cut] = (low[...].astype(F32) + from_y[...].astype(F32)).astype(BF16)
    out[:, :, cut:] = (high[...].astype(F32) + from_x[...].astype(F32)).astype(BF16)


def add_second(low, from_y, high, from_x):
    planes, rows, cut = low.shape
    spec = lambda columns: pl.BlockSpec((1, rows, columns), lambda i: (i, 0, 0))
    rest = high.shape[2]
    return pl.pallas_call(
        add_second_kernel,
        grid=(planes,),
        in_specs=[spec(cut), spec(cut), spec(rest), spec(rest)],
        out_specs=spec(cut + rest),
        out_shape=jax.ShapeDtypeStruct((planes, rows, cut + rest), BF16),
        compiler_params=vmem(24),
    )(low, from_y, high, from_x)


def quarter_of(where, parts, core, side, store):
    mine, x_part, y_part, far_low, far_high = parts
    near, same = where[2] == core, where[3] == side

    @pl.when(near & same)
    def _():
        store(mine[...])

    @pl.when(near & ~same)
    def _():
        store(x_part[...])

    @pl.when(~near & same)
    def _():
        store(y_part[...])

    @pl.when(~near & ~same)
    def _():
        store(jnp.concatenate([far_low[...], far_high[...]], axis=1))


def give_kernel(where, *refs):
    out = refs[-1]
    for core in range(2):

        @pl.when(where[0] != core)
        def _():
            for side in range(2):

                def store(value):
                    out[side] = value

                quarter_of(where, refs[:-1], core, side, store)


def give_rows(place, parts):
    rows, columns = parts[0].shape
    return pl.pallas_call(
        give_kernel,
        in_specs=[scalar_spec()] + [whole_spec()] * 5,
        out_specs=whole_spec(),
        out_shape=jax.ShapeDtypeStruct((2, rows, columns), BF16),
        compiler_params=vmem(24),
    )(place.spot, *parts)


def finish_kernel(write, where, *refs):
    parts, arrived = refs[:5], refs[5]
    outs, kept = refs[6:-1], refs[-1]
    for core in range(2):

        @pl.when(where[0] == core)
        def _():
            for side in range(2):

                def store(value):
                    kept[side] = value

                quarter_of(where, parts, core, side, store)
            halves = [kept[...], arrived[...]]
            if core:
                halves = halves[::-1]
            lower, higher = (half.astype(F32).reshape(-1, half.shape[2]) for half in halves)
            write(lower, higher, *outs)


def finish(place, pieces, write, shapes):
    *parts, arrived = pieces
    return pl.pallas_call(
        functools.partial(finish_kernel, write),
        in_specs=[scalar_spec()] + [whole_spec()] * 6,
        out_specs=[whole_spec()] * len(shapes),
        out_shape=[jax.ShapeDtypeStruct(shape, F32) for shape in shapes],
        scratch_shapes=[pltpu.VMEM(arrived.shape, BF16)],
        compiler_params=vmem(40),
    )(place.spot, *parts, arrived)


def split_rows_kernel(where, arrived, low_keep, low_send, high_keep, high_send, total):
    planes = arrived.shape[0]
    rows, cut = low_keep.shape[2:]
    total[...] = functools.reduce(jnp.add, (arrived[plane].astype(F32) for plane in range(planes)))
    for dy in range(2):
        for dx in range(2):
            row = ((where[2] ^ dy) * 2 + (where[3] ^ dx)) * rows
            part = total[pl.ds(pl.multiple_of(row, 8), rows), :].astype(BF16)
            (low_send if dx else low_keep)[dy, 0] = part[:, :cut]
            (high_send if dy else high_keep)[dx, 0] = part[:, cut:]


def split_rows(place, arrived):
    _, rows, columns = arrived.shape
    cut = lane_cut(columns)
    low = jax.ShapeDtypeStruct((2, 1, rows // 4, cut), BF16)
    high = jax.ShapeDtypeStruct((2, 1, rows // 4, columns - cut), BF16)
    return pl.pallas_call(
        split_rows_kernel,
        in_specs=[scalar_spec(), whole_spec()],
        out_specs=[whole_spec()] * 4,
        out_shape=[low, low, high, high],
        scratch_shapes=[pltpu.VMEM((rows, columns), F32)],
        compiler_params=vmem(24),
    )(place.spot, arrived)


def collect_lines(place, partial):
    arrived = yield place.over_z(partial.reshape(place.planes, -1, partial.shape[1]))
    return (yield from collect(place, split_rows(place, arrived), along_z=False))


def collect(place, pieces, along_z=True):
    low, low_send, high, high_send = pieces
    low, high, from_x, from_y = yield low, high, place.along_x(low_send), place.along_y(high_send)
    low, low_send, high, high_send = add_first(low, from_x, high, from_y)
    low, high, from_y, from_x = yield low, high, place.along_y(low_send), place.along_x(high_send)
    cut = low.shape[2]
    plane = add_second(low, from_y, high, from_x)
    if along_z:
        arrived = yield place.over_z(plane)
        mine = jnp.sum(arrived.astype(F32), axis=0).astype(BF16)
    else:
        mine = plane[0]
    mine, x_part, y_part = yield mine, place.along_x(mine), place.along_y(mine)
    far_low, far_high = place.along_x(y_part[:, :cut]), place.along_y(x_part[:, cut:])
    parts = yield mine, x_part, y_part, far_low, far_high
    parts, arrived = yield parts, place.core(give_rows(place, parts))
    return (*parts, arrived)


def vectors_kernel(first, half, where, block, rows, shift):
    turned = block[...].astype(F32).T
    rows[...] = turned[first : first + rows.shape[0]]
    shift[...] = jnp.zeros_like(shift)
    for core in range(2):

        @pl.when(where[0] == core)
        def _():
            for row, at in ((4, 0), (5, 2 * half)):
                shift[:, at : at + half] = turned[first + row : first + row + 1, core * half : (core + 1) * half]


def vectors(place, full, at, count):
    width = full.shape[0]
    tile = at // LANES
    return pl.pallas_call(
        functools.partial(vectors_kernel, at - tile * LANES, width // 2),
        grid=(1,),
        in_specs=[scalar_spec(), pl.BlockSpec((width, LANES), lambda i: (0, tile))],
        out_specs=[pl.BlockSpec((count, width), lambda i: (0, 0)), pl.BlockSpec((1, 3 * width // 2), lambda i: (0, 0))],
        out_shape=[jax.ShapeDtypeStruct((count, width), F32), jax.ShapeDtypeStruct((1, 3 * width // 2), F32)],
        compiler_params=vmem(24),
    )(place.spot, full)


def norm_and_project_kernel(half, other, weights, shift, rows, tokens, normed, inv_std, low, packed):
    step = pl.program_id(0)
    blocks = pl.num_programs(0) // 2

    @pl.when(step < blocks)
    def _():
        tokens[...] = half[...]

    @pl.when(step >= blocks)
    def _():
        tokens[...] = other[...]

    n, inv_std[...] = normalize(tokens[...].astype(F32))
    normed[...] = n.astype(BF16)
    low[...] = (n * rows[0:1, :] + rows[2:3, :]).astype(BF16)
    columns = packed.shape[1]
    packed[...] = (
        jnp.dot(low[...], weights[:, :columns], preferred_element_type=F32) + shift[...]
    ).astype(BF16)


def norm_and_project(half, other, weights, shift, rows, columns):
    size, width = half.shape
    blocks = 2
    block = size // blocks
    own = lambda shape: pl.BlockSpec(shape, lambda i: (i, 0))
    still = lambda array: pl.BlockSpec(array.shape, lambda i: (0, 0), pipeline_mode=pl.Buffered(1))
    wide = jax.ShapeDtypeStruct((2 * size, width), BF16)
    return pl.pallas_call(
        norm_and_project_kernel,
        grid=(2 * blocks,),
        in_specs=[
            pl.BlockSpec((block, width), lambda i: (jnp.minimum(i, blocks - 1), 0)),
            pl.BlockSpec((block, width), lambda i: (jnp.maximum(i - blocks, 0), 0)),
            still(weights),
            still(shift),
            still(rows),
        ],
        out_specs=[own((block, width)), own((block, width)), own((block, 1)), own((block, width)), own((block, columns))],
        out_shape=[
            wide,
            wide,
            jax.ShapeDtypeStruct((2 * size, 1), F32),
            wide,
            jax.ShapeDtypeStruct((2 * size, columns), BF16),
        ],
        compiler_params=vmem(32),
        cost_estimate=pl.CostEstimate(flops=size * width, bytes_accessed=size * width, transcendentals=0),
    )(half, other, weights, shift, rows)


def project_and_norm_kernel(
    half, where, tokens, mine, other, w_mine, w_other, rows, attended, full_out, residual, normed, inv_std, low
):
    step = pl.program_id(0)
    for core in range(2):
        here, there = slice(core * half, (core + 1) * half), slice((1 - core) * half, (2 - core) * half)

        @pl.when((where[0] == core) & (step == 0))
        def _():
            full_out[:, here] = w_mine[:, :half]
            full_out[:, there] = w_other[:, :half]

        @pl.when(where[0] == core)
        def _():
            attended[:, here] = mine[:, :half]
            attended[:, there] = other[:, :half]

    value = tokens[...].astype(F32) + jnp.dot(attended[...], full_out[...], preferred_element_type=F32) + rows[6:7, :]

    @pl.when(step < pl.num_programs(0) // 2)
    def _():
        residual[...] = value

    n, inv_std[...] = normalize(value)
    normed[...] = n.astype(BF16)
    low[...] = (n * rows[1:2, :] + rows[3:4, :]).astype(BF16)


def project_and_norm(place, tokens, mine, other, w_mine, w_other, rows):
    count, width = tokens.shape
    blocks = 4
    block = count // blocks
    own = lambda columns: pl.BlockSpec((block, columns), lambda i: (i, 0))
    still = lambda shape: pl.BlockSpec(shape, lambda i: (0, 0), pipeline_mode=pl.Buffered(1))
    wide = jax.ShapeDtypeStruct((count, width), BF16)
    return pl.pallas_call(
        functools.partial(project_and_norm_kernel, width // 2),
        grid=(blocks,),
        in_specs=[
            scalar_spec(),
            own(width),
            own(mine.shape[1]),
            pl.BlockSpec((block, other.shape[1]), lambda i: ((i + blocks // 2) % blocks, 0)),
            still(w_mine.shape),
            still(w_other.shape),
            still(rows.shape),
        ],
        out_specs=[
            own(width),
            pl.BlockSpec((width, width), lambda i: (0, 0)),
            pl.BlockSpec((block, width), lambda i: (jnp.minimum(i, blocks // 2 - 1), 0)),
            own(width),
            own(1),
            own(width),
        ],
        out_shape=[
            wide,
            jax.ShapeDtypeStruct((width, width), BF16),
            jax.ShapeDtypeStruct((count // 2, width), F32),
            wide,
            jax.ShapeDtypeStruct((count, 1), F32),
            wide,
        ],
        compiler_params=vmem(32),
        cost_estimate=pl.CostEstimate(flops=count * width, bytes_accessed=count * width, transcendentals=0),
    )(place.spot, tokens, mine, other, w_mine, w_other, rows)


def sum_devices(place, value):
    ways = [place.core, place.along_x, place.along_y]
    step = 1
    while step < place.planes:
        ways.append(functools.partial(place.along_z, step=step))
        step *= 2
    for way in ways:
        value, other = yield value, way(value)
        value = value + other
    return value


def norm_back_kernel(half, where, part, arrived, upstream, normed, inv_std, gain, low, own_columns, own_rows, sums):
    step = pl.program_id(0)
    e = part[...].astype(F32) + arrived[...].astype(F32)
    n = normed[...].astype(F32)
    scaled = e * gain[...]
    first_mean = jnp.mean(scaled, axis=-1, keepdims=True)
    second_mean = jnp.mean(scaled * n, axis=-1, keepdims=True)
    cot = upstream[...].astype(F32)
    d = cot + inv_std[...] * (scaled - first_mean - n * second_mean)
    d_low = d.astype(BF16)
    low[...] = d_low
    for core in range(2):

        @pl.when(where[0] == core)
        def _():
            own_columns[...] = d_low[:, core * half : (core + 1) * half]

    @pl.when(step < pl.num_programs(0) // 2)
    def _():
        own_rows[...] = d

    rows = jnp.concatenate([jnp.sum(v, axis=0, keepdims=True) for v in (e * n, e, d, cot)] + [jnp.zeros((4, e.shape[1]), F32)])

    @pl.when(step == 0)
    def _():
        sums[...] = rows

    @pl.when(step > 0)
    def _():
        sums[...] += rows


def norm_back_second(place, part, arrived, upstream, normed, inv_std, gain):
    tokens, width = part.shape
    size = tokens // 8
    by_row = pl.BlockSpec((size, width), lambda i: (i, 0))
    turned = pl.BlockSpec((size, width), lambda i: ((i + 4) % 8, 0))
    return pl.pallas_call(
        functools.partial(norm_back_kernel, width // 2),
        grid=(8,),
        in_specs=[
            scalar_spec(),
            by_row,
            turned,
            by_row,
            by_row,
            pl.BlockSpec((size, 1), lambda i: (i, 0)),
            pl.BlockSpec((1, width), lambda i: (0, 0)),
        ],
        out_specs=[
            by_row,
            pl.BlockSpec((size, width // 2), lambda i: (i, 0)),
            pl.BlockSpec((size, width), lambda i: (jnp.minimum(i, 3), 0)),
            pl.BlockSpec((8, width), lambda i: (0, 0)),
        ],
        out_shape=[
            jax.ShapeDtypeStruct((tokens, width), BF16),
            jax.ShapeDtypeStruct((tokens, width // 2), BF16),
            jax.ShapeDtypeStruct((tokens // 2, width), F32),
            jax.ShapeDtypeStruct((8, width), F32),
        ],
        compiler_params=vmem(24),
    )(place.spot, part, arrived, upstream, normed, inv_std, gain)


def norm_back_first_kernel(part, arrived, d_resid, normed, inv_std, gain, grad, sums):
    e = part[...].astype(F32) + arrived[...].astype(F32)
    n = normed[...].astype(F32)
    scaled = e * gain[...]
    first_mean = jnp.mean(scaled, axis=-1, keepdims=True)
    second_mean = jnp.mean(scaled * n, axis=-1, keepdims=True)
    grad[...] = (d_resid[...] + inv_std[...] * (scaled - first_mean - n * second_mean)).astype(BF16)
    rows = jnp.concatenate([jnp.sum(v, axis=0, keepdims=True) for v in (e * n, e)] + [jnp.zeros((6, e.shape[1]), F32)])

    @pl.when(pl.program_id(0) == 0)
    def _():
        sums[...] = rows

    @pl.when(pl.program_id(0) > 0)
    def _():
        sums[...] += rows


def norm_back_first(part, arrived, d_resid, normed, inv_std, gain):
    tokens, width = arrived.shape
    size = tokens // 4
    by_row = pl.BlockSpec((size, width), lambda i: (i, 0))
    return pl.pallas_call(
        norm_back_first_kernel,
        grid=(4,),
        in_specs=[by_row] * 4 + [pl.BlockSpec((size, 1), lambda i: (i, 0)), pl.BlockSpec((1, width), lambda i: (0, 0))],
        out_specs=[by_row, pl.BlockSpec((8, width), lambda i: (0, 0))],
        out_shape=[jax.ShapeDtypeStruct((tokens, width), BF16), jax.ShapeDtypeStruct((8, width), F32)],
        compiler_params=vmem(24),
    )(part, arrived, d_resid, normed, inv_std, gain)


def normalize(values):
    row_mean = jnp.mean(values, axis=-1, keepdims=True)
    centred = values - row_mean
    variance = jnp.mean(centred * centred, axis=-1, keepdims=True)
    inv_std = lax.rsqrt(variance + EPSILON)
    return centred * inv_std, inv_std


def layer_norm(values, gain_row, shift_row):
    row_mean = jnp.mean(values, axis=-1, keepdims=True)
    centred = values - row_mean
    variance = jnp.mean(centred * centred, axis=-1, keepdims=True)
    inv_std = lax.rsqrt(variance + EPSILON)
    normed = centred * inv_std
    return (normed * gain_row + shift_row, normed, inv_std)


def norm_back(upstream, normed, inv_std, gain_row):
    scaled = upstream * gain_row
    first_mean = jnp.mean(scaled, axis=-1, keepdims=True)
    second_mean = jnp.mean(scaled * normed, axis=-1, keepdims=True)
    return inv_std * (scaled - first_mean - normed * second_mean)


def gelu_and_slope(values):
    square = values * values
    tangent = jnp.tanh(GELU_SCALE * values * (1.0 + GELU_CUBE * square))
    half = 0.5 * (1.0 + tangent)
    slope = half + 0.5 * values * (1.0 - tangent * tangent) * GELU_SCALE * (1.0 + 3.0 * GELU_CUBE * square)
    return values * half, slope


def dot(a, b):
    return jnp.dot(a, b, preferred_element_type=F32)


def dot_t(a, b):
    return lax.dot_general(a, b, (((1,), (1,)), ((), ())), preferred_element_type=F32)


def t_dot(a, b):
    return lax.dot_general(a, b, (((0,), (0,)), ((), ())), preferred_element_type=F32)


def image_on_chip(inputs, key_mask, w_qkv, w_out, w_up, w_down, norm_gains, biases, up_bias, cotangent):
    place = Place()
    img_count, tok_count, width = inputs.shape
    shard = w_qkv.shape[0]
    fsdp = lax.axis_size("fsdp")
    half_width = width // 2
    hidden = w_up.shape[1]
    half_hidden = -(-hidden // 2 // LANES) * LANES
    up_shard = up_bias.shape[0]
    up_cols = -(-up_shard // shard)

    def halves_qkv(w):
        return jnp.moveaxis(w.reshape(w.shape[0], 3, 2, half_width), 2, 0).reshape(2, w.shape[0], 3 * half_width)

    def halves_hidden(w):
        padded = jnp.pad(w, ((0, 0), (0, 2 * half_hidden - hidden)))
        return jnp.stack([padded[:, :half_hidden], padded[:, half_hidden:]])

    small = jnp.concatenate(
        [
            norm_gains,
            biases,
            jnp.pad(up_bias, (0, up_cols * shard - up_shard)).reshape(up_cols, shard),
        ]
    )
    n_small = small.shape[0]
    spare = -(3 * half_width) % LANES
    extra = jnp.pad(small.T, ((0, 0), (0, spare - n_small)))
    c = place.c

    qkv_halves = halves_qkv(w_qkv)
    give = jnp.concatenate([pick(qkv_halves, 1 - c), extra], axis=1)
    keep = jnp.concatenate([pick(qkv_halves, c), extra], axis=1)
    qkv = Transfer(spread(place, give, keep))
    tokens_in = Transfer(to_image(place, pick(inputs, place.x), pick(inputs, 1 - place.x)))
    w_out, w_up, w_down, cotangent = close_round(qkv, hold=(w_out, w_up, w_down, cotangent))
    close_round(qkv)

    out_pad = -half_width % LANES
    out_cols = half_width + out_pad
    out_halves = jnp.pad(jnp.moveaxis(w_out.reshape(shard, 2, half_width), 1, 0), ((0, 0), (0, 0), (0, out_pad)))
    down_halves = halves_hidden(w_down.T)
    down = Transfer(spread(place, pick(down_halves, 1 - c), pick(down_halves, c)))
    rest = jnp.concatenate([out_halves, halves_hidden(w_up)], axis=2)
    out_up = Transfer(spread(place, pick(rest, 1 - c), pick(rest, c), corner=True))
    upstream_parts = pick(cotangent, place.x), pick(cotangent, 1 - place.x)
    close_round(out_up)
    key_mask, *upstream_parts = close_round(qkv, tokens_in, out_up, hold=(key_mask, *upstream_parts))

    upstream_in = Transfer(to_image(place, *upstream_parts))
    other_mask = place.core(key_mask)
    close_round(qkv, tokens_in)

    live_keys = image_order(place, pick(jnp.where(c == place.y, key_mask, other_mask), place.x))
    mask_bias = jnp.where(live_keys > 0, 0.0, NEG_FILL).astype(F32)[:, None]
    (mask_bias,) = close_round(qkv, out_up, down, upstream_in, hold=(mask_bias,))

    full_first = assemble(place, qkv.result, 0, 3 * half_width + spare)
    full_qkv = full_first[:, : 3 * half_width]
    small_rows, qkv_shift = vectors(place, full_first, 3 * half_width, 16)
    gain_rows, bias_rows = small_rows[:2], small_rows[2:8]
    up_shift = (
        small_rows[8 : 8 + up_cols].reshape(up_cols, fsdp, shard).transpose(1, 0, 2).reshape(fsdp, up_cols * shard)[:, :up_shard]
    ).reshape(hidden)
    up_shift = pick(jnp.pad(up_shift, (0, 2 * half_hidden - hidden)).reshape(2, half_hidden), c)
    tokens, first_normed, first_inv, first_low, packed = norm_and_project(
        *tokens_in.result, full_first, qkv_shift, small_rows, 3 * half_width
    )
    (packed,) = close_round(out_up, down, upstream_in, hold=(packed,))

    attended_half, raised, inv_total = attention_forward(packed, mask_bias)
    (attended_half,) = close_round(out_up, down, hold=(attended_half,))

    half_out = assemble(place, out_up.result, 0, out_cols)
    attended, full_out, residual_half, second_normed, second_inv, second_low = project_and_norm(
        place, tokens, attended_half, place.core(attended_half), half_out, place.core(half_out), small_rows
    )
    half = residual_half.shape[0]
    (second_low,) = close_round(down, hold=(second_low,))

    full_up = assemble(place, out_up.result, out_cols, half_hidden)
    active, slope = gelu_and_slope(dot(second_low, full_up) + up_shift)
    active, slope = active.astype(BF16), slope.astype(BF16)
    active, slope = close_round(down, hold=(active, slope))

    upstream = jnp.concatenate(upstream_in.result)
    dw_down = t_dot(upstream, active).astype(BF16)
    down_grad = Transfer(collect_lines(place, dw_down))
    full_down = assemble(place, down.result, 0, half_hidden)
    d_active = dot(upstream, full_down)
    d_upper = (d_active * slope.astype(F32)).astype(BF16)
    d_second_part = dot_t(d_upper, full_up).astype(BF16)
    (d_second_part,) = close_round(hold=(d_second_part,))

    d_second_other = place.core(d_second_part)
    *dw_up, d_upper_sums = weight_grad(place, [(second_low, d_upper)], with_sums=True)
    down_part = dot_t(active, full_down).astype(BF16)
    down_sum = down_part[:half].astype(F32) + place.core(down_part[half:]).astype(F32)
    layer_half = (residual_half + down_sum + bias_rows[5]).astype(BF16)
    *dw_up, d_second_other, layer_half = close_round(hold=(*dw_up, d_second_other, layer_half))

    up_grad = Transfer(collect(place, dw_up))
    layer_out = Transfer(from_image(place, layer_half))
    d_resid_low, d_resid_columns, d_resid_half, by_width = norm_back_second(
        place, d_second_part, d_second_other, upstream, second_normed, second_inv, gain_rows[1:]
    )
    d_attended = dot_t(d_resid_low, lax.dynamic_slice_in_dim(full_out, c * half_width, half_width)).astype(BF16)
    d_packed = attention_backward(packed, d_attended, attended_half, raised, inv_total)
    (d_packed,) = close_round(up_grad, layer_out, hold=(d_packed,))

    def own_part(row):
        size = row.shape[0]
        return jnp.where(c == 0, jnp.pad(row, (0, size)), jnp.pad(row, (size, 0)))

    by_hidden = own_part(d_upper_sums[0])[:hidden].reshape(fsdp, up_shard)
    by_hidden = jnp.pad(by_hidden, ((0, 0), (0, up_cols * shard - up_shard))).reshape(fsdp, up_cols, shard)
    by_hidden = by_hidden.transpose(1, 0, 2).reshape(up_cols, width)
    pack_sum = dot(jnp.ones((8, d_packed.shape[0]), BF16), d_packed)[0]
    riders = jnp.concatenate(
        [
            own_part(pack_sum[:half_width])[None],
            own_part(pack_sum[2 * half_width :])[None],
            jnp.where(c == 0, by_width[:4], 0.0),
            by_hidden,
        ]
    )
    riders = jnp.pad(riders, ((0, LANES - riders.shape[0]), (0, 0))).T
    dw_last = weight_grad(place, [(first_low, d_packed), (attended, d_resid_columns)], riders)
    *dw_last, d_packed = close_round(up_grad, down_grad, hold=(*dw_last, d_packed))

    last_grad = Transfer(collect(place, dw_last))
    d_first_part = dot_t(d_packed, full_qkv).astype(BF16)
    grad_half, first_sums = norm_back_first(
        d_first_part,
        place.core(d_first_part[half:]),
        d_resid_half,
        first_normed,
        first_inv,
        gain_rows[:1],
    )
    late = Transfer(sum_devices(place, first_sums[:2].reshape(-1, LANES)))
    (grad_half,) = close_round(last_grad, down_grad, hold=(grad_half,))

    def write_hidden(lower, higher, out):
        out[:, :half_hidden] = lower[:, :half_hidden]
        out[:, half_hidden:] = higher[:, : hidden - half_hidden]

    def write_last(lower, higher, qkv_out, proj, rest):
        for i in range(3):
            here = slice(i * half_width, (i + 1) * half_width)
            qkv_out[:, i * width : i * width + half_width] = lower[:, here]
            qkv_out[:, i * width + half_width : (i + 1) * width] = higher[:, here]
        here = slice(3 * half_width, 4 * half_width)
        proj[:, :half_width] = lower[:, here]
        proj[:, half_width:] = higher[:, here]
        rest[...] = lower[:, 4 * half_width :] + higher[:, 4 * half_width :]

    close_round(up_grad, last_grad, down_grad, late)
    grad_in = Transfer(from_image(place, grad_half))
    close_round(up_grad, last_grad, down_grad, late, grad_in)
    grad_in, layer_out = close_round(
        up_grad, last_grad, down_grad, late, hold=(grad_in.result, layer_out.result)
    )
    close_round(up_grad, last_grad, down_grad, late)
    (grad_up,) = finish(place, up_grad.result, write_hidden, [(shard, hidden)])
    (grad_down,) = finish(place, down_grad.result, write_hidden, [(shard, hidden)])
    grad_up, grad_down = close_round(last_grad, late, hold=(grad_up, grad_down))
    grad_qkv, grad_proj, rest_sums = finish(
        place, last_grad.result, write_last, [(shard, 3 * width), (shard, width), (shard, LANES)]
    )
    rows = rest_sums[:, : 6 + up_cols].T
    first_rows = lax.dynamic_slice_in_dim(late.result.reshape(2, width), lax.axis_index("fsdp") * shard, shard, axis=1)
    grad_upbias = rows[6:].reshape(up_cols * shard)[:up_shard]
    grad_gains = jnp.stack([first_rows[0], rows[2]])
    grad_biases = jnp.stack([first_rows[1], rows[3], rows[0], rows[1], rows[4], rows[5]])
    return (layer_out, grad_in, grad_qkv, grad_proj, grad_up, grad_down.T, grad_gains, grad_biases, grad_upbias)


def for_sending(array):
    return jax.tree.map(lambda a: a.astype(jnp.bfloat16) if a.dtype == jnp.float32 else a, array)


def gelu_tanh(values):
    return (
        0.5
        * values
        * (1.0 + jnp.tanh(GELU_SCALE * (values + GELU_CUBE * values * values * values)))
    )


def gelu_slope(values):
    tangent = jnp.tanh(GELU_SCALE * (values + GELU_CUBE * values * values * values))
    return 0.5 * (1.0 + tangent) + 0.5 * values * (1.0 - tangent * tangent) * GELU_SCALE * (
        1.0 + 3.0 * GELU_CUBE * values * values
    )


def block_scores(q_block, keys_full, live, score_scale):
    scores = (
        jnp.einsum("qhd,khd->hqk", q_block, keys_full, preferred_element_type=jnp.float32)
        * score_scale
    )
    return jnp.where(live[None, None, :] > 0, scores, NEG_FILL)


def forward_image(pieces, block_rows, score_scale):
    query, keys_full, values_full, live = pieces
    out_parts = []
    total_parts = []
    for start in range(0, query.shape[0], block_rows):
        masked = block_scores(query[start : start + block_rows], keys_full, live, score_scale)
        top_score = jnp.max(masked, axis=-1, keepdims=True)
        log_total = top_score + jnp.log(
            jnp.sum(jnp.exp(masked - top_score), axis=-1, keepdims=True)
        )
        probs_low = jnp.exp(masked - log_total).astype(jnp.bfloat16)
        out_parts.append(
            jnp.einsum(
                "hqk,khd->qhd", probs_low, values_full, preferred_element_type=jnp.float32
            ).astype(jnp.bfloat16)
        )
        total_parts.append(log_total)
    return (jnp.concatenate(out_parts, axis=0), jnp.concatenate(total_parts, axis=1))


def backward_image(pieces, block_rows, score_scale):
    query, keys_full, values_full, live, log_totals, d_heads = pieces
    dq_parts = []
    dk_total = jnp.zeros(keys_full.shape, jnp.float32)
    dv_total = jnp.zeros(values_full.shape, jnp.float32)
    for start in range(0, query.shape[0], block_rows):
        q_block = query[start : start + block_rows]
        d_block = d_heads[start : start + block_rows]
        masked = block_scores(q_block, keys_full, live, score_scale)
        probs = jnp.exp(masked - log_totals[:, start : start + block_rows])
        probs_low = probs.astype(jnp.bfloat16)
        d_probs = jnp.einsum(
            "qhd,khd->hqk", d_block, values_full, preferred_element_type=jnp.float32
        )
        row_dot = jnp.sum(probs * d_probs, axis=-1, keepdims=True)
        d_scores = (probs * (d_probs - row_dot)).astype(jnp.bfloat16)
        dq_block = (
            jnp.einsum("hqk,khd->qhd", d_scores, keys_full, preferred_element_type=jnp.float32)
            * score_scale
        )
        dq_parts.append(dq_block.astype(jnp.bfloat16))
        dk_total = dk_total + jnp.einsum(
            "hqk,qhd->khd", d_scores, q_block, preferred_element_type=jnp.float32
        )
        dv_total = dv_total + jnp.einsum(
            "hqk,qhd->khd", probs_low, d_block, preferred_element_type=jnp.float32
        )
    return (
        jnp.concatenate(dq_parts, axis=0),
        (dk_total * score_scale).astype(jnp.bfloat16),
        dv_total.astype(jnp.bfloat16),
    )


def heads_over_seq(inputs, key_mask, w_qkv, w_out, w_up, w_down, norm_gains, biases, up_bias, cotangent):
    img_count, tok_count, width = inputs.shape
    seq_len = key_mask.shape[1]
    row_count = img_count * tok_count
    head_cols = width // lax.axis_size("seq")
    local_heads = head_cols // HEAD_DIM
    block_rows = min(QBLOCK, seq_len)
    score_scale = 1.0 / math.sqrt(HEAD_DIM)
    gathered = (
        lax.all_gather(w_qkv, "fsdp", axis=0, tiled=True),
        lax.all_gather(w_out, "fsdp", axis=0, tiled=True),
        lax.all_gather(w_up, "fsdp", axis=0, tiled=True),
        lax.all_gather(w_down, "fsdp", axis=1, tiled=True),
        lax.all_gather(norm_gains, "fsdp", axis=1, tiled=True),
        lax.all_gather(biases, "fsdp", axis=1, tiled=True),
        lax.all_gather(up_bias, "fsdp", axis=0, tiled=True),
    )
    full_qkv, full_out, full_up, full_down, full_gains, full_biases, full_upbias = gathered
    gain_rows = full_gains.astype(jnp.float32)
    bias_rows = full_biases.astype(jnp.float32)
    up_shift = full_upbias.astype(jnp.float32)
    qkv_shift = jnp.concatenate([bias_rows[2], jnp.zeros((width,), jnp.float32), bias_rows[3]])
    tok_wide = inputs.reshape(row_count, width).astype(jnp.float32)
    first_out, first_normed, first_inv = layer_norm(tok_wide, gain_rows[0], bias_rows[0])
    first_low = first_out.astype(jnp.bfloat16)
    packed = (jnp.dot(first_low, full_qkv, preferred_element_type=jnp.float32) + qkv_shift).astype(
        jnp.bfloat16
    )
    by_heads = lax.all_to_all(
        packed.reshape(img_count, tok_count, 3, width),
        "seq",
        split_axis=3,
        concat_axis=1,
        tiled=True,
    )
    query = by_heads[:, :, 0].reshape(img_count, seq_len, local_heads, HEAD_DIM)
    keys_full = by_heads[:, :, 1].reshape(img_count, seq_len, local_heads, HEAD_DIM)
    values_full = by_heads[:, :, 2].reshape(img_count, seq_len, local_heads, HEAD_DIM)

    def run_forward(pieces):
        return forward_image(pieces, block_rows, score_scale)

    attended_heads, log_totals = lax.map(run_forward, (query, keys_full, values_full, key_mask))
    attended = lax.all_to_all(
        for_sending(attended_heads.reshape(img_count, seq_len, head_cols)),
        "seq",
        split_axis=1,
        concat_axis=2,
        tiled=True,
    ).reshape(row_count, width)
    residual = (
        tok_wide + jnp.dot(attended, full_out, preferred_element_type=jnp.float32) + bias_rows[4]
    )
    second_out, second_normed, second_inv = layer_norm(residual, gain_rows[1], bias_rows[1])
    second_low = second_out.astype(jnp.bfloat16)
    upper = jnp.dot(second_low, full_up, preferred_element_type=jnp.float32) + up_shift
    active = gelu_tanh(upper).astype(jnp.bfloat16)
    layer_out = (
        residual + jnp.dot(active, full_down, preferred_element_type=jnp.float32) + bias_rows[5]
    ).astype(jnp.bfloat16)
    back_qkv, back_out, back_up, back_down, back_gains, back_biases, back_upbias = gathered
    back_gain_rows = back_gains.astype(jnp.float32)
    upstream = cotangent.reshape(row_count, width)
    grad_wide = upstream.astype(jnp.float32)
    d_active = jnp.dot(upstream, back_down.T, preferred_element_type=jnp.float32)
    dw_down = jnp.dot(active.T, upstream, preferred_element_type=jnp.float32)
    d_upper = (d_active * gelu_slope(upper)).astype(jnp.bfloat16)
    dw_up = jnp.dot(second_low.T, d_upper, preferred_element_type=jnp.float32)
    d_second = jnp.dot(d_upper, back_up.T, preferred_element_type=jnp.float32)
    d_resid = grad_wide + norm_back(d_second, second_normed, second_inv, back_gain_rows[1])
    d_resid_low = d_resid.astype(jnp.bfloat16)
    dw_out = jnp.dot(attended.T, d_resid_low, preferred_element_type=jnp.float32)
    d_attended = jnp.dot(d_resid_low, back_out.T, preferred_element_type=jnp.float32).astype(
        jnp.bfloat16
    )
    d_heads = lax.all_to_all(
        d_attended.reshape(img_count, tok_count, width),
        "seq",
        split_axis=2,
        concat_axis=1,
        tiled=True,
    ).reshape(img_count, seq_len, local_heads, HEAD_DIM)

    def run_backward(pieces):
        return backward_image(pieces, block_rows, score_scale)

    dq_heads, dk_heads, dv_heads = lax.map(
        run_backward, (query, keys_full, values_full, key_mask, log_totals, d_heads)
    )
    stacked = jnp.stack(
        [
            dq_heads.reshape(img_count, seq_len, head_cols),
            dk_heads.reshape(img_count, seq_len, head_cols),
            dv_heads.reshape(img_count, seq_len, head_cols),
        ],
        axis=2,
    )
    d_packed = (
        lax.all_to_all(for_sending(stacked), "seq", split_axis=1, concat_axis=3, tiled=True)
        .astype(stacked.dtype)
        .reshape(row_count, 3 * width)
    )
    d_pack_wide = d_packed.astype(jnp.float32)
    dw_qkv = jnp.dot(first_low.T, d_packed, preferred_element_type=jnp.float32)
    d_first = jnp.dot(d_packed, back_qkv.T, preferred_element_type=jnp.float32)
    grad_in = (d_resid + norm_back(d_first, first_normed, first_inv, back_gain_rows[0])).astype(
        jnp.bfloat16
    )
    d_gains = jnp.stack(
        [jnp.sum(d_first * first_normed, axis=0), jnp.sum(d_second * second_normed, axis=0)]
    )
    d_biases = jnp.stack(
        [
            jnp.sum(d_first, axis=0),
            jnp.sum(d_second, axis=0),
            jnp.sum(d_pack_wide[:, :width], axis=0),
            jnp.sum(d_pack_wide[:, 2 * width :], axis=0),
            jnp.sum(d_resid, axis=0),
            jnp.sum(grad_wide, axis=0),
        ]
    )
    d_upbias = jnp.sum(d_upper.astype(jnp.float32), axis=0)
    owned = (
        lax.psum_scatter(dw_qkv, "fsdp", scatter_dimension=0, tiled=True),
        lax.psum_scatter(dw_out, "fsdp", scatter_dimension=0, tiled=True),
        lax.psum_scatter(dw_up, "fsdp", scatter_dimension=0, tiled=True),
        lax.psum_scatter(dw_down, "fsdp", scatter_dimension=1, tiled=True),
        lax.psum_scatter(d_gains, "fsdp", scatter_dimension=1, tiled=True),
        lax.psum_scatter(d_biases, "fsdp", scatter_dimension=1, tiled=True),
        lax.psum_scatter(d_upbias, "fsdp", scatter_dimension=0, tiled=True),
    )
    summed = lax.psum((owned[0], owned[1], owned[2], owned[3], owned[4], owned[5], owned[6]), "seq")
    grad_qkv, grad_proj, grad_up, grad_down, grad_gains, grad_biases, grad_upbias = summed
    return (
        layer_out.reshape(img_count, tok_count, width),
        grad_in.reshape(img_count, tok_count, width),
        grad_qkv,
        grad_proj,
        grad_up,
        grad_down,
        grad_gains,
        grad_biases,
        grad_upbias,
    )


def solution(mesh):
    in_specs = (
        P("fsdp", "seq", None),
        P("fsdp", None),
        P("fsdp", None),
        P("fsdp", None),
        P("fsdp", None),
        P(None, "fsdp"),
        P(None, "fsdp"),
        P(None, "fsdp"),
        P("fsdp"),
        P("fsdp", "seq", None),
    )
    out_specs = (
        P("fsdp", "seq", None),
        P("fsdp", "seq", None),
        P("fsdp", None),
        P("fsdp", None),
        P("fsdp", None),
        P(None, "fsdp"),
        P(None, "fsdp"),
        P(None, "fsdp"),
        P("fsdp"),
    )

    def layer(*args):
        images = args[0].shape[0] // mesh.shape["fsdp"]
        planes = mesh.shape["fsdp"] // 2
        fits = mesh.shape["seq"] == 4 and images == 2 and planes * 2 == mesh.shape["fsdp"] and planes & (planes - 1) == 0
        plan = image_on_chip if fits else heads_over_seq
        return jax.shard_map(plan, mesh=mesh, in_specs=in_specs, out_specs=out_specs, check_vma=False)(*args)

    return layer
```

profile of v0, /device:TPU:0, one launch (start us, length us, event | category | flops | bytes accessed | tf_op | source)
XLA Modules:
  0.0 488.2 jit_solution(9114653307622102267)
XLA Ops:
  2.3 2.0 reshape.158
  10.8 6.2 %all-to-all-start = ((bf16[4,72,1792]{2,1,0:T(8,128)(2,1)}), bf16[4,72,1792]{2,1,0:T(8,128)(2,1)S(1)}, u32[]{:S(2)}, u32[]{:S(2)}) async-start(bf16[4,72,1792]{2,1,0:T(8,128)(2,1)} %broadcast_in_dim.60), calls=%async_computation | async-start | bytes 2064384 | tf_op jit(solution)/shard_map/all_to_all | solution.py:195
  22.9 2.4 dynamic-slice_bitcast_fusion.2
  27.2 9.0 %collective-permute-done.2 = bf16[256,1152]{1,0:T(8,128)(2,1)} collective-permute-done((bf16[256,1152]{1,0:T(8,128)(2,1)}, bf16[256,1152]{1,0:T(8,128)(2,1)}, u32[]{:S(2)}, u32[]{:S(2)}) %collective-permute-start.2) | collective-permute-done | bytes 589856 | tf_op jit(solution)/shard_map/ppermute | solution.py:177
  36.2 6.5 %all-to-all-done = bf16[4,72,1792]{2,1,0:T(8,128)(2,1)S(1)} async-done(((bf16[4,72,1792]{2,1,0:T(8,128)(2,1)}), bf16[4,72,1792]{2,1,0:T(8,128)(2,1)S(1)}, u32[]{:S(2)}, u32[]{:S(2)}) %all-to-all-start) | async-done | bytes 1032224 | tf_op jit(solution)/shard_map/all_to_all | solution.py:195
  48.0 4.4 all-to-all-start.1
  59.3 4.3 collective-permute-done.5.y_part
  65.1 1.9 collective-permute-done.4.x_part
  73.6 6.1 %collective-permute-done.11 = bf16[256,1152]{1,0:T(8,128)(2,1)} collective-permute-done((bf16[256,1152]{1,0:T(8,128)(2,1)}, bf16[256,1152]{1,0:T(8,128)(2,1)}, u32[]{:S(2)}, u32[]{:S(2)}) %collective-permute-start.11) | collective-permute-done | bytes 589856 | tf_op jit(solution)/shard_map/ppermute | solution.py:177
  79.7 6.0 %collective-permute-done.7.refs_0_ = bf16[3,72,896]{2,1,0:T(8,128)(2,1)S(1)} collective-permute-done((bf16[3,72,896]{2,1,0:T(8,128)(2,1)}, bf16[3,72,896]{2,1,0:T(8,128)(2,1)S(1)}, u32[]{:S(2)}, u32[]{:S(2)}) %collective-permute-start.7) | collective-permute-done | bytes 387104 | tf_op jit(solution)/shard_map/ppermute | solution.py:177
  85.7 3.6 collective-permute-done.8.refs_1_
  93.7 2.2 pad_maximum_fusion.2
  99.2 2.8 shard_map.169
  104.2 8.0 %shard_map.171 = (bf16[1024,1152]{1,0:T(8,128)(2,1)S(1)}, bf16[1024,1152]{1,0:T(8,128)(2,1)S(1)}, f32[1024,1]{1,0:T(8,128)S(1)}, bf16[1024,1152]{1,0:T(8,128)(2,1)S(1)}, bf16[1024,1728]{1,0:T(8,128)(2,1)S(1)}) custom-call(bf16[512,1152]{1,0:T(8,128)(2,1)S(1)} %copy-done.18, bf16[512,1152]{1,0:T(8,128)(2,1)} %collective-permute-done.6.other, ...), custom_call_target="tpu_custom_call" | custom-call | flops 589824 | bytes 589824 | tf_op jit(solution)/shard_map/pallas_call | solution.py:620
  116.7 2.5 maximum_select_fusion.1
  121.5 4.5 all-to-all-start.2
  126.0 2.0 collective-permute-start.16
  128.0 2.0 copy-done.2
  130.0 19.5 %shard_map.172 = (bf16[1024,640]{1,0:T(8,128)(2,1)S(1)}, bf16[8,1024,1024]{2,1,0:T(8,128)(2,1)}, f32[8,1,1024]{2,1,0:T(1,128)S(1)}) custom-call(bf16[1024,1728]{1,0:T(8,128)(2,1)S(1)} %copy-done.2, f32[1024,1]{1,0:T(8,128)S(1)} %broadcast_select_fusion.2.bias_ref), custom_call_target="tpu_custom_call" | custom-call | flops 8388608 | bytes 1769472 | tf_op jit(solution)/shard_map/pallas_call | solution.py:61
  151.2 4.9 %collective-permute-done.16.refs_0_ = bf16[3,72,2816]{2,1,0:T(8,128)(2,1)S(1)} collective-permute-done((bf16[3,72,2816]{2,1,0:T(8,128)(2,1)S(1)}, bf16[3,72,2816]{2,1,0:T(8,128)(2,1)S(1)}, u32[]{:S(2)}, u32[]{:S(2)}) %collective-permute-start.16) | collective-permute-done | bytes 1216544 | tf_op jit(solution)/shard_map/ppermute | solution.py:177
  158.4 3.0 shard_map.173
  164.3 1.9 collective-permute-start.18
  170.1 3.4 shard_map.175
  173.6 11.0 %shard_map.174 = (bf16[1024,1152]{1,0:T(8,128)(2,1)S(1)}, bf16[1152,1152]{1,0:T(8,128)(2,1)S(1)}, f32[512,1152]{1,0:T(8,128)S(1)}, bf16[1024,1152]{1,0:T(8,128)(...) custom-call(s32[5]{0:T(128)S(1)} %stack.66.where, bf16[1024,1152]{1,0:T(8,128)(2,1)S(1)} %copy-done.22, ...), custom_call_target="tpu_custom_call" | custom-call | flops 1179648 | bytes 1179648 | tf_op jit(solution)/shard_map/pallas_call | solution.py:678
  184.6 2.9 collective-permute-done.18.y_part
  192.3 11.0 %add_convert_fusion = (bf16[1024,2176]{1,0:T(8,128)(2,1)}, bf16[1024,2176]{1,0:T(8,128)(2,1)S(1)}) fusion(f32[2176]{0:T(1024)S(1)} %dynamic-slice_reduce_fusion, bf16[1024,1152]{1,0:T(8,128)(2,1)S(1)} %get-tuple-element.292.refs_0_, bf16[1152,2176]{1,0:T(8,128)(2,1)S(1)} %bitcast.105), kind=kOutput, calls=%fused_computation.2 | convolution fusion | flops 5178392576 | bytes 16294400 | tf_op jit(solution)/shard_map/dot_general | solution.py:853
  204.0 7.8 %convolution_convert_fusion = bf16[1152,2176]{1,0:T(8,128)(2,1)} fusion(bf16[1024,1152]{1,0:T(8,128)(2,1)S(1)} %constant_dynamic-update-slice_fusion.upstream, bf16[1024,2176]{1,0:T(8,128)(2,1)S(1)} %get-tuple-element.311), kind=kOutput, calls=%fused_computation | convolution fusion | flops 5136334848 | bytes 11829248 | tf_op jit(solution)/shard_map/dot_general | solution.py:861
  211.7 5.1 %all-to-all-start.3 = ((bf16[4,288,2176]{2,1,0:T(8,128)(2,1)}), bf16[4,288,2176]{2,1,0:T(8,128)(2,1)}, u32[]{:S(2)}, u32[]{:S(2)}) async-start(bf16[4,288,2176]{2,1,0:T(8,128)(2,1)} %bitcast.114), calls=%async_computation.3 | async-start | bytes 10027008 | tf_op jit(solution)/shard_map/all_to_all | solution.py:195
  216.9 3.2 shard_map.176
  220.7 6.4 %multiply_convert_fusion.refs_1_ = bf16[1024,2176]{1,0:T(8,128)(2,1)S(1)} fusion(bf16[1024,2176]{1,0:T(8,128)(2,1)S(1)} %copy-done.85, bf16[1024,1152]{1,0:T(8,128)(2,1)S(1)} %copy-done.6, bf16[1152,2176]{1,0:T(8,128)(2,1)S(1)} %bitcast.103), kind=kOutput, calls=%fused_computation.1 | convolution fusion | flops 5140512768 | bytes 16285696 | tf_op jit(solution)/shard_map/dot_general | solution.py:853
  227.2 7.5 %convolution_convert_fusion.2.part = bf16[1024,1152]{1,0:T(8,128)(2,1)} fusion(bf16[1024,2176]{1,0:T(8,128)(2,1)S(1)} %multiply_convert_fusion.refs_1_, bf16[1152,2176]{1,0:T(8,128)(2,1)S(1)} %bitcast.108), kind=kOutput, calls=%fused_computation.9 | convolution fusion | flops 5135007744 | bytes 11829248 | tf_op jit(solution)/shard_map/dot_general | solution.py:857
  234.8 6.7 %convolution_convert_fusion.1 = bf16[1024,1152]{1,0:T(8,128)(2,1)S(1)} fusion(bf16[1024,2176]{1,0:T(8,128)(2,1)S(1)} %bitcast.124, bf16[1152,2176]{1,0:T(8,128)(2,1)S(1)} %bitcast.104), kind=kOutput, calls=%fused_computation.8 | convolution fusion | flops 5135007744 | bytes 11829248 | tf_op jit(solution)/shard_map/dot_general | solution.py:857
  244.5 11.3 %shard_map.177 = (bf16[2,4,72,1024]{3,2,1,0:T(8,128)(2,1)}, bf16[2,4,72,1024]{3,2,1,0:T(8,128)(2,1)}, bf16[2,4,72,1152]{3,2,1,0:T(8,128)(2,1)}, bf16[2,4,72,1152]{3,2,1,0:T(8,128)(2,1)}, f32[8,2176]{1,0:T(8,128)}) custom-call(s32[5]{0:T(128)} %copy-done.63, bf16[1024,1152]{1,0:T(8,128)(2,1)} %copy-done.25, bf16[1024,2176]{1,0:T(8,128)(2,1)} %copy-done.72), custom_call_target="tpu_custom_call" | custom-call | flops 1179648 | bytes 2506752 | tf_op jit(solution)/shard_map/pallas_call | solution.py:382
  257.0 2.2 add_convert_fusion.1
  265.1 7.8 %shard_map.178 = (bf16[1024,1152]{1,0:T(8,128)(2,1)S(1)}, bf16[1024,576]{1,0:T(8,128)(2,1)S(1)}, f32[512,1152]{1,0:T(8,128)S(1)}, f32[8,1152]{1,0:T(8,128)S(1)}) custom-call(s32[5]{0:T(128)S(1)} %copy-done.64, bf16[1024,1152]{1,0:T(8,128)(2,1)} %convolution_convert_fusion.2.part, bf16[1024,1152]{1,0:T(8,128)(2,1)} %collective-permute-done.23.arrived, ...), custom_call_target="tpu_custom_call" | custom-call | tf_op jit(solution)/shard_map/pallas_call | solution.py:760
  275.4 2.7 convolution_convert_fusion.3
  278.2 2.4 copy.82.d_out_ref
  280.6 26.3 %shard_map.179.refs_2_ = bf16[1024,1728]{1,0:T(8,128)(2,1)} custom-call(bf16[1024,1728]{1,0:T(8,128)(2,1)} %copy-done.1, bf16[1024,576]{1,0:T(8,128)(2,1)} %copy.82.d_out_ref, bf16[1024,640]{1,0:T(8,128)(2,1)} %copy-done.8, bf16[8,1024,1024]{2,1,0:T(8,128)(2,1)} %get-tuple-element.322.probs_ref, f32[8,1,1024]{2,1,0:T(1,128)} %copy-done.68), custom_call_target="tpu_custom_call" | custom-call | flops 8388608 | bytes 1769472 | tf_op jit(solution)/shard_map/pallas_call | solution.py:132
  306.9 2.2 shard_map.180
  310.8 2.4 collective-permute-start.29
  316.2 13.1 %shard_map.181 = (bf16[2,4,72,1152]{3,2,1,0:T(8,128)(2,1)}, bf16[2,4,72,1152]{3,2,1,0:T(8,128)(2,1)}, bf16[2,4,72,1280]{3,2,1,0:T(8,128)(2,1)}, bf16[2,4,72,1280]{3,2,1,0:T(8,128)(2,1)}) custom-call(s32[5]{0:T(128)} %copy-done.63, bf16[1024,1152]{1,0:T(8,128)(2,1)} %copy-done.19, bf16[1024,1152]{1,0:T(8,128)(2,1)} %copy-done.20, ...), custom_call_target="tpu_custom_call" | custom-call | flops 1179648 | bytes 2801664 | tf_op jit(solution)/shard_map/pallas_call | solution.py:382
  333.0 8.3 %fusion.2.part = bf16[1024,1152]{1,0:T(8,128)(2,1)S(1)} fusion(bf16[1024,1728]{1,0:T(8,128)(2,1)} %shard_map.179.refs_2_, bf16[1152,1792]{1,0:T(8,128)(2,1)} %bitcast.95), kind=kOutput, calls=%fused_computation.10 | convolution fusion | flops 4078043136 | bytes 10027008 | tf_op jit(solution)/shard_map/dot_general | solution.py:857
  344.5 5.3 %all-to-all-start.4 = ((bf16[4,72,2176]{2,1,0:T(8,128)(2,1)}), bf16[4,72,2176]{2,1,0:T(8,128)(2,1)}, u32[]{:S(2)}, u32[]{:S(2)}) async-start(bf16[4,72,2176]{2,1,0:T(8,128)(2,1)} %copy-done.12), calls=%async_computation.4 | async-start | bytes 2506752 | tf_op jit(solution)/shard_map/all_to_all | solution.py:195
  349.9 3.8 shard_map.183
  361.0 6.5 %collective-permute-done.33.from_x = bf16[2,1,72,1024]{3,2,1,0:T(8,128)(2,1)S(1)} collective-permute-done((bf16[2,1,72,1024]{3,2,1,0:T(8,128)(2,1)S(1)}, bf16[2,1,72,1024]{3,2,1,0:T(8,128)(2,1)S(1)}, u32[]{:S(2)}, u32[]{:S(2)}) %collective-permute-start.33) | collective-permute-done | bytes 294944 | tf_op jit(solution)/shard_map/ppermute | solution.py:177
  367.5 5.1 %collective-permute-done.34.from_y = bf16[2,1,72,1152]{3,2,1,0:T(8,128)(2,1)S(1)} collective-permute-done((bf16[2,1,72,1152]{3,2,1,0:T(8,128)(2,1)S(1)}, bf16[2,1,72,1152]{3,2,1,0:T(8,128)(2,1)S(1)}, u32[]{:S(2)}, u32[]{:S(2)}) %collective-permute-start.34) | collective-permute-done | bytes 331808 | tf_op jit(solution)/shard_map/ppermute | solution.py:177
  372.6 3.9 shard_map.185
  383.3 13.0 %collective-permute-done.38.from_y = bf16[1,72,1024]{2,1,0:T(8,128)(2,1)} collective-permute-done((bf16[1,72,1024]{2,1,0:T(8,128)(2,1)}, bf16[1,72,1024]{2,1,0:T(8,128)(2,1)}, u32[]{:S(2)}, u32[]{:S(2)}) %collective-permute-start.38) | collective-permute-done | bytes 147488 | tf_op jit(solution)/shard_map/ppermute | solution.py:177
  397.1 3.5 shard_map.187
  400.6 5.2 %all-to-all-start.5 = ((bf16[4,72,2432]{2,1,0:T(8,128)(2,1)}), bf16[4,72,2432]{2,1,0:T(8,128)(2,1)}, u32[]{:S(2)}, u32[]{:S(2)}) async-start(bf16[4,72,2432]{2,1,0:T(8,128)(2,1)} %shard_map.187), calls=%async_computation.5 | async-start | bytes 2801664 | tf_op jit(solution)/shard_map/all_to_all | solution.py:195
  410.0 4.2 collective-permute-start.44
  417.0 4.7 collective-permute-done.47
  425.8 2.5 maximum_select_fusion.3
  428.3 7.1 %collective-permute-done.45 = f32[18,128]{1,0:T(8,128)S(1)} collective-permute-done((f32[18,128]{1,0:T(8,128)S(1)}, f32[18,128]{1,0:T(8,128)S(1)}, u32[]{:S(2)}, u32[]{:S(2)}) %collective-permute-start.45) | collective-permute-done | bytes 9248 | tf_op jit(solution)/shard_map/ppermute | solution.py:177
  435.5 3.4 collective-permute-done.42.refs_2_
  447.8 2.3 collective-permute-done.54
  451.9 3.8 collective-permute-done.52.refs_3_
  456.5 2.5 maximum_select_fusion.2
  458.9 2.0 collective-permute-done.49.refs_4_
  464.7 2.0 collective-permute-start.59
  472.9 2.6 collective-permute-start.61
  477.5 2.3 shard_map.192
  479.8 2.3 shard_map.193
  482.0 3.0 shard_map.194
  (403 shorter events, 145.4 us)
Async XLA Ops:
  10.8 31.9 %all-to-all-start = ((bf16[4,72,1792]{2,1,0:T(8,128)(2,1)}), bf16[4,72,1792]{2,1,0:T(8,128)(2,1)S(1)}, u32[]{:S(2)}, u32[]{:S(2)}) async-start(bf16[4,72,1792]{2,1,0:T(8,128)(2,1)} %broadcast_in_dim.60), calls=%async_computation | async-start | bytes 2064384 | tf_op jit(solution)/shard_map/all_to_all | solution.py:195
  18.3 7.0 %collective-permute-start.3 = (bf16[144,2816]{1,0:T(8,128)(2,1)}, bf16[144,2816]{1,0:T(8,128)(2,1)}, u32[]{:S(2)}, u32[]{:S(2)}) collective-permute-start(bf16[144,2816]{1,0:T(8,128)(2,1)} %get-tuple-element.478), channel_id=1, source_target_pairs={{0,4},{1,5},{2,6},{3,7},{4,0},{5,1},{6,2},{7,3},{8,12},{9,13},{10,... | collective-permute-start | bytes 2433032 | tf_op jit(solution)/shard_map/ppermute | solution.py:177
  20.0 16.2 %collective-permute-start.2 = (bf16[256,1152]{1,0:T(8,128)(2,1)}, bf16[256,1152]{1,0:T(8,128)(2,1)}, u32[]{:S(2)}, u32[]{:S(2)}) collective-permute-start(bf16[256,1152]{1,0:T(8,128)(2,1)} %get-tuple-element.495), channel_id=1, source_target_pairs={{0,1},{1,0},{2,5},{3,4},{4,3},{5,2},{6,7},{7,6},{8,9},{9,8},{10,13... | collective-permute-start | bytes 1769480 | tf_op jit(solution)/shard_map/ppermute | solution.py:177
  21.5 14.7 %collective-permute-start.1 = (bf16[256,1152]{1,0:T(8,128)(2,1)}, bf16[256,1152]{1,0:T(8,128)(2,1)}, u32[]{:S(2)}, u32[]{:S(2)}) collective-permute-start(bf16[256,1152]{1,0:T(8,128)(2,1)} %get-tuple-element.242), channel_id=1, source_target_pairs={{2,4},{3,5},{4,2},{5,3},{10,12},{11,13},{12,10},{13,11},{18,20},{1... | collective-permute-start | bytes 1769480 | tf_op jit(solution)/shard_map/ppermute | solution.py:177
  45.0 18.6 %collective-permute-start.5 = (bf16[3,72,1792]{2,1,0:T(8,128)(2,1)}, bf16[3,72,1792]{2,1,0:T(8,128)(2,1)}, u32[]{:S(2)}, u32[]{:S(2)}) collective-permute-start(bf16[3,72,1792]{2,1,0:T(8,128)(2,1)} %pad_maximum_fusion.4.own), channel_id=1, source_target_pairs={{0,2},{1,3},{2,0},{3,1},{4,6},{5,7},{6,4},{7,5},{8,10},{9,11},{10,... | collective-permute-start | bytes 2322440 | tf_op jit(solution)/shard_map/ppermute | solution.py:177
  46.5 20.5 %collective-permute-start.4 = (bf16[3,72,1792]{2,1,0:T(8,128)(2,1)}, bf16[3,72,1792]{2,1,0:T(8,128)(2,1)}, u32[]{:S(2)}, u32[]{:S(2)}) collective-permute-start(bf16[3,72,1792]{2,1,0:T(8,128)(2,1)} %pad_maximum_fusion.4.own), channel_id=1, source_target_pairs={{0,1},{1,0},{2,3},{3,2},{4,5},{5,4},{6,7},{7,6},{8,9},{9,8},{10,11... | collective-permute-start | bytes 2322440 | tf_op jit(solution)/shard_map/ppermute | solution.py:177
  48.0 41.4 %all-to-all-start.1 = ((bf16[4,72,2816]{2,1,0:T(8,128)(2,1)}), bf16[4,72,2816]{2,1,0:T(8,128)(2,1)}, u32[]{:S(2)}, u32[]{:S(2)}) async-start(bf16[4,72,2816]{2,1,0:T(8,128)(2,1)} %broadcast_in_dim.62), calls=%async_computation.1 | async-start | bytes 3244032 | tf_op jit(solution)/shard_map/all_to_all | solution.py:195
  54.8 12.2 %collective-permute-start.6 = (bf16[512,1152]{1,0:T(8,128)(2,1)S(1)}, bf16[512,1152]{1,0:T(8,128)(2,1)}, u32[]{:S(2)}, u32[]{:S(2)}) collective-permute-start(bf16[512,1152]{1,0:T(8,128)(2,1)S(1)} %pad_maximum_fusion.1.half), channel_id=1, source_target_pairs={{0,4},{1,5},{2,6},{3,7},{4,0},{5,1},{6,2},{7,3},{8,12},{9,13},{10,... | collective-permute-start | bytes 3538952 | tf_op jit(solution)/shard_map/ppermute | solution.py:177
  56.6 17.0 %collective-permute-start.9 = (bf16[144,2176]{1,0:T(8,128)(2,1)}, bf16[144,2176]{1,0:T(8,128)(2,1)}, u32[]{:S(2)}, u32[]{:S(2)}) collective-permute-start(bf16[144,2176]{1,0:T(8,128)(2,1)} %get-tuple-element.483), channel_id=1, source_target_pairs={{0,4},{1,5},{2,6},{3,7},{4,0},{5,1},{6,2},{7,3},{8,12},{9,13},{10,... | collective-permute-start | bytes 1880072 | tf_op jit(solution)/shard_map/ppermute | solution.py:177
  58.8 21.0 %collective-permute-start.11 = (bf16[256,1152]{1,0:T(8,128)(2,1)}, bf16[256,1152]{1,0:T(8,128)(2,1)}, u32[]{:S(2)}, u32[]{:S(2)}) collective-permute-start(bf16[256,1152]{1,0:T(8,128)(2,1)} %get-tuple-element.253), channel_id=1, source_target_pairs={{0,1},{1,0},{2,5},{3,4},{4,3},{5,2},{6,7},{7,6},{8,9},{9,8},{10,13... | collective-permute-start | bytes 1769480 | tf_op jit(solution)/shard_map/ppermute | solution.py:177
  63.6 16.1 %collective-permute-start.10 = (bf16[256,1152]{1,0:T(8,128)(2,1)}, bf16[256,1152]{1,0:T(8,128)(2,1)}, u32[]{:S(2)}, u32[]{:S(2)}) collective-permute-start(bf16[256,1152]{1,0:T(8,128)(2,1)} %get-tuple-element.259), channel_id=1, source_target_pairs={{2,4},{3,5},{4,2},{5,3},{10,12},{11,13},{12,10},{13,11},{18,20},{1... | collective-permute-start | bytes 1769480 | tf_op jit(solution)/shard_map/ppermute | solution.py:177
  70.6 15.1 %collective-permute-start.7 = (bf16[3,72,896]{2,1,0:T(8,128)(2,1)}, bf16[3,72,896]{2,1,0:T(8,128)(2,1)S(1)}, u32[]{:S(2)}, u32[]{:S(2)}) collective-permute-start(bf16[3,72,896]{2,1,0:T(8,128)(2,1)} %slice.148), channel_id=1, source_target_pairs={{0,1},{1,0},{2,3},{3,2},{4,5},{5,4},{6,7},{7,6},{8,9},{9,8},{10,11... | collective-permute-start | bytes 1161224 | tf_op jit(solution)/shard_map/ppermute | solution.py:177
  72.1 17.2 %collective-permute-start.8 = (bf16[3,72,896]{2,1,0:T(8,128)(2,1)}, bf16[3,72,896]{2,1,0:T(8,128)(2,1)S(1)}, u32[]{:S(2)}, u32[]{:S(2)}) collective-permute-start(bf16[3,72,896]{2,1,0:T(8,128)(2,1)} %slice.149), channel_id=1, source_target_pairs={{0,2},{1,3},{2,0},{3,1},{4,6},{5,7},{6,4},{7,5},{8,10},{9,11},{10,... | collective-permute-start | bytes 1161224 | tf_op jit(solution)/shard_map/ppermute | solution.py:177
  91.0 29.4 %collective-permute-start.14 = (bf16[3,72,2816]{2,1,0:T(8,128)(2,1)S(1)}, bf16[3,72,2816]{2,1,0:T(8,128)(2,1)}, u32[]{:S(2)}, u32[]{:S(2)}) collective-permute-start(bf16[3,72,2816]{2,1,0:T(8,128)(2,1)S(1)} %pad_maximum_fusion.own), channel_id=1, source_target_pairs={{0,2},{1,3},{2,0},{3,1},{4,6},{5,7},{6,4},{7,5},{8,10},{9,11},{10,... | collective-permute-start | bytes 3649544 | tf_op jit(solution)/shard_map/ppermute | solution.py:177
  91.5 28.8 %collective-permute-start.13 = (bf16[3,72,2816]{2,1,0:T(8,128)(2,1)S(1)}, bf16[3,72,2816]{2,1,0:T(8,128)(2,1)}, u32[]{:S(2)}, u32[]{:S(2)}) collective-permute-start(bf16[3,72,2816]{2,1,0:T(8,128)(2,1)S(1)} %pad_maximum_fusion.own), channel_id=1, source_target_pairs={{0,1},{1,0},{2,3},{3,2},{4,5},{5,4},{6,7},{7,6},{8,9},{9,8},{10,11... | collective-permute-start | bytes 3649544 | tf_op jit(solution)/shard_map/ppermute | solution.py:177
  95.9 24.4 %collective-permute-start.15 = (bf16[512,1152]{1,0:T(8,128)(2,1)}, bf16[512,1152]{1,0:T(8,128)(2,1)}, u32[]{:S(2)}, u32[]{:S(2)}) collective-permute-start(bf16[512,1152]{1,0:T(8,128)(2,1)} %pad_maximum_fusion.2), channel_id=1, source_target_pairs={{0,4},{1,5},{2,6},{3,7},{4,0},{5,1},{6,2},{7,3},{8,12},{9,13},{10,... | collective-permute-start | bytes 3538952 | tf_op jit(solution)/shard_map/ppermute | solution.py:177
  121.5 35.7 %all-to-all-start.2 = ((bf16[4,72,2176]{2,1,0:T(8,128)(2,1)}), bf16[4,72,2176]{2,1,0:T(8,128)(2,1)}, u32[]{:S(2)}, u32[]{:S(2)}) async-start(bf16[4,72,2176]{2,1,0:T(8,128)(2,1)} %broadcast_in_dim.66), calls=%async_computation.2 | async-start | bytes 2506752 | tf_op jit(solution)/shard_map/all_to_all | solution.py:195
  126.0 30.1 %collective-permute-start.16 = (bf16[3,72,2816]{2,1,0:T(8,128)(2,1)S(1)}, bf16[3,72,2816]{2,1,0:T(8,128)(2,1)S(1)}, u32[]{:S(2)}, u32[]{:S(2)}) collective-permute-start(bf16[3,72,2816]{2,1,0:T(8,128)(2,1)S(1)} %pad_maximum_fusion.own), channel_id=1, source_target_pairs={{0,3},{1,2},{2,1},{3,0},{4,7},{5,6},{6,5},{7,4},{8,11},{9,10},{10,... | collective-permute-start | bytes 3649544 | tf_op jit(solution)/shard_map/ppermute | solution.py:177
  157.2 16.4 %collective-permute-start.19 = (bf16[1024,640]{1,0:T(8,128)(2,1)}, bf16[1024,640]{1,0:T(8,128)(2,1)}, u32[]{:S(2)}, u32[]{:S(2)}) collective-permute-start(bf16[1024,640]{1,0:T(8,128)(2,1)} %copy-done.8), channel_id=1, source_target_pairs={{0,4},{1,5},{2,6},{3,7},{4,0},{5,1},{6,2},{7,3},{8,12},{9,13},{10,... | collective-permute-start | bytes 3932168 | tf_op jit(solution)/shard_map/ppermute | solution.py:177
  161.4 12.1 %collective-permute-start.20 = (bf16[1152,640]{1,0:T(8,128)(2,1)}, bf16[1152,640]{1,0:T(8,128)(2,1)}, u32[]{:S(2)}, u32[]{:S(2)}) collective-permute-start(bf16[1152,640]{1,0:T(8,128)(2,1)} %bitcast.34.w_mine), channel_id=1, source_target_pairs={{0,4},{1,5},{2,6},{3,7},{4,0},{5,1},{6,2},{7,3},{8,12},{9,13},{10,... | collective-permute-start | bytes 4423688 | tf_op jit(solution)/shard_map/ppermute | solution.py:177
  164.3 23.3 %collective-permute-start.18 = (bf16[3,72,2176]{2,1,0:T(8,128)(2,1)}, bf16[3,72,2176]{2,1,0:T(8,128)(2,1)}, u32[]{:S(2)}, u32[]{:S(2)}) collective-permute-start(bf16[3,72,2176]{2,1,0:T(8,128)(2,1)} %pad_maximum_fusion.3.own), channel_id=1, source_target_pairs={{0,2},{1,3},{2,0},{3,1},{4,6},{5,7},{6,4},{7,5},{8,10},{9,11},{10,... | collective-permute-start | bytes 2820104 | tf_op jit(solution)/shard_map/ppermute | solution.py:177
  166.2 22.8 %collective-permute-start.17 = (bf16[3,72,2176]{2,1,0:T(8,128)(2,1)}, bf16[3,72,2176]{2,1,0:T(8,128)(2,1)}, u32[]{:S(2)}, u32[]{:S(2)}) collective-permute-start(bf16[3,72,2176]{2,1,0:T(8,128)(2,1)} %pad_maximum_fusion.3.own), channel_id=1, source_target_pairs={{0,1},{1,0},{2,3},{3,2},{4,5},{5,4},{6,7},{7,6},{8,9},{9,8},{10,11... | collective-permute-start | bytes 2820104 | tf_op jit(solution)/shard_map/ppermute | solution.py:177
  190.1 13.3 %collective-permute-start.21 = (bf16[3,72,1024]{2,1,0:T(8,128)(2,1)S(1)}, bf16[3,72,1024]{2,1,0:T(8,128)(2,1)S(1)}, u32[]{:S(2)}, u32[]{:S(2)}) collective-permute-start(bf16[3,72,1024]{2,1,0:T(8,128)(2,1)S(1)} %slice.152), channel_id=1, source_target_pairs={{0,1},{1,0},{2,3},{3,2},{4,5},{5,4},{6,7},{7,6},{8,9},{9,8},{10,11... | collective-permute-start | bytes 1327112 | tf_op jit(solution)/shard_map/ppermute | solution.py:177
  192.0 12.0 %collective-permute-start.22 = (bf16[3,72,1152]{2,1,0:T(8,128)(2,1)S(1)}, bf16[3,72,1152]{2,1,0:T(8,128)(2,1)S(1)}, u32[]{:S(2)}, u32[]{:S(2)}) collective-permute-start(bf16[3,72,1152]{2,1,0:T(8,128)(2,1)S(1)} %slice.153), channel_id=1, source_target_pairs={{0,2},{1,3},{2,0},{3,1},{4,6},{5,7},{6,4},{7,5},{8,10},{9,11},{10,... | collective-permute-start | bytes 1493000 | tf_op jit(solution)/shard_map/ppermute | solution.py:177
  211.7 119.2 %all-to-all-start.3 = ((bf16[4,288,2176]{2,1,0:T(8,128)(2,1)}), bf16[4,288,2176]{2,1,0:T(8,128)(2,1)}, u32[]{:S(2)}, u32[]{:S(2)}) async-start(bf16[4,288,2176]{2,1,0:T(8,128)(2,1)} %bitcast.114), calls=%async_computation.3 | async-start | bytes 10027008 | tf_op jit(solution)/shard_map/all_to_all | solution.py:195
  234.7 24.5 %collective-permute-start.23 = (bf16[1024,1152]{1,0:T(8,128)(2,1)}, bf16[1024,1152]{1,0:T(8,128)(2,1)}, u32[]{:S(2)}, u32[]{:S(2)}) collective-permute-start(bf16[1024,1152]{1,0:T(8,128)(2,1)} %convolution_convert_fusion.2.part), channel_id=1, source_target_pairs={{0,4},{1,5},{2,6},{3,7},{4,0},{5,1},{6,2},{7,3},{8,12},{9,13},{10,... | collective-permute-start | bytes 7077896 | tf_op jit(solution)/shard_map/ppermute | solution.py:177
  243.9 13.0 %collective-permute-start.24 = (bf16[512,1152]{1,0:T(8,128)(2,1)}, bf16[512,1152]{1,0:T(8,128)(2,1)}, u32[]{:S(2)}, u32[]{:S(2)}) collective-permute-start(bf16[512,1152]{1,0:T(8,128)(2,1)} %slice.193), channel_id=1, source_target_pairs={{0,4},{1,5},{2,6},{3,7},{4,0},{5,1},{6,2},{7,3},{8,12},{9,13},{10,... | collective-permute-start | bytes 3538952 | tf_op jit(solution)/shard_map/ppermute | solution.py:177
  259.2 47.7 %collective-permute-start.25 = (bf16[2,4,72,1024]{3,2,1,0:T(8,128)(2,1)}, bf16[2,4,72,1024]{3,2,1,0:T(8,128)(2,1)S(1)}, u32[]{:S(2)}, u32[]{:S(2)}) collective-permute-start(bf16[2,4,72,1024]{3,2,1,0:T(8,128)(2,1)} %get-tuple-element.314), channel_id=1, source_target_pairs={{0,1},{1,0},{2,3},{3,2},{4,5},{5,4},{6,7},{7,6},{8,9},{9,8},{10,11... | collective-permute-start | bytes 3538952 | tf_op jit(solution)/shard_map/ppermute | solution.py:177
  260.4 46.5 %collective-permute-start.26 = (bf16[2,4,72,1152]{3,2,1,0:T(8,128)(2,1)}, bf16[2,4,72,1152]{3,2,1,0:T(8,128)(2,1)S(1)}, u32[]{:S(2)}, u32[]{:S(2)}) collective-permute-start(bf16[2,4,72,1152]{3,2,1,0:T(8,128)(2,1)} %get-tuple-element.315), channel_id=1, source_target_pairs={{0,2},{1,3},{2,0},{3,1},{4,6},{5,7},{6,4},{7,5},{8,10},{9,11},{10,... | collective-permute-start | bytes 3981320 | tf_op jit(solution)/shard_map/ppermute | solution.py:177
  262.8 44.1 %collective-permute-start.28 = (bf16[256,1152]{1,0:T(8,128)(2,1)}, bf16[256,1152]{1,0:T(8,128)(2,1)}, u32[]{:S(2)}, u32[]{:S(2)}) collective-permute-start(bf16[256,1152]{1,0:T(8,128)(2,1)} %get-tuple-element.491), channel_id=1, source_target_pairs={{0,1},{1,0},{2,5},{3,4},{4,3},{5,2},{6,7},{7,6},{8,9},{9,8},{10,13... | collective-permute-start | bytes 1769480 | tf_op jit(solution)/shard_map/ppermute | solution.py:177
  263.6 43.2 %collective-permute-start.27 = (bf16[256,1152]{1,0:T(8,128)(2,1)}, bf16[256,1152]{1,0:T(8,128)(2,1)}, u32[]{:S(2)}, u32[]{:S(2)}) collective-permute-start(bf16[256,1152]{1,0:T(8,128)(2,1)} %get-tuple-element.401), channel_id=1, source_target_pairs={{2,4},{3,5},{4,2},{5,3},{10,12},{11,13},{12,10},{13,11},{18,20},{1... | collective-permute-start | bytes 1769480 | tf_op jit(solution)/shard_map/ppermute | solution.py:177
  310.8 18.5 %collective-permute-start.29 = (bf16[4,72,1024]{2,1,0:T(8,128)(2,1)}, bf16[4,72,1024]{2,1,0:T(8,128)(2,1)S(1)}, u32[]{:S(2)}, u32[]{:S(2)}) collective-permute-start(bf16[4,72,1024]{2,1,0:T(8,128)(2,1)} %get-tuple-element.330), channel_id=1, source_target_pairs={{0,2},{1,3},{2,0},{3,1},{4,6},{5,7},{6,4},{7,5},{8,10},{9,11},{10,... | collective-permute-start | bytes 1769480 | tf_op jit(solution)/shard_map/ppermute | solution.py:177
  313.2 16.9 %collective-permute-start.30 = (bf16[4,72,1152]{2,1,0:T(8,128)(2,1)S(1)}, bf16[4,72,1152]{2,1,0:T(8,128)(2,1)S(1)}, u32[]{:S(2)}, u32[]{:S(2)}) collective-permute-start(bf16[4,72,1152]{2,1,0:T(8,128)(2,1)S(1)} %get-tuple-element.331), channel_id=1, source_target_pairs={{0,1},{1,0},{2,3},{3,2},{4,5},{5,4},{6,7},{7,6},{8,9},{9,8},{10,11... | collective-permute-start | bytes 1990664 | tf_op jit(solution)/shard_map/ppermute | solution.py:177
  331.0 41.6 %collective-permute-start.31 = (bf16[2,4,72,1152]{3,2,1,0:T(8,128)(2,1)}, bf16[2,4,72,1152]{3,2,1,0:T(8,128)(2,1)}, u32[]{:S(2)}, u32[]{:S(2)}) collective-permute-start(bf16[2,4,72,1152]{3,2,1,0:T(8,128)(2,1)} %get-tuple-element.348), channel_id=1, source_target_pairs={{0,1},{1,0},{2,3},{3,2},{4,5},{5,4},{6,7},{7,6},{8,9},{9,8},{10,11... | collective-permute-start | bytes 3981320 | tf_op jit(solution)/shard_map/ppermute | solution.py:177
  331.9 40.7 %collective-permute-start.32 = (bf16[2,4,72,1280]{3,2,1,0:T(8,128)(2,1)}, bf16[2,4,72,1280]{3,2,1,0:T(8,128)(2,1)}, u32[]{:S(2)}, u32[]{:S(2)}) collective-permute-start(bf16[2,4,72,1280]{3,2,1,0:T(8,128)(2,1)} %get-tuple-element.349), channel_id=1, source_target_pairs={{0,2},{1,3},{2,0},{3,1},{4,6},{5,7},{6,4},{7,5},{8,10},{9,11},{10,... | collective-permute-start | bytes 4423688 | tf_op jit(solution)/shard_map/ppermute | solution.py:177
  342.4 13.4 %collective-permute-start.35 = (bf16[512,1152]{1,0:T(8,128)(2,1)}, bf16[512,1152]{1,0:T(8,128)(2,1)S(1)}, u32[]{:S(2)}, u32[]{:S(2)}) collective-permute-start(bf16[512,1152]{1,0:T(8,128)(2,1)} %slice.197), channel_id=1, source_target_pairs={{0,4},{1,5},{2,6},{3,7},{4,0},{5,1},{6,2},{7,3},{8,12},{9,13},{10,... | collective-permute-start | bytes 3538952 | tf_op jit(solution)/shard_map/ppermute | solution.py:177
  344.5 52.5 %all-to-all-start.4 = ((bf16[4,72,2176]{2,1,0:T(8,128)(2,1)}), bf16[4,72,2176]{2,1,0:T(8,128)(2,1)}, u32[]{:S(2)}, u32[]{:S(2)}) async-start(bf16[4,72,2176]{2,1,0:T(8,128)(2,1)} %copy-done.12), calls=%async_computation.4 | async-start | bytes 2506752 | tf_op jit(solution)/shard_map/all_to_all | solution.py:195
  353.7 18.9 %collective-permute-start.34 = (bf16[2,1,72,1152]{3,2,1,0:T(8,128)(2,1)S(1)}, bf16[2,1,72,1152]{3,2,1,0:T(8,128)(2,1)S(1)}, u32[]{:S(2)}, u32[]{:S(2)}) collective-permute-start(bf16[2,1,72,1152]{3,2,1,0:T(8,128)(2,1)S(1)} %get-tuple-element.354), channel_id=1, source_target_pairs={{0,2},{1,3},{2,0},{3,1},{4,6},{5,7},{6,4},{7,5},{8,10},{9,11},{10,... | collective-permute-start | bytes 995336 | tf_op jit(solution)/shard_map/ppermute | solution.py:177
  354.7 12.8 %collective-permute-start.33 = (bf16[2,1,72,1024]{3,2,1,0:T(8,128)(2,1)S(1)}, bf16[2,1,72,1024]{3,2,1,0:T(8,128)(2,1)S(1)}, u32[]{:S(2)}, u32[]{:S(2)}) collective-permute-start(bf16[2,1,72,1024]{3,2,1,0:T(8,128)(2,1)S(1)} %get-tuple-element.353), channel_id=1, source_target_pairs={{0,1},{1,0},{2,3},{3,2},{4,5},{5,4},{6,7},{7,6},{8,9},{9,8},{10,11... | collective-permute-start | bytes 884744 | tf_op jit(solution)/shard_map/ppermute | solution.py:177
  376.5 20.5 %collective-permute-start.37 = (bf16[4,72,1280]{2,1,0:T(8,128)(2,1)}, bf16[4,72,1280]{2,1,0:T(8,128)(2,1)S(1)}, u32[]{:S(2)}, u32[]{:S(2)}) collective-permute-start(bf16[4,72,1280]{2,1,0:T(8,128)(2,1)} %get-tuple-element.367), channel_id=1, source_target_pairs={{0,1},{1,0},{2,3},{3,2},{4,5},{5,4},{6,7},{7,6},{8,9},{9,8},{10,11... | collective-permute-start | bytes 2211848 | tf_op jit(solution)/shard_map/ppermute | solution.py:177
  377.4 19.7 %collective-permute-start.36 = (bf16[4,72,1152]{2,1,0:T(8,128)(2,1)}, bf16[4,72,1152]{2,1,0:T(8,128)(2,1)}, u32[]{:S(2)}, u32[]{:S(2)}) collective-permute-start(bf16[4,72,1152]{2,1,0:T(8,128)(2,1)} %get-tuple-element.366), channel_id=1, source_target_pairs={{0,2},{1,3},{2,0},{3,1},{4,6},{5,7},{6,4},{7,5},{8,10},{9,11},{10,... | collective-permute-start | bytes 1990664 | tf_op jit(solution)/shard_map/ppermute | solution.py:177
  380.5 16.5 %collective-permute-start.39 = (bf16[1,72,1152]{2,1,0:T(8,128)(2,1)}, bf16[1,72,1152]{2,1,0:T(8,128)(2,1)}, u32[]{:S(2)}, u32[]{:S(2)}) collective-permute-start(bf16[1,72,1152]{2,1,0:T(8,128)(2,1)} %get-tuple-element.375), channel_id=1, source_target_pairs={{0,1},{1,0},{2,3},{3,2},{4,5},{5,4},{6,7},{7,6},{8,9},{9,8},{10,11... | collective-permute-start | bytes 497672 | tf_op jit(solution)/shard_map/ppermute | solution.py:177
  381.7 14.6 %collective-permute-start.38 = (bf16[1,72,1024]{2,1,0:T(8,128)(2,1)}, bf16[1,72,1024]{2,1,0:T(8,128)(2,1)}, u32[]{:S(2)}, u32[]{:S(2)}) collective-permute-start(bf16[1,72,1024]{2,1,0:T(8,128)(2,1)} %get-tuple-element.374), channel_id=1, source_target_pairs={{0,2},{1,3},{2,0},{3,1},{4,6},{5,7},{6,4},{7,5},{8,10},{9,11},{10,... | collective-permute-start | bytes 442376 | tf_op jit(solution)/shard_map/ppermute | solution.py:177
  400.6 38.3 %all-to-all-start.5 = ((bf16[4,72,2432]{2,1,0:T(8,128)(2,1)}), bf16[4,72,2432]{2,1,0:T(8,128)(2,1)}, u32[]{:S(2)}, u32[]{:S(2)}) async-start(bf16[4,72,2432]{2,1,0:T(8,128)(2,1)} %shard_map.187), calls=%async_computation.5 | async-start | bytes 2801664 | tf_op jit(solution)/shard_map/all_to_all | solution.py:195
  406.6 15.1 %collective-permute-start.47 = (bf16[256,1152]{1,0:T(8,128)(2,1)}, bf16[256,1152]{1,0:T(8,128)(2,1)S(1)}, u32[]{:S(2)}, u32[]{:S(2)}) collective-permute-start(bf16[256,1152]{1,0:T(8,128)(2,1)} %get-tuple-element.489), channel_id=1, source_target_pairs={{0,1},{1,0},{2,5},{3,4},{4,3},{5,2},{6,7},{7,6},{8,9},{9,8},{10,13... | collective-permute-start | bytes 1769480 | tf_op jit(solution)/shard_map/ppermute | solution.py:177
  407.4 17.0 %collective-permute-start.46 = (bf16[256,1152]{1,0:T(8,128)(2,1)S(1)}, bf16[256,1152]{1,0:T(8,128)(2,1)}, u32[]{:S(2)}, u32[]{:S(2)}) collective-permute-start(bf16[256,1152]{1,0:T(8,128)(2,1)S(1)} %get-tuple-element.398), channel_id=1, source_target_pairs={{2,4},{3,5},{4,2},{5,3},{10,12},{11,13},{12,10},{13,11},{18,20},{1... | collective-permute-start | bytes 1769480 | tf_op jit(solution)/shard_map/ppermute | solution.py:177
  410.0 25.6 %collective-permute-start.44 = (bf16[72,2176]{1,0:T(8,128)(2,1)S(1)}, bf16[72,2176]{1,0:T(8,128)(2,1)S(1)}, u32[]{:S(2)}, u32[]{:S(2)}) collective-permute-start(bf16[72,2176]{1,0:T(8,128)(2,1)S(1)} %bitcast.109), channel_id=1, source_target_pairs={{0,2},{1,3},{2,0},{3,1},{4,6},{5,7},{6,4},{7,5},{8,10},{9,11},{10,... | collective-permute-start | bytes 940040 | tf_op jit(solution)/shard_map/ppermute | solution.py:177
  414.1 21.4 %collective-permute-start.43 = (bf16[72,2176]{1,0:T(8,128)(2,1)S(1)}, bf16[72,2176]{1,0:T(8,128)(2,1)S(1)}, u32[]{:S(2)}, u32[]{:S(2)}) collective-permute-start(bf16[72,2176]{1,0:T(8,128)(2,1)S(1)} %bitcast.110), channel_id=1, source_target_pairs={{0,1},{1,0},{2,3},{3,2},{4,5},{5,4},{6,7},{7,6},{8,9},{9,8},{10,11... | collective-permute-start | bytes 940040 | tf_op jit(solution)/shard_map/ppermute | solution.py:177
  416.8 22.0 %collective-permute-start.42 = (bf16[72,2176]{1,0:T(8,128)(2,1)S(1)}, bf16[72,2176]{1,0:T(8,128)(2,1)S(1)}, u32[]{:S(2)}, u32[]{:S(2)}) collective-permute-start(bf16[72,2176]{1,0:T(8,128)(2,1)S(1)} %reduce_sum.24.refs_0_), channel_id=1, source_target_pairs={{0,2},{1,3},{2,0},{3,1},{4,6},{5,7},{6,4},{7,5},{8,10},{9,11},{10,... | collective-permute-start | bytes 940040 | tf_op jit(solution)/shard_map/ppermute | solution.py:177
  422.5 16.3 %collective-permute-start.41 = (bf16[72,2176]{1,0:T(8,128)(2,1)S(1)}, bf16[72,2176]{1,0:T(8,128)(2,1)S(1)}, u32[]{:S(2)}, u32[]{:S(2)}) collective-permute-start(bf16[72,2176]{1,0:T(8,128)(2,1)S(1)} %reduce_sum.24.refs_0_), channel_id=1, source_target_pairs={{0,1},{1,0},{2,3},{3,2},{4,5},{5,4},{6,7},{7,6},{8,9},{9,8},{10,11... | collective-permute-start | bytes 940040 | tf_op jit(solution)/shard_map/ppermute | solution.py:177
  424.4 11.0 %collective-permute-start.45 = (f32[18,128]{1,0:T(8,128)S(1)}, f32[18,128]{1,0:T(8,128)S(1)}, u32[]{:S(2)}, u32[]{:S(2)}) collective-permute-start(f32[18,128]{1,0:T(8,128)S(1)} %add.191), channel_id=1, source_target_pairs={{0,1},{1,0},{2,3},{3,2},{4,5},{5,4},{6,7},{7,6},{8,9},{9,8},{10,11... | collective-permute-start | bytes 27656 | tf_op jit(solution)/shard_map/ppermute | solution.py:177
  440.5 20.5 %collective-permute-start.51 = (bf16[72,2432]{1,0:T(8,128)(2,1)S(1)}, bf16[72,2432]{1,0:T(8,128)(2,1)S(1)}, u32[]{:S(2)}, u32[]{:S(2)}) collective-permute-start(bf16[72,2432]{1,0:T(8,128)(2,1)S(1)} %reduce_sum.25.refs_0_), channel_id=1, source_target_pairs={{0,2},{1,3},{2,0},{3,1},{4,6},{5,7},{6,4},{7,5},{8,10},{9,11},{10,... | collective-permute-start | bytes 1050632 | tf_op jit(solution)/shard_map/ppermute | solution.py:177
  441.4 19.6 %collective-permute-start.50 = (bf16[72,2432]{1,0:T(8,128)(2,1)S(1)}, bf16[72,2432]{1,0:T(8,128)(2,1)S(1)}, u32[]{:S(2)}, u32[]{:S(2)}) collective-permute-start(bf16[72,2432]{1,0:T(8,128)(2,1)S(1)} %reduce_sum.25.refs_0_), channel_id=1, source_target_pairs={{0,1},{1,0},{2,3},{3,2},{4,5},{5,4},{6,7},{7,6},{8,9},{9,8},{10,11... | collective-permute-start | bytes 1050632 | tf_op jit(solution)/shard_map/ppermute | solution.py:177
  442.9 7.3 %collective-permute-start.54 = (f32[18,128]{1,0:T(8,128)S(1)}, f32[18,128]{1,0:T(8,128)S(1)}, u32[]{:S(2)}, u32[]{:S(2)}) collective-permute-start(f32[18,128]{1,0:T(8,128)S(1)} %add.192), channel_id=1, source_target_pairs={{0,2},{1,3},{2,0},{3,1},{4,6},{5,7},{6,4},{7,5},{8,10},{9,11},{10,... | collective-permute-start | bytes 27656 | tf_op jit(solution)/shard_map/ppermute | solution.py:177
  444.5 11.1 %collective-permute-start.52 = (bf16[72,1024]{1,0:T(8,128)(2,1)S(1)}, bf16[72,1024]{1,0:T(8,128)(2,1)S(1)}, u32[]{:S(2)}, u32[]{:S(2)}) collective-permute-start(bf16[72,1024]{1,0:T(8,128)(2,1)S(1)} %slice.177), channel_id=1, source_target_pairs={{0,1},{1,0},{2,3},{3,2},{4,5},{5,4},{6,7},{7,6},{8,9},{9,8},{10,11... | collective-permute-start | bytes 442376 | tf_op jit(solution)/shard_map/ppermute | solution.py:177
  445.4 13.5 %collective-permute-start.48 = (bf16[72,1024]{1,0:T(8,128)(2,1)S(1)}, bf16[72,1024]{1,0:T(8,128)(2,1)S(1)}, u32[]{:S(2)}, u32[]{:S(2)}) collective-permute-start(bf16[72,1024]{1,0:T(8,128)(2,1)S(1)} %slice.175), channel_id=1, source_target_pairs={{0,1},{1,0},{2,3},{3,2},{4,5},{5,4},{6,7},{7,6},{8,9},{9,8},{10,11... | collective-permute-start | bytes 442376 | tf_op jit(solution)/shard_map/ppermute | solution.py:177
  450.2 8.8 %collective-permute-start.53 = (bf16[72,1152]{1,0:T(8,128)(2,1)S(1)}, bf16[72,1152]{1,0:T(8,128)(2,1)S(1)}, u32[]{:S(2)}, u32[]{:S(2)}) collective-permute-start(bf16[72,1152]{1,0:T(8,128)(2,1)S(1)} %slice.178), channel_id=1, source_target_pairs={{0,2},{1,3},{2,0},{3,1},{4,6},{5,7},{6,4},{7,5},{8,10},{9,11},{10,... | collective-permute-start | bytes 497672 | tf_op jit(solution)/shard_map/ppermute | solution.py:177
  455.7 5.3 %collective-permute-start.49 = (bf16[72,1152]{1,0:T(8,128)(2,1)S(1)}, bf16[72,1152]{1,0:T(8,128)(2,1)S(1)}, u32[]{:S(2)}, u32[]{:S(2)}) collective-permute-start(bf16[72,1152]{1,0:T(8,128)(2,1)S(1)} %slice.176), channel_id=1, source_target_pairs={{0,2},{1,3},{2,0},{3,1},{4,6},{5,7},{6,4},{7,5},{8,10},{9,11},{10,... | collective-permute-start | bytes 497672 | tf_op jit(solution)/shard_map/ppermute | solution.py:177
  461.7 8.2 %collective-permute-start.58 = (bf16[2,72,2176]{2,1,0:T(8,128)(2,1)S(1)}, bf16[2,72,2176]{2,1,0:T(8,128)(2,1)S(1)}, u32[]{:S(2)}, u32[]{:S(2)}) collective-permute-start(bf16[2,72,2176]{2,1,0:T(8,128)(2,1)S(1)} %shard_map.190), channel_id=1, source_target_pairs={{0,4},{1,5},{2,6},{3,7},{4,0},{5,1},{6,2},{7,3},{8,12},{9,13},{10,... | collective-permute-start | bytes 1880072 | tf_op jit(solution)/shard_map/ppermute | solution.py:177
  462.4 7.4 %collective-permute-start.55 = (bf16[2,72,2176]{2,1,0:T(8,128)(2,1)S(1)}, bf16[2,72,2176]{2,1,0:T(8,128)(2,1)S(1)}, u32[]{:S(2)}, u32[]{:S(2)}) collective-permute-start(bf16[2,72,2176]{2,1,0:T(8,128)(2,1)S(1)} %shard_map.189), channel_id=1, source_target_pairs={{0,4},{1,5},{2,6},{3,7},{4,0},{5,1},{6,2},{7,3},{8,12},{9,13},{10,... | collective-permute-start | bytes 1880072 | tf_op jit(solution)/shard_map/ppermute | solution.py:177
  463.0 6.8 %collective-permute-start.57 = (bf16[72,1280]{1,0:T(8,128)(2,1)S(1)}, bf16[72,1280]{1,0:T(8,128)(2,1)S(1)}, u32[]{:S(2)}, u32[]{:S(2)}) collective-permute-start(bf16[72,1280]{1,0:T(8,128)(2,1)S(1)} %slice.180), channel_id=1, source_target_pairs={{0,2},{1,3},{2,0},{3,1},{4,6},{5,7},{6,4},{7,5},{8,10},{9,11},{10,... | collective-permute-start | bytes 552968 | tf_op jit(solution)/shard_map/ppermute | solution.py:177
  463.9 6.0 %collective-permute-start.56 = (bf16[72,1152]{1,0:T(8,128)(2,1)S(1)}, bf16[72,1152]{1,0:T(8,128)(2,1)S(1)}, u32[]{:S(2)}, u32[]{:S(2)}) collective-permute-start(bf16[72,1152]{1,0:T(8,128)(2,1)S(1)} %slice.179), channel_id=1, source_target_pairs={{0,1},{1,0},{2,3},{3,2},{4,5},{5,4},{6,7},{7,6},{8,9},{9,8},{10,11... | collective-permute-start | bytes 497672 | tf_op jit(solution)/shard_map/ppermute | solution.py:177
  472.9 9.2 %collective-permute-start.60 = (bf16[2,72,2432]{2,1,0:T(8,128)(2,1)}, bf16[2,72,2432]{2,1,0:T(8,128)(2,1)}, u32[]{:S(2)}, u32[]{:S(2)}) collective-permute-start(bf16[2,72,2432]{2,1,0:T(8,128)(2,1)} %shard_map.191), channel_id=1, source_target_pairs={{0,4},{1,5},{2,6},{3,7},{4,0},{5,1},{6,2},{7,3},{8,12},{9,13},{10,... | collective-permute-start | bytes 2101256 | tf_op jit(solution)/shard_map/ppermute | solution.py:177
  472.9 9.2 %collective-permute-start.61 = (f32[18,128]{1,0:T(8,128)S(1)}, f32[18,128]{1,0:T(8,128)S(1)}, u32[]{:S(2)}, u32[]{:S(2)}) collective-permute-start(f32[18,128]{1,0:T(8,128)S(1)} %add.194), channel_id=1, source_target_pairs={{0,16},{1,17},{2,18},{3,19},{4,20},{5,21},{6,22},{7,23},{8,24},{9,... | collective-permute-start | bytes 27656 | tf_op jit(solution)/shard_map/ppermute | solution.py:177
  (95 other events, 705.8 us)
where the time goes:
time: 498 us; the launch traced here: 488 us
  Pallas kernels  138 us (28%)
  waiting for transfers between devices  104 us (21%)
  starting transfers between devices  92.2 us (19%)
  local copies, waits for them, and re-layouts  71.5 us (14%)
  matrix products  50.9 us (10%)
  other arithmetic  29.6 us (6%)
    ppermute x62, waiting for transfers between devices, send(): return lax.ppermute(value, ('fsdp', 'seq'), pairs)  97.2 us
    ppermute x62, starting transfers between devices, send(): return lax.ppermute(value, ('fsdp', 'seq'), pairs)  61.5 us
    unnamed x185, local copies, waits for them, and re-layouts  37.6 us
    all_to_all x6, starting transfers between devices, over_z(): lax.all_to_all(value, 'fsdp', 0, 0, axis_index_groups=self.z_lines, tiled...  30.7 us
    pallas_call x1, Pallas kernels, attention_backward(): pl.pallas_call(functools.partial(attention_backward_kernel, block, heads)...  26.3 us
    dot_general x4, matrix products, dot_t(): lax.dot_general(a, b, (((1,), (1,)), ((), ())), preferred_element_type=F32)  25.2 us
    pallas_call x2, Pallas kernels, weight_grad(): pl.pallas_call(functools.partial(weight_grad_kernel, cut, group, rows, le...  24.3 us
    pallas_call x1, Pallas kernels, attention_forward(): pl.pallas_call(functools.partial(attention_forward_kernel, block, heads),...  19.5 us
  transfers between devices with their start and end apart: 68, of which 28 were waited for; matrix products, arithmetic and copies ran while one was open for 19% of the time, Pallas kernels for 26%

commit v1 on v0

--- a/solution.py
+++ b/solution.py
@@ -279,6 +279,34 @@
     return pieces
 
 
+def halve_kernel(where, weights, extra, give, keep):
+    half = weights.shape[1] // 6
+    for core in range(2):
+
+        @pl.when(where[0] == core)
+        def _():
+            for i in range(3):
+                at = slice(i * half, (i + 1) * half)
+                for out, side in ((keep, core), (give, 1 - core)):
+                    start = (2 * i + side) * half
+                    out[:, at] = weights[:, start : start + half]
+
+    for out in (give, keep):
+        out[:, 3 * half :] = extra[...]
+
+
+def halve(place, weights, extra):
+    rows = weights.shape[0]
+    shape = jax.ShapeDtypeStruct((rows, weights.shape[1] // 2 + extra.shape[1]), BF16)
+    return pl.pallas_call(
+        halve_kernel,
+        in_specs=[scalar_spec()] + [whole_spec()] * 2,
+        out_specs=[whole_spec()] * 2,
+        out_shape=[shape, shape],
+        compiler_params=vmem(16),
+    )(place.spot, weights, extra)
+
+
 def assemble_kernel(planes, start, size, where, block, own, x_part, y_part, *refs):
     *far, out, sems = refs
     z, k = where[1], where[4]
@@ -355,7 +383,9 @@
             total[:, at + start : at + end] = jnp.dot(left, right[:, start:end], preferred_element_type=F32)
         at += columns
     if with_riders:
-        total[:, at:] = riders[...]
+        rows_of = riders[...]
+        rest = jnp.zeros((total.shape[1] - at - rows_of.shape[0], rows_of.shape[1]), F32)
+        total[:, at:] = jnp.concatenate([rows_of, rest], axis=0).T
     for plane in range(group):
         for dy in range(2):
             for dx in range(2):
@@ -370,7 +400,7 @@
     tokens, width = pairs[0][0].shape
     rows = width // planes // 4
     group = planes
-    columns = sum(right.shape[1] for _, right in pairs) + (0 if riders is None else riders.shape[1])
+    columns = sum(right.shape[1] for _, right in pairs) + (0 if riders is None else LANES)
     rider_list = [] if riders is None else [riders]
     cut = lane_cut(columns)
     still = lambda shape: pl.BlockSpec(shape, lambda i: (0, 0), pipeline_mode=pl.Buffered(1))
@@ -385,7 +415,7 @@
         in_specs=[scalar_spec()]
         + [still(left.shape) for left, _ in pairs]
         + [still(right.shape) for _, right in pairs]
-        + [pl.BlockSpec((group * 4 * rows, extra.shape[1]), lambda i: (i, 0)) for extra in rider_list],
+        + [pl.BlockSpec((extra.shape[0], group * 4 * rows), lambda i: (0, i)) for extra in rider_list],
         out_specs=[low_spec, low_spec, high_spec, high_spec] + [pl.BlockSpec(s.shape, lambda i: (0, 0)) for s in sum_shapes],
         out_shape=[low, low, high, high] + sum_shapes,
         scratch_shapes=[pltpu.VMEM((group * 4 * rows, columns), F32)] + [pltpu.VMEM((width, tokens), BF16) for _ in pairs],
@@ -720,7 +750,9 @@
     return value
 
 
-def norm_back_kernel(half, where, part, arrived, upstream, normed, inv_std, gain, low, own_columns, own_rows, sums):
+def norm_back_kernel(
+    half, where, part, arrived, upstream, normed, inv_std, gain, weights, own_columns, d_attended, own_rows, sums
+):
     step = pl.program_id(0)
     e = part[...].astype(F32) + arrived[...].astype(F32)
     n = normed[...].astype(F32)
@@ -730,7 +762,10 @@
     cot = upstream[...].astype(F32)
     d = cot + inv_std[...] * (scaled - first_mean - n * second_mean)
     d_low = d.astype(BF16)
-    low[...] = d_low
+    rows_here = weights[pl.ds(pl.multiple_of(where[0] * half, 16), half), :]
+    d_attended[...] = lax.dot_general(
+        d_low, rows_here, (((1,), (1,)), ((), ())), preferred_element_type=F32
+    ).astype(BF16)
     for core in range(2):
 
         @pl.when(where[0] == core)
@@ -752,14 +787,14 @@
         sums[...] += rows
 
 
-def norm_back_second(place, part, arrived, upstream, normed, inv_std, gain):
+def norm_back_second(place, part, arrived, upstream, normed, inv_std, gain, weights):
     tokens, width = part.shape
-    size = tokens // 8
+    size = tokens // 4
     by_row = pl.BlockSpec((size, width), lambda i: (i, 0))
-    turned = pl.BlockSpec((size, width), lambda i: ((i + 4) % 8, 0))
+    turned = pl.BlockSpec((size, width), lambda i: ((i + 2) % 4, 0))
     return pl.pallas_call(
         functools.partial(norm_back_kernel, width // 2),
-        grid=(8,),
+        grid=(4,),
         in_specs=[
             scalar_spec(),
             by_row,
@@ -768,21 +803,58 @@
             by_row,
             pl.BlockSpec((size, 1), lambda i: (i, 0)),
             pl.BlockSpec((1, width), lambda i: (0, 0)),
+            pl.BlockSpec((width, width), lambda i: (0, 0), pipeline_mode=pl.Buffered(1)),
         ],
         out_specs=[
-            by_row,
             pl.BlockSpec((size, width // 2), lambda i: (i, 0)),
-            pl.BlockSpec((size, width), lambda i: (jnp.minimum(i, 3), 0)),
+            pl.BlockSpec((size, width // 2), lambda i: (i, 0)),
+            pl.BlockSpec((size, width), lambda i: (jnp.minimum(i, 1), 0)),
             pl.BlockSpec((8, width), lambda i: (0, 0)),
         ],
         out_shape=[
-            jax.ShapeDtypeStruct((tokens, width), BF16),
+            jax.ShapeDtypeStruct((tokens, width // 2), BF16),
             jax.ShapeDtypeStruct((tokens, width // 2), BF16),
             jax.ShapeDtypeStruct((tokens // 2, width), F32),
             jax.ShapeDtypeStruct((8, width), F32),
         ],
-        compiler_params=vmem(24),
-    )(place.spot, part, arrived, upstream, normed, inv_std, gain)
+        compiler_params=vmem(58),
+    )(place.spot, part, arrived, upstream, normed, inv_std, gain, weights)
+
+
+def rider_rows_kernel(hidden, up_shard, up_cols, where, pack, by_width, by_hidden, out):
+    width = out.shape[1]
+    half, half_hidden = width // 2, by_hidden.shape[1]
+    shard = width // (hidden // up_shard)
+    out[...] = jnp.zeros_like(out)
+    for core in range(2):
+
+        @pl.when(where[0] == core)
+        def _():
+            here = slice(core * half, (core + 1) * half)
+            out[0:1, here] = pack[0:1, :half]
+            out[1:2, here] = pack[0:1, 2 * half :]
+            if core == 0:
+                out[2:6, :] = by_width[:4, :]
+            for owner in range(hidden // up_shard):
+                for row in range(up_cols):
+                    start = owner * up_shard + row * shard
+                    first = max(start, core * half_hidden)
+                    last = min(start + shard, (owner + 1) * up_shard, (core + 1) * half_hidden, hidden)
+                    if first < last:
+                        at = owner * shard + first - start
+                        out[6 + row : 7 + row, at : at + last - first] = by_hidden[
+                            0:1, first - core * half_hidden : last - core * half_hidden
+                        ]
+
+
+def rider_rows(place, pack, by_width, by_hidden, hidden, up_shard, up_cols):
+    return pl.pallas_call(
+        functools.partial(rider_rows_kernel, hidden, up_shard, up_cols),
+        in_specs=[scalar_spec()] + [whole_spec()] * 3,
+        out_specs=whole_spec(),
+        out_shape=jax.ShapeDtypeStruct((-(-(6 + up_cols) // 8) * 8, by_width.shape[1]), F32),
+        compiler_params=vmem(16),
+    )(place.spot, pack, by_width, by_hidden)
 
 
 def norm_back_first_kernel(part, arrived, d_resid, normed, inv_std, gain, grad, sums):
@@ -872,9 +944,6 @@
     up_shard = up_bias.shape[0]
     up_cols = -(-up_shard // shard)
 
-    def halves_qkv(w):
-        return jnp.moveaxis(w.reshape(w.shape[0], 3, 2, half_width), 2, 0).reshape(2, w.shape[0], 3 * half_width)
-
     def halves_hidden(w):
         padded = jnp.pad(w, ((0, 0), (0, 2 * half_hidden - hidden)))
         return jnp.stack([padded[:, :half_hidden], padded[:, half_hidden:]])
@@ -891,9 +960,7 @@
     extra = jnp.pad(small.T, ((0, 0), (0, spare - n_small)))
     c = place.c
 
-    qkv_halves = halves_qkv(w_qkv)
-    give = jnp.concatenate([pick(qkv_halves, 1 - c), extra], axis=1)
-    keep = jnp.concatenate([pick(qkv_halves, c), extra], axis=1)
+    give, keep = halve(place, w_qkv, extra)
     qkv = Transfer(spread(place, give, keep))
     tokens_in = Transfer(to_image(place, pick(inputs, place.x), pick(inputs, 1 - place.x)))
     w_out, w_up, w_down, cotangent = close_round(qkv, hold=(w_out, w_up, w_down, cotangent))
@@ -964,30 +1031,14 @@
 
     up_grad = Transfer(collect(place, dw_up))
     layer_out = Transfer(from_image(place, layer_half))
-    d_resid_low, d_resid_columns, d_resid_half, by_width = norm_back_second(
-        place, d_second_part, d_second_other, upstream, second_normed, second_inv, gain_rows[1:]
-    )
-    d_attended = dot_t(d_resid_low, lax.dynamic_slice_in_dim(full_out, c * half_width, half_width)).astype(BF16)
+    d_resid_columns, d_attended, d_resid_half, by_width = norm_back_second(
+        place, d_second_part, d_second_other, upstream, second_normed, second_inv, gain_rows[1:], full_out
+    )
     d_packed = attention_backward(packed, d_attended, attended_half, raised, inv_total)
     (d_packed,) = close_round(up_grad, layer_out, hold=(d_packed,))
 
-    def own_part(row):
-        size = row.shape[0]
-        return jnp.where(c == 0, jnp.pad(row, (0, size)), jnp.pad(row, (size, 0)))
-
-    by_hidden = own_part(d_upper_sums[0])[:hidden].reshape(fsdp, up_shard)
-    by_hidden = jnp.pad(by_hidden, ((0, 0), (0, up_cols * shard - up_shard))).reshape(fsdp, up_cols, shard)
-    by_hidden = by_hidden.transpose(1, 0, 2).reshape(up_cols, width)
-    pack_sum = dot(jnp.ones((8, d_packed.shape[0]), BF16), d_packed)[0]
-    riders = jnp.concatenate(
-        [
-            own_part(pack_sum[:half_width])[None],
-            own_part(pack_sum[2 * half_width :])[None],
-            jnp.where(c == 0, by_width[:4], 0.0),
-            by_hidden,
-        ]
-    )
-    riders = jnp.pad(riders, ((0, LANES - riders.shape[0]), (0, 0))).T
+    pack_sum = dot(jnp.ones((8, d_packed.shape[0]), BF16), d_packed)
+    riders = rider_rows(place, pack_sum, by_width, d_upper_sums, hidden, up_shard, up_cols)
     dw_last = weight_grad(place, [(first_low, d_packed), (attended, d_resid_columns)], riders)
     *dw_last, d_packed = close_round(up_grad, down_grad, hold=(*dw_last, d_packed))
 
@@ -1002,7 +1053,7 @@
         gain_rows[:1],
     )
     late = Transfer(sum_devices(place, first_sums[:2].reshape(-1, LANES)))
-    (grad_half,) = close_round(last_grad, down_grad, hold=(grad_half,))
+    (grad_half,) = close_round(last_grad, down_grad, late, hold=(grad_half,))
 
     def write_hidden(lower, higher, out):
         out[:, :half_hidden] = lower[:, :half_hidden]
@@ -1027,7 +1078,7 @@
     close_round(up_grad, last_grad, down_grad, late)
     (grad_up,) = finish(place, up_grad.result, write_hidden, [(shard, hidden)])
     (grad_down,) = finish(place, down_grad.result, write_hidden, [(shard, hidden)])
-    grad_up, grad_down = close_round(last_grad, late, hold=(grad_up, grad_down))
+    grad_up, grad_down = close_round(last_grad, hold=(grad_up, grad_down))
     grad_qkv, grad_proj, rest_sums = finish(
         place, last_grad.result, write_last, [(shard, 3 * width), (shard, width), (shard, LANES)]
     )

time: 498 us -> 491 us (0.986)
  other arithmetic: 29.6 us -> 23.9 us
    ppermute x62, waiting for transfers between devices: 97.2 us -> 90.5 us  [send(): return lax.ppermute(value, ('fsdp', 'seq'), pairs)]
    ppermute x62, starting transfers between devices: 61.5 us -> 67.6 us  [send(): return lax.ppermute(value, ('fsdp', 'seq'), pairs)]
    unnamed x185 -> x212, local copies, waits for them, and re-layouts: 37.6 us -> 43.7 us
    pallas_call x1 -> x3, Pallas kernels: 7.83 us -> 13.2 us  [the longest x1 11.4 us: norm_back_second(): pl.pallas_call(functools.partial(norm_back_kernel, width // 2), grid=(4,)...]
    dot_general x4 -> x3, matrix products: 25.2 us -> 22.8 us  [dot_t(): lax.dot_general(a, b, (((1,), (1,)), ((), ())), preferred_element_type=F32)]
  transfers between devices with their start and end apart: 68 -> 68, of which waited for: 28 -> 25; matrix products, arithmetic and copies ran while one was open for 19% -> 17% of each run, Pallas kernels for 26% -> 26%
where the time goes in v1:
time: 491 us; the launch traced here: 482 us
  Pallas kernels  137 us (28%)
  waiting for transfers between devices  101 us (21%)
  starting transfers between devices  96.8 us (20%)
  local copies, waits for them, and re-layouts  69.9 us (14%)
  matrix products  50.4 us (10%)
  other arithmetic  23.9 us (5%)
    ppermute x62, waiting for transfers between devices, send(): return lax.ppermute(value, ('fsdp', 'seq'), pairs)  90.5 us
    ppermute x62, starting transfers between devices, send(): return lax.ppermute(value, ('fsdp', 'seq'), pairs)  67.6 us
    unnamed x212, local copies, waits for them, and re-layouts  43.7 us
    all_to_all x6, starting transfers between devices, over_z(): lax.all_to_all(value, 'fsdp', 0, 0, axis_index_groups=self.z_lines, tiled...  29.2 us
    pallas_call x1, Pallas kernels, attention_backward(): pl.pallas_call(functools.partial(attention_backward_kernel, block, heads)...  26.3 us
    pallas_call x2, Pallas kernels, weight_grad(): pl.pallas_call(functools.partial(weight_grad_kernel, cut, group, rows, le...  24.3 us
    dot_general x3, matrix products, dot_t(): lax.dot_general(a, b, (((1,), (1,)), ((), ())), preferred_element_type=F32)  22.8 us
    dot_general x3, matrix products, dot(): return jnp.dot(a, b, preferred_element_type=F32)  20 us
  transfers between devices with their start and end apart: 68, of which 25 were waited for; matrix products, arithmetic and copies ran while one was open for 17% of the time, Pallas kernels for 26%

profile of v1, /device:TPU:0, one launch (start us, length us, event | category | flops | bytes accessed | tf_op | source)
XLA Modules:
  0.0 482.0 jit_solution(12679856906455628762)
XLA Ops:
  10.3 6.2 %all-to-all-start = ((bf16[4,72,1792]{2,1,0:T(8,128)(2,1)}), bf16[4,72,1792]{2,1,0:T(8,128)(2,1)S(1)}, u32[]{:S(2)}, u32[]{:S(2)}) async-start(bf16[4,72,1792]{2,1,0:T(8,128)(2,1)} %broadcast_in_dim.50), calls=%async_computation | async-start | bytes 2064384 | tf_op jit(solution)/shard_map/all_to_all | solution.py:195
  22.5 2.4 dynamic-slice_bitcast_fusion.2
  24.9 1.8 maximum_select_fusion
  26.8 8.8 %collective-permute-done.2 = bf16[256,1152]{1,0:T(8,128)(2,1)} collective-permute-done((bf16[256,1152]{1,0:T(8,128)(2,1)}, bf16[256,1152]{1,0:T(8,128)(2,1)}, u32[]{:S(2)}, u32[]{:S(2)}) %collective-permute-start.2) | collective-permute-done | bytes 589856 | tf_op jit(solution)/shard_map/ppermute | solution.py:177
  35.6 6.5 %all-to-all-done = bf16[4,72,1792]{2,1,0:T(8,128)(2,1)S(1)} async-done(((bf16[4,72,1792]{2,1,0:T(8,128)(2,1)}), bf16[4,72,1792]{2,1,0:T(8,128)(2,1)S(1)}, u32[]{:S(2)}, u32[]{:S(2)}) %all-to-all-start) | async-done | bytes 1032224 | tf_op jit(solution)/shard_map/all_to_all | solution.py:195
  47.5 4.3 all-to-all-start.1
  58.6 4.4 collective-permute-done.5.y_part
  64.6 1.9 collective-permute-done.4.x_part
  66.5 1.8 slice.125
  68.3 1.8 slice.124
  73.0 6.1 %collective-permute-done.11 = bf16[256,1152]{1,0:T(8,128)(2,1)} collective-permute-done((bf16[256,1152]{1,0:T(8,128)(2,1)}, bf16[256,1152]{1,0:T(8,128)(2,1)}, u32[]{:S(2)}, u32[]{:S(2)}) %collective-permute-start.11) | collective-permute-done | bytes 589856 | tf_op jit(solution)/shard_map/ppermute | solution.py:177
  79.1 6.0 %collective-permute-done.7.refs_0_ = bf16[3,72,896]{2,1,0:T(8,128)(2,1)S(1)} collective-permute-done((bf16[3,72,896]{2,1,0:T(8,128)(2,1)}, bf16[3,72,896]{2,1,0:T(8,128)(2,1)S(1)}, u32[]{:S(2)}, u32[]{:S(2)}) %collective-permute-start.7) | collective-permute-done | bytes 387104 | tf_op jit(solution)/shard_map/ppermute | solution.py:177
  85.1 3.6 collective-permute-done.8.refs_1_
  94.5 2.8 shard_map.170
  99.4 8.1 %shard_map.172 = (bf16[1024,1152]{1,0:T(8,128)(2,1)S(1)}, bf16[1024,1152]{1,0:T(8,128)(2,1)S(1)}, f32[1024,1]{1,0:T(8,128)S(1)}, bf16[1024,1152]{1,0:T(8,128)(2,1)S(1)}, bf16[1024,1728]{1,0:T(8,128)(2,1)S(1)}) custom-call(bf16[512,1152]{1,0:T(8,128)(2,1)S(1)} %copy-done.21, bf16[512,1152]{1,0:T(8,128)(2,1)} %collective-permute-done.6.other, ...), custom_call_target="tpu_custom_call" | custom-call | flops 589824 | bytes 589824 | tf_op jit(solution)/shard_map/pallas_call | solution.py:650
  107.6 1.8 copy-done.1
  112.2 2.5 maximum_select_fusion.1
  115.9 2.3 collective-permute-done.14.y_part
  121.4 4.5 all-to-all-start.2
  127.3 2.0 copy-done.2
  129.3 19.5 %shard_map.173 = (bf16[1024,640]{1,0:T(8,128)(2,1)S(1)}, bf16[8,1024,1024]{2,1,0:T(8,128)(2,1)}, f32[8,1,1024]{2,1,0:T(1,128)S(1)}) custom-call(bf16[1024,1728]{1,0:T(8,128)(2,1)S(1)} %copy-done.2, f32[1024,1]{1,0:T(8,128)S(1)} %broadcast_select_fusion.2.bias_ref), custom_call_target="tpu_custom_call" | custom-call | flops 8388608 | bytes 1769472 | tf_op jit(solution)/shard_map/pallas_call | solution.py:61
  150.5 3.2 collective-permute-done.16.refs_0_
  158.5 2.0 shard_map.174
  163.4 1.9 collective-permute-start.18
  171.6 2.4 copy-done.24
  174.1 9.2 %shard_map.175 = (bf16[1024,1152]{1,0:T(8,128)(2,1)S(1)}, bf16[1152,1152]{1,0:T(8,128)(2,1)S(1)}, f32[512,1152]{1,0:T(8,128)S(1)}, bf16[1024,1152]{1,0:T(8,128)(...) custom-call(s32[5]{0:T(128)S(1)} %stack.66.where, bf16[1024,1152]{1,0:T(8,128)(2,1)S(1)} %copy-done.24, ...), custom_call_target="tpu_custom_call" | custom-call | flops 1179648 | bytes 1179648 | tf_op jit(solution)/shard_map/pallas_call | solution.py:708
  183.3 3.4 collective-permute-done.18.y_part
  191.5 11.0 %add_convert_fusion = (bf16[1024,2176]{1,0:T(8,128)(2,1)}, bf16[1024,2176]{1,0:T(8,128)(2,1)S(1)}) fusion(f32[2176]{0:T(1024)S(1)} %dynamic-slice_reduce_fusion, bf16[1024,1152]{1,0:T(8,128)(2,1)S(1)} %get-tuple-element.296.refs_0_, bf16[1152,2176]{1,0:T(8,128)(2,1)S(1)} %bitcast.93), kind=kOutput, calls=%fused_computation.2 | convolution fusion | flops 5178392576 | bytes 16294400 | tf_op jit(solution)/shard_map/dot_general | solution.py:925
  203.1 7.6 %convolution_convert_fusion = bf16[1152,2176]{1,0:T(8,128)(2,1)} fusion(bf16[1024,1152]{1,0:T(8,128)(2,1)S(1)} %constant_dynamic-update-slice_fusion.upstream, bf16[1024,2176]{1,0:T(8,128)(2,1)S(1)} %get-tuple-element.315), kind=kOutput, calls=%fused_computation | convolution fusion | flops 5136334848 | bytes 11829248 | tf_op jit(solution)/shard_map/dot_general | solution.py:933
  210.8 5.1 %all-to-all-start.3 = ((bf16[4,288,2176]{2,1,0:T(8,128)(2,1)}), bf16[4,288,2176]{2,1,0:T(8,128)(2,1)}, u32[]{:S(2)}, u32[]{:S(2)}) async-start(bf16[4,288,2176]{2,1,0:T(8,128)(2,1)} %bitcast.101), calls=%async_computation.3 | async-start | bytes 10027008 | tf_op jit(solution)/shard_map/all_to_all | solution.py:195
  216.0 3.2 shard_map.177
  219.2 8.4 %multiply_convert_fusion.refs_1_ = bf16[1024,2176]{1,0:T(8,128)(2,1)S(1)} fusion(bf16[1024,2176]{1,0:T(8,128)(2,1)} %get-tuple-element.309, bf16[1024,1152]{1,0:T(8,128)(2,1)S(1)} %copy-done.85, bf16[1152,2176]{1,0:T(8,128)(2,1)S(1)} %bitcast.91), kind=kOutput, calls=%fused_computation.1 | convolution fusion | flops 5140512768 | bytes 16285696 | tf_op jit(solution)/shard_map/dot_general | solution.py:925
  227.6 7.5 %convolution_convert_fusion.2.part = bf16[1024,1152]{1,0:T(8,128)(2,1)} fusion(bf16[1024,2176]{1,0:T(8,128)(2,1)S(1)} %multiply_convert_fusion.refs_1_, bf16[1152,2176]{1,0:T(8,128)(2,1)S(1)} %bitcast.96), kind=kOutput, calls=%fused_computation.9 | convolution fusion | flops 5135007744 | bytes 11829248 | tf_op jit(solution)/shard_map/dot_general | solution.py:929
  235.2 7.0 %convolution_convert_fusion.1 = bf16[1024,1152]{1,0:T(8,128)(2,1)S(1)} fusion(bf16[1024,2176]{1,0:T(8,128)(2,1)S(1)} %bitcast.110, bf16[1152,2176]{1,0:T(8,128)(2,1)S(1)} %bitcast.92), kind=kOutput, calls=%fused_computation.8 | convolution fusion | flops 5135007744 | bytes 11829248 | tf_op jit(solution)/shard_map/dot_general | solution.py:929
  243.4 11.3 %shard_map.178 = (bf16[2,4,72,1024]{3,2,1,0:T(8,128)(2,1)}, bf16[2,4,72,1024]{3,2,1,0:T(8,128)(2,1)}, bf16[2,4,72,1152]{3,2,1,0:T(8,128)(2,1)}, bf16[2,4,72,1152]{3,2,1,0:T(8,128)(2,1)}, f32[8,2176]{1,0:T(8,128)}) custom-call(s32[5]{0:T(128)} %copy-done.71, bf16[1024,1152]{1,0:T(8,128)(2,1)} %copy-done.27, bf16[1024,2176]{1,0:T(8,128)(2,1)} %copy-done.87), custom_call_target="tpu_custom_call" | custom-call | flops 1179648 | bytes 2506752 | tf_op jit(solution)/shard_map/pallas_call | solution.py:412
  260.7 11.4 %shard_map.179 = (bf16[1024,576]{1,0:T(8,128)(2,1)}, bf16[1024,576]{1,0:T(8,128)(2,1)}, f32[512,1152]{1,0:T(8,128)}, f32[8,1152]{1,0:T(8,128)}) custom-call(s32[5]{0:T(128)} %copy-done.71, bf16[1024,1152]{1,0:T(8,128)(2,1)} %convolution_convert_fusion.2.part, bf16[1024,1152]{1,0:T(8,128)(2,1)} %collective-permute-done.23.arrived, ...), custom_call_target="tpu_custom_call" | custom-call | tf_op jit(solution)/shard_map/pallas_call | solution.py:795
  272.1 26.3 %shard_map.180.refs_2_ = bf16[1024,1728]{1,0:T(8,128)(2,1)} custom-call(bf16[1024,1728]{1,0:T(8,128)(2,1)} %copy-done.1, bf16[1024,576]{1,0:T(8,128)(2,1)} %get-tuple-element.325.d_out_ref, bf16[1024,640]{1,0:T(8,128)(2,1)} %copy-done.5, bf16[8,1024,1024]{2,1,0:T(8,128)(2,1)} %get-tuple-element.326.probs_ref, f32[8,1,1024]{2,1,0:T(1,128)} %copy-done.82), custom_call_target="tpu_custom_call" | custom-call | flops 8388608 | bytes 1769472 | tf_op jit(solution)/shard_map/pallas_call | solution.py:132
  302.0 2.4 collective-permute-start.29
  306.4 13.1 %shard_map.183 = (bf16[2,4,72,1152]{3,2,1,0:T(8,128)(2,1)}, bf16[2,4,72,1152]{3,2,1,0:T(8,128)(2,1)}, bf16[2,4,72,1280]{3,2,1,0:T(8,128)(2,1)}, bf16[2,4,72,1280]{3,2,1,0:T(8,128)(2,1)}) custom-call(s32[5]{0:T(128)} %copy-done.71, bf16[1024,1152]{1,0:T(8,128)(2,1)} %copy-done.30, bf16[1024,1152]{1,0:T(8,128)(2,1)} %copy-done.31, ...), custom_call_target="tpu_custom_call" | custom-call | flops 1179648 | bytes 2801664 | tf_op jit(solution)/shard_map/pallas_call | solution.py:412
  321.2 4.1 all-to-all-done.3.arrived
  327.9 8.3 %fusion.2.part = bf16[1024,1152]{1,0:T(8,128)(2,1)S(1)} fusion(bf16[1024,1728]{1,0:T(8,128)(2,1)} %shard_map.180.refs_2_, bf16[1152,1792]{1,0:T(8,128)(2,1)} %bitcast.83), kind=kOutput, calls=%fused_computation.10 | convolution fusion | flops 4078043136 | bytes 10027008 | tf_op jit(solution)/shard_map/dot_general | solution.py:929
  339.4 4.5 all-to-all-start.4
  344.0 4.6 shard_map.185
  354.8 1.7 shard_map.186
  356.7 5.3 %collective-permute-done.33.from_x = bf16[2,1,72,1024]{3,2,1,0:T(8,128)(2,1)} collective-permute-done((bf16[2,1,72,1024]{3,2,1,0:T(8,128)(2,1)}, bf16[2,1,72,1024]{3,2,1,0:T(8,128)(2,1)}, u32[]{:S(2)}, u32[]{:S(2)}) %collective-permute-start.33) | collective-permute-done | bytes 294944 | tf_op jit(solution)/shard_map/ppermute | solution.py:177
  362.0 4.8 %collective-permute-done.34.from_y = bf16[2,1,72,1152]{3,2,1,0:T(8,128)(2,1)} collective-permute-done((bf16[2,1,72,1152]{3,2,1,0:T(8,128)(2,1)}, bf16[2,1,72,1152]{3,2,1,0:T(8,128)(2,1)}, u32[]{:S(2)}, u32[]{:S(2)}) %collective-permute-start.34) | collective-permute-done | bytes 331808 | tf_op jit(solution)/shard_map/ppermute | solution.py:177
  369.5 4.0 shard_map.187
  380.4 13.5 %collective-permute-done.41 = f32[18,128]{1,0:T(8,128)S(1)} collective-permute-done((f32[18,128]{1,0:T(8,128)S(1)}, f32[18,128]{1,0:T(8,128)S(1)}, u32[]{:S(2)}, u32[]{:S(2)}) %collective-permute-start.41) | collective-permute-done | bytes 9248 | tf_op jit(solution)/shard_map/ppermute | solution.py:177
  395.2 3.5 shard_map.189
  398.7 4.5 all-to-all-start.5
  406.6 3.1 collective-permute-start.45
  412.5 7.8 %collective-permute-done.48 = bf16[256,1152]{1,0:T(8,128)(2,1)} collective-permute-done((bf16[256,1152]{1,0:T(8,128)(2,1)}, bf16[256,1152]{1,0:T(8,128)(2,1)}, u32[]{:S(2)}, u32[]{:S(2)}) %collective-permute-start.48) | collective-permute-done | bytes 589856 | tf_op jit(solution)/shard_map/ppermute | solution.py:177
  421.2 6.7 %collective-permute-start.46 = (f32[18,128]{1,0:T(8,128)S(1)}, f32[18,128]{1,0:T(8,128)S(1)}, u32[]{:S(2)}, u32[]{:S(2)}) collective-permute-start(f32[18,128]{1,0:T(8,128)S(1)} %add.169), channel_id=1, source_target_pairs={{0,2},{1,3},{2,0},{3,1},{4,6},{5,7},{6,4},{7,5},{8,10},{9,11},{10,... | collective-permute-start | bytes 27656 | tf_op jit(solution)/shard_map/ppermute | solution.py:177
  428.8 6.6 %collective-permute-done.46 = f32[18,128]{1,0:T(8,128)S(1)} collective-permute-done((f32[18,128]{1,0:T(8,128)S(1)}, f32[18,128]{1,0:T(8,128)S(1)}, u32[]{:S(2)}, u32[]{:S(2)}) %collective-permute-start.46) | collective-permute-done | bytes 9248 | tf_op jit(solution)/shard_map/ppermute | solution.py:177
  435.5 1.6 reduce_sum.25.refs_0_
  439.1 2.0 collective-permute-start.55
  443.3 3.1 collective-permute-start.54
  446.4 5.0 %collective-permute-done.53.refs_3_ = bf16[72,1024]{1,0:T(8,128)(2,1)S(1)} collective-permute-done((bf16[72,1024]{1,0:T(8,128)(2,1)S(1)}, bf16[72,1024]{1,0:T(8,128)(2,1)S(1)}, u32[]{:S(2)}, u32[]{:S(2)}) %collective-permute-start.53) | collective-permute-done | bytes 147488 | tf_op jit(solution)/shard_map/ppermute | solution.py:177
  452.9 3.4 maximum_select_fusion.2
  461.4 2.9 collective-permute-start.60
  464.3 1.7 collective-permute-done.60
  471.4 2.3 shard_map.194
  473.6 2.3 shard_map.195
  476.0 3.0 shard_map.196
  (411 shorter events, 133.4 us)
Async XLA Ops:
  10.3 31.9 %all-to-all-start = ((bf16[4,72,1792]{2,1,0:T(8,128)(2,1)}), bf16[4,72,1792]{2,1,0:T(8,128)(2,1)S(1)}, u32[]{:S(2)}, u32[]{:S(2)}) async-start(bf16[4,72,1792]{2,1,0:T(8,128)(2,1)} %broadcast_in_dim.50), calls=%async_computation | async-start | bytes 2064384 | tf_op jit(solution)/shard_map/all_to_all | solution.py:195
  17.7 7.2 %collective-permute-start.3 = (bf16[144,2816]{1,0:T(8,128)(2,1)}, bf16[144,2816]{1,0:T(8,128)(2,1)}, u32[]{:S(2)}, u32[]{:S(2)}) collective-permute-start(bf16[144,2816]{1,0:T(8,128)(2,1)} %get-tuple-element.480), channel_id=1, source_target_pairs={{0,4},{1,5},{2,6},{3,7},{4,0},{5,1},{6,2},{7,3},{8,12},{9,13},{10,... | collective-permute-start | bytes 2433032 | tf_op jit(solution)/shard_map/ppermute | solution.py:177
  19.4 16.2 %collective-permute-start.2 = (bf16[256,1152]{1,0:T(8,128)(2,1)}, bf16[256,1152]{1,0:T(8,128)(2,1)}, u32[]{:S(2)}, u32[]{:S(2)}) collective-permute-start(bf16[256,1152]{1,0:T(8,128)(2,1)} %get-tuple-element.497), channel_id=1, source_target_pairs={{0,1},{1,0},{2,5},{3,4},{4,3},{5,2},{6,7},{7,6},{8,9},{9,8},{10,13... | collective-permute-start | bytes 1769480 | tf_op jit(solution)/shard_map/ppermute | solution.py:177
  20.9 14.7 %collective-permute-start.1 = (bf16[256,1152]{1,0:T(8,128)(2,1)}, bf16[256,1152]{1,0:T(8,128)(2,1)}, u32[]{:S(2)}, u32[]{:S(2)}) collective-permute-start(bf16[256,1152]{1,0:T(8,128)(2,1)} %get-tuple-element.246), channel_id=1, source_target_pairs={{2,4},{3,5},{4,2},{5,3},{10,12},{11,13},{12,10},{13,11},{18,20},{1... | collective-permute-start | bytes 1769480 | tf_op jit(solution)/shard_map/ppermute | solution.py:177
  44.5 18.6 %collective-permute-start.5 = (bf16[3,72,1792]{2,1,0:T(8,128)(2,1)}, bf16[3,72,1792]{2,1,0:T(8,128)(2,1)}, u32[]{:S(2)}, u32[]{:S(2)}) collective-permute-start(bf16[3,72,1792]{2,1,0:T(8,128)(2,1)} %pad_maximum_fusion.4.own), channel_id=1, source_target_pairs={{0,2},{1,3},{2,0},{3,1},{4,6},{5,7},{6,4},{7,5},{8,10},{9,11},{10,... | collective-permute-start | bytes 2322440 | tf_op jit(solution)/shard_map/ppermute | solution.py:177
  46.0 20.5 %collective-permute-start.4 = (bf16[3,72,1792]{2,1,0:T(8,128)(2,1)}, bf16[3,72,1792]{2,1,0:T(8,128)(2,1)}, u32[]{:S(2)}, u32[]{:S(2)}) collective-permute-start(bf16[3,72,1792]{2,1,0:T(8,128)(2,1)} %pad_maximum_fusion.4.own), channel_id=1, source_target_pairs={{0,1},{1,0},{2,3},{3,2},{4,5},{5,4},{6,7},{7,6},{8,9},{9,8},{10,11... | collective-permute-start | bytes 2322440 | tf_op jit(solution)/shard_map/ppermute | solution.py:177
  47.5 41.4 %all-to-all-start.1 = ((bf16[4,72,2816]{2,1,0:T(8,128)(2,1)}), bf16[4,72,2816]{2,1,0:T(8,128)(2,1)}, u32[]{:S(2)}, u32[]{:S(2)}) async-start(bf16[4,72,2816]{2,1,0:T(8,128)(2,1)} %broadcast_in_dim.52), calls=%async_computation.1 | async-start | bytes 3244032 | tf_op jit(solution)/shard_map/all_to_all | solution.py:195
  54.3 12.3 %collective-permute-start.6 = (bf16[512,1152]{1,0:T(8,128)(2,1)S(1)}, bf16[512,1152]{1,0:T(8,128)(2,1)}, u32[]{:S(2)}, u32[]{:S(2)}) collective-permute-start(bf16[512,1152]{1,0:T(8,128)(2,1)S(1)} %pad_maximum_fusion.1.half), channel_id=1, source_target_pairs={{0,4},{1,5},{2,6},{3,7},{4,0},{5,1},{6,2},{7,3},{8,12},{9,13},{10,... | collective-permute-start | bytes 3538952 | tf_op jit(solution)/shard_map/ppermute | solution.py:177
  56.0 17.0 %collective-permute-start.9 = (bf16[144,2176]{1,0:T(8,128)(2,1)}, bf16[144,2176]{1,0:T(8,128)(2,1)}, u32[]{:S(2)}, u32[]{:S(2)}) collective-permute-start(bf16[144,2176]{1,0:T(8,128)(2,1)} %get-tuple-element.485), channel_id=1, source_target_pairs={{0,4},{1,5},{2,6},{3,7},{4,0},{5,1},{6,2},{7,3},{8,12},{9,13},{10,... | collective-permute-start | bytes 1880072 | tf_op jit(solution)/shard_map/ppermute | solution.py:177
  58.1 21.0 %collective-permute-start.11 = (bf16[256,1152]{1,0:T(8,128)(2,1)}, bf16[256,1152]{1,0:T(8,128)(2,1)}, u32[]{:S(2)}, u32[]{:S(2)}) collective-permute-start(bf16[256,1152]{1,0:T(8,128)(2,1)} %get-tuple-element.257), channel_id=1, source_target_pairs={{0,1},{1,0},{2,5},{3,4},{4,3},{5,2},{6,7},{7,6},{8,9},{9,8},{10,13... | collective-permute-start | bytes 1769480 | tf_op jit(solution)/shard_map/ppermute | solution.py:177
  63.1 16.1 %collective-permute-start.10 = (bf16[256,1152]{1,0:T(8,128)(2,1)}, bf16[256,1152]{1,0:T(8,128)(2,1)}, u32[]{:S(2)}, u32[]{:S(2)}) collective-permute-start(bf16[256,1152]{1,0:T(8,128)(2,1)} %get-tuple-element.263), channel_id=1, source_target_pairs={{2,4},{3,5},{4,2},{5,3},{10,12},{11,13},{12,10},{13,11},{18,20},{1... | collective-permute-start | bytes 1769480 | tf_op jit(solution)/shard_map/ppermute | solution.py:177
  70.0 15.1 %collective-permute-start.7 = (bf16[3,72,896]{2,1,0:T(8,128)(2,1)}, bf16[3,72,896]{2,1,0:T(8,128)(2,1)S(1)}, u32[]{:S(2)}, u32[]{:S(2)}) collective-permute-start(bf16[3,72,896]{2,1,0:T(8,128)(2,1)} %slice.124), channel_id=1, source_target_pairs={{0,1},{1,0},{2,3},{3,2},{4,5},{5,4},{6,7},{7,6},{8,9},{9,8},{10,11... | collective-permute-start | bytes 1161224 | tf_op jit(solution)/shard_map/ppermute | solution.py:177
  71.5 17.2 %collective-permute-start.8 = (bf16[3,72,896]{2,1,0:T(8,128)(2,1)}, bf16[3,72,896]{2,1,0:T(8,128)(2,1)S(1)}, u32[]{:S(2)}, u32[]{:S(2)}) collective-permute-start(bf16[3,72,896]{2,1,0:T(8,128)(2,1)} %slice.125), channel_id=1, source_target_pairs={{0,2},{1,3},{2,0},{3,1},{4,6},{5,7},{6,4},{7,5},{8,10},{9,11},{10,... | collective-permute-start | bytes 1161224 | tf_op jit(solution)/shard_map/ppermute | solution.py:177
  90.4 27.8 %collective-permute-start.14 = (bf16[3,72,2816]{2,1,0:T(8,128)(2,1)S(1)}, bf16[3,72,2816]{2,1,0:T(8,128)(2,1)S(1)}, u32[]{:S(2)}, u32[]{:S(2)}) collective-permute-start(bf16[3,72,2816]{2,1,0:T(8,128)(2,1)S(1)} %pad_maximum_fusion.own), channel_id=1, source_target_pairs={{0,2},{1,3},{2,0},{3,1},{4,6},{5,7},{6,4},{7,5},{8,10},{9,11},{10,... | collective-permute-start | bytes 3649544 | tf_op jit(solution)/shard_map/ppermute | solution.py:177
  91.0 28.2 %collective-permute-start.13 = (bf16[3,72,2816]{2,1,0:T(8,128)(2,1)S(1)}, bf16[3,72,2816]{2,1,0:T(8,128)(2,1)S(1)}, u32[]{:S(2)}, u32[]{:S(2)}) collective-permute-start(bf16[3,72,2816]{2,1,0:T(8,128)(2,1)S(1)} %pad_maximum_fusion.own), channel_id=1, source_target_pairs={{0,1},{1,0},{2,3},{3,2},{4,5},{5,4},{6,7},{7,6},{8,9},{9,8},{10,11... | collective-permute-start | bytes 3649544 | tf_op jit(solution)/shard_map/ppermute | solution.py:177
  94.3 21.5 %collective-permute-start.15 = (bf16[512,1152]{1,0:T(8,128)(2,1)S(1)}, bf16[512,1152]{1,0:T(8,128)(2,1)S(1)}, u32[]{:S(2)}, u32[]{:S(2)}) collective-permute-start(bf16[512,1152]{1,0:T(8,128)(2,1)S(1)} %pad_maximum_fusion.2), channel_id=1, source_target_pairs={{0,4},{1,5},{2,6},{3,7},{4,0},{5,1},{6,2},{7,3},{8,12},{9,13},{10,... | collective-permute-start | bytes 3538952 | tf_op jit(solution)/shard_map/ppermute | solution.py:177
  121.4 33.3 %all-to-all-start.2 = ((bf16[4,72,2176]{2,1,0:T(8,128)(2,1)}), bf16[4,72,2176]{2,1,0:T(8,128)(2,1)}, u32[]{:S(2)}, u32[]{:S(2)}) async-start(bf16[4,72,2176]{2,1,0:T(8,128)(2,1)} %broadcast_in_dim.56), calls=%async_computation.2 | async-start | bytes 2506752 | tf_op jit(solution)/shard_map/all_to_all | solution.py:195
  125.9 27.8 %collective-permute-start.16 = (bf16[3,72,2816]{2,1,0:T(8,128)(2,1)S(1)}, bf16[3,72,2816]{2,1,0:T(8,128)(2,1)S(1)}, u32[]{:S(2)}, u32[]{:S(2)}) collective-permute-start(bf16[3,72,2816]{2,1,0:T(8,128)(2,1)S(1)} %pad_maximum_fusion.own), channel_id=1, source_target_pairs={{0,3},{1,2},{2,1},{3,0},{4,7},{5,6},{6,5},{7,4},{8,11},{9,10},{10,... | collective-permute-start | bytes 3649544 | tf_op jit(solution)/shard_map/ppermute | solution.py:177
  154.7 15.8 %collective-permute-start.19 = (bf16[1024,640]{1,0:T(8,128)(2,1)}, bf16[1024,640]{1,0:T(8,128)(2,1)}, u32[]{:S(2)}, u32[]{:S(2)}) collective-permute-start(bf16[1024,640]{1,0:T(8,128)(2,1)} %copy-done.5), channel_id=1, source_target_pairs={{0,4},{1,5},{2,6},{3,7},{4,0},{5,1},{6,2},{7,3},{8,12},{9,13},{10,... | collective-permute-start | bytes 3932168 | tf_op jit(solution)/shard_map/ppermute | solution.py:177
  160.6 9.9 %collective-permute-start.20 = (bf16[1152,640]{1,0:T(8,128)(2,1)}, bf16[1152,640]{1,0:T(8,128)(2,1)}, u32[]{:S(2)}, u32[]{:S(2)}) collective-permute-start(bf16[1152,640]{1,0:T(8,128)(2,1)} %bitcast.31.w_mine), channel_id=1, source_target_pairs={{0,4},{1,5},{2,6},{3,7},{4,0},{5,1},{6,2},{7,3},{8,12},{9,13},{10,... | collective-permute-start | bytes 4423688 | tf_op jit(solution)/shard_map/ppermute | solution.py:177
  163.4 23.3 %collective-permute-start.18 = (bf16[3,72,2176]{2,1,0:T(8,128)(2,1)}, bf16[3,72,2176]{2,1,0:T(8,128)(2,1)}, u32[]{:S(2)}, u32[]{:S(2)}) collective-permute-start(bf16[3,72,2176]{2,1,0:T(8,128)(2,1)} %pad_maximum_fusion.3.own), channel_id=1, source_target_pairs={{0,2},{1,3},{2,0},{3,1},{4,6},{5,7},{6,4},{7,5},{8,10},{9,11},{10,... | collective-permute-start | bytes 2820104 | tf_op jit(solution)/shard_map/ppermute | solution.py:177
  165.4 22.8 %collective-permute-start.17 = (bf16[3,72,2176]{2,1,0:T(8,128)(2,1)}, bf16[3,72,2176]{2,1,0:T(8,128)(2,1)}, u32[]{:S(2)}, u32[]{:S(2)}) collective-permute-start(bf16[3,72,2176]{2,1,0:T(8,128)(2,1)} %pad_maximum_fusion.3.own), channel_id=1, source_target_pairs={{0,1},{1,0},{2,3},{3,2},{4,5},{5,4},{6,7},{7,6},{8,9},{9,8},{10,11... | collective-permute-start | bytes 2820104 | tf_op jit(solution)/shard_map/ppermute | solution.py:177
  189.2 13.3 %collective-permute-start.21 = (bf16[3,72,1024]{2,1,0:T(8,128)(2,1)S(1)}, bf16[3,72,1024]{2,1,0:T(8,128)(2,1)S(1)}, u32[]{:S(2)}, u32[]{:S(2)}) collective-permute-start(bf16[3,72,1024]{2,1,0:T(8,128)(2,1)S(1)} %slice.128), channel_id=1, source_target_pairs={{0,1},{1,0},{2,3},{3,2},{4,5},{5,4},{6,7},{7,6},{8,9},{9,8},{10,11... | collective-permute-start | bytes 1327112 | tf_op jit(solution)/shard_map/ppermute | solution.py:177
  190.9 12.2 %collective-permute-start.22 = (bf16[3,72,1152]{2,1,0:T(8,128)(2,1)S(1)}, bf16[3,72,1152]{2,1,0:T(8,128)(2,1)S(1)}, u32[]{:S(2)}, u32[]{:S(2)}) collective-permute-start(bf16[3,72,1152]{2,1,0:T(8,128)(2,1)S(1)} %slice.129), channel_id=1, source_target_pairs={{0,2},{1,3},{2,0},{3,1},{4,6},{5,7},{6,4},{7,5},{8,10},{9,11},{10,... | collective-permute-start | bytes 1493000 | tf_op jit(solution)/shard_map/ppermute | solution.py:177
  210.8 114.5 %all-to-all-start.3 = ((bf16[4,288,2176]{2,1,0:T(8,128)(2,1)}), bf16[4,288,2176]{2,1,0:T(8,128)(2,1)}, u32[]{:S(2)}, u32[]{:S(2)}) async-start(bf16[4,288,2176]{2,1,0:T(8,128)(2,1)} %bitcast.101), calls=%async_computation.3 | async-start | bytes 10027008 | tf_op jit(solution)/shard_map/all_to_all | solution.py:195
  235.2 20.0 %collective-permute-start.23 = (bf16[1024,1152]{1,0:T(8,128)(2,1)}, bf16[1024,1152]{1,0:T(8,128)(2,1)}, u32[]{:S(2)}, u32[]{:S(2)}) collective-permute-start(bf16[1024,1152]{1,0:T(8,128)(2,1)} %convolution_convert_fusion.2.part), channel_id=1, source_target_pairs={{0,4},{1,5},{2,6},{3,7},{4,0},{5,1},{6,2},{7,3},{8,12},{9,13},{10,... | collective-permute-start | bytes 7077896 | tf_op jit(solution)/shard_map/ppermute | solution.py:177
  242.3 12.4 %collective-permute-start.24 = (bf16[512,1152]{1,0:T(8,128)(2,1)S(1)}, bf16[512,1152]{1,0:T(8,128)(2,1)S(1)}, u32[]{:S(2)}, u32[]{:S(2)}) collective-permute-start(bf16[512,1152]{1,0:T(8,128)(2,1)S(1)} %slice.162), channel_id=1, source_target_pairs={{0,4},{1,5},{2,6},{3,7},{4,0},{5,1},{6,2},{7,3},{8,12},{9,13},{10,... | collective-permute-start | bytes 3538952 | tf_op jit(solution)/shard_map/ppermute | solution.py:177
  255.2 43.3 %collective-permute-start.26 = (bf16[2,4,72,1152]{3,2,1,0:T(8,128)(2,1)}, bf16[2,4,72,1152]{3,2,1,0:T(8,128)(2,1)S(1)}, u32[]{:S(2)}, u32[]{:S(2)}) collective-permute-start(bf16[2,4,72,1152]{3,2,1,0:T(8,128)(2,1)} %get-tuple-element.319), channel_id=1, source_target_pairs={{0,2},{1,3},{2,0},{3,1},{4,6},{5,7},{6,4},{7,5},{8,10},{9,11},{10,... | collective-permute-start | bytes 3981320 | tf_op jit(solution)/shard_map/ppermute | solution.py:177
  256.2 42.2 %collective-permute-start.25 = (bf16[2,4,72,1024]{3,2,1,0:T(8,128)(2,1)}, bf16[2,4,72,1024]{3,2,1,0:T(8,128)(2,1)S(1)}, u32[]{:S(2)}, u32[]{:S(2)}) collective-permute-start(bf16[2,4,72,1024]{3,2,1,0:T(8,128)(2,1)} %get-tuple-element.318), channel_id=1, source_target_pairs={{0,1},{1,0},{2,3},{3,2},{4,5},{5,4},{6,7},{7,6},{8,9},{9,8},{10,11... | collective-permute-start | bytes 3538952 | tf_op jit(solution)/shard_map/ppermute | solution.py:177
  258.6 39.8 %collective-permute-start.28 = (bf16[256,1152]{1,0:T(8,128)(2,1)}, bf16[256,1152]{1,0:T(8,128)(2,1)}, u32[]{:S(2)}, u32[]{:S(2)}) collective-permute-start(bf16[256,1152]{1,0:T(8,128)(2,1)} %get-tuple-element.493), channel_id=1, source_target_pairs={{0,1},{1,0},{2,5},{3,4},{4,3},{5,2},{6,7},{7,6},{8,9},{9,8},{10,13... | collective-permute-start | bytes 1769480 | tf_op jit(solution)/shard_map/ppermute | solution.py:177
  259.2 39.3 %collective-permute-start.27 = (bf16[256,1152]{1,0:T(8,128)(2,1)S(1)}, bf16[256,1152]{1,0:T(8,128)(2,1)}, u32[]{:S(2)}, u32[]{:S(2)}) collective-permute-start(bf16[256,1152]{1,0:T(8,128)(2,1)S(1)} %get-tuple-element.407), channel_id=1, source_target_pairs={{2,4},{3,5},{4,2},{5,3},{10,12},{11,13},{12,10},{13,11},{18,20},{1... | collective-permute-start | bytes 1769480 | tf_op jit(solution)/shard_map/ppermute | solution.py:177
  300.4 19.9 %collective-permute-start.30 = (bf16[4,72,1152]{2,1,0:T(8,128)(2,1)S(1)}, bf16[4,72,1152]{2,1,0:T(8,128)(2,1)S(1)}, u32[]{:S(2)}, u32[]{:S(2)}) collective-permute-start(bf16[4,72,1152]{2,1,0:T(8,128)(2,1)S(1)} %get-tuple-element.335), channel_id=1, source_target_pairs={{0,1},{1,0},{2,3},{3,2},{4,5},{5,4},{6,7},{7,6},{8,9},{9,8},{10,11... | collective-permute-start | bytes 1990664 | tf_op jit(solution)/shard_map/ppermute | solution.py:177
  302.0 17.5 %collective-permute-start.29 = (bf16[4,72,1024]{2,1,0:T(8,128)(2,1)S(1)}, bf16[4,72,1024]{2,1,0:T(8,128)(2,1)S(1)}, u32[]{:S(2)}, u32[]{:S(2)}) collective-permute-start(bf16[4,72,1024]{2,1,0:T(8,128)(2,1)S(1)} %get-tuple-element.334), channel_id=1, source_target_pairs={{0,2},{1,3},{2,0},{3,1},{4,6},{5,7},{6,4},{7,5},{8,10},{9,11},{10,... | collective-permute-start | bytes 1769480 | tf_op jit(solution)/shard_map/ppermute | solution.py:177
  325.3 41.6 %collective-permute-start.31 = (bf16[2,4,72,1152]{3,2,1,0:T(8,128)(2,1)}, bf16[2,4,72,1152]{3,2,1,0:T(8,128)(2,1)}, u32[]{:S(2)}, u32[]{:S(2)}) collective-permute-start(bf16[2,4,72,1152]{3,2,1,0:T(8,128)(2,1)} %get-tuple-element.352), channel_id=1, source_target_pairs={{0,1},{1,0},{2,3},{3,2},{4,5},{5,4},{6,7},{7,6},{8,9},{9,8},{10,11... | collective-permute-start | bytes 3981320 | tf_op jit(solution)/shard_map/ppermute | solution.py:177
  326.4 40.4 %collective-permute-start.32 = (bf16[2,4,72,1280]{3,2,1,0:T(8,128)(2,1)}, bf16[2,4,72,1280]{3,2,1,0:T(8,128)(2,1)}, u32[]{:S(2)}, u32[]{:S(2)}) collective-permute-start(bf16[2,4,72,1280]{3,2,1,0:T(8,128)(2,1)} %get-tuple-element.353), channel_id=1, source_target_pairs={{0,2},{1,3},{2,0},{3,1},{4,6},{5,7},{6,4},{7,5},{8,10},{9,11},{10,... | collective-permute-start | bytes 4423688 | tf_op jit(solution)/shard_map/ppermute | solution.py:177
  337.3 14.2 %collective-permute-start.35 = (bf16[512,1152]{1,0:T(8,128)(2,1)}, bf16[512,1152]{1,0:T(8,128)(2,1)S(1)}, u32[]{:S(2)}, u32[]{:S(2)}) collective-permute-start(bf16[512,1152]{1,0:T(8,128)(2,1)} %slice.164), channel_id=1, source_target_pairs={{0,4},{1,5},{2,6},{3,7},{4,0},{5,1},{6,2},{7,3},{8,12},{9,13},{10,... | collective-permute-start | bytes 3538952 | tf_op jit(solution)/shard_map/ppermute | solution.py:177
  339.4 55.8 %all-to-all-start.4 = ((bf16[4,72,2176]{2,1,0:T(8,128)(2,1)}), bf16[4,72,2176]{2,1,0:T(8,128)(2,1)}, u32[]{:S(2)}, u32[]{:S(2)}) async-start(bf16[4,72,2176]{2,1,0:T(8,128)(2,1)} %copy-done.9), calls=%async_computation.4 | async-start | bytes 2506752 | tf_op jit(solution)/shard_map/all_to_all | solution.py:195
  350.0 16.8 %collective-permute-start.34 = (bf16[2,1,72,1152]{3,2,1,0:T(8,128)(2,1)}, bf16[2,1,72,1152]{3,2,1,0:T(8,128)(2,1)}, u32[]{:S(2)}, u32[]{:S(2)}) collective-permute-start(bf16[2,1,72,1152]{3,2,1,0:T(8,128)(2,1)} %get-tuple-element.358), channel_id=1, source_target_pairs={{0,2},{1,3},{2,0},{3,1},{4,6},{5,7},{6,4},{7,5},{8,10},{9,11},{10,... | collective-permute-start | bytes 995336 | tf_op jit(solution)/shard_map/ppermute | solution.py:177
  350.6 11.4 %collective-permute-start.33 = (bf16[2,1,72,1024]{3,2,1,0:T(8,128)(2,1)}, bf16[2,1,72,1024]{3,2,1,0:T(8,128)(2,1)}, u32[]{:S(2)}, u32[]{:S(2)}) collective-permute-start(bf16[2,1,72,1024]{3,2,1,0:T(8,128)(2,1)} %get-tuple-element.357), channel_id=1, source_target_pairs={{0,1},{1,0},{2,3},{3,2},{4,5},{5,4},{6,7},{7,6},{8,9},{9,8},{10,11... | collective-permute-start | bytes 884744 | tf_op jit(solution)/shard_map/ppermute | solution.py:177
  356.6 10.2 %collective-permute-start.36 = (f32[18,128]{1,0:T(8,128)S(1)}, f32[18,128]{1,0:T(8,128)S(1)}, u32[]{:S(2)}, u32[]{:S(2)}) collective-permute-start(f32[18,128]{1,0:T(8,128)S(1)} %reshape.153), channel_id=1, source_target_pairs={{0,4},{1,5},{2,6},{3,7},{4,0},{5,1},{6,2},{7,3},{8,12},{9,13},{10,... | collective-permute-start | bytes 27656 | tf_op jit(solution)/shard_map/ppermute | solution.py:177
  373.6 21.6 %collective-permute-start.38 = (bf16[4,72,1280]{2,1,0:T(8,128)(2,1)}, bf16[4,72,1280]{2,1,0:T(8,128)(2,1)S(1)}, u32[]{:S(2)}, u32[]{:S(2)}) collective-permute-start(bf16[4,72,1280]{2,1,0:T(8,128)(2,1)} %get-tuple-element.372), channel_id=1, source_target_pairs={{0,1},{1,0},{2,3},{3,2},{4,5},{5,4},{6,7},{7,6},{8,9},{9,8},{10,11... | collective-permute-start | bytes 2211848 | tf_op jit(solution)/shard_map/ppermute | solution.py:177
  374.4 20.8 %collective-permute-start.37 = (bf16[4,72,1152]{2,1,0:T(8,128)(2,1)}, bf16[4,72,1152]{2,1,0:T(8,128)(2,1)}, u32[]{:S(2)}, u32[]{:S(2)}) collective-permute-start(bf16[4,72,1152]{2,1,0:T(8,128)(2,1)} %get-tuple-element.371), channel_id=1, source_target_pairs={{0,2},{1,3},{2,0},{3,1},{4,6},{5,7},{6,4},{7,5},{8,10},{9,11},{10,... | collective-permute-start | bytes 1990664 | tf_op jit(solution)/shard_map/ppermute | solution.py:177
  377.8 16.8 %collective-permute-start.40 = (bf16[1,72,1152]{2,1,0:T(8,128)(2,1)S(1)}, bf16[1,72,1152]{2,1,0:T(8,128)(2,1)S(1)}, u32[]{:S(2)}, u32[]{:S(2)}) collective-permute-start(bf16[1,72,1152]{2,1,0:T(8,128)(2,1)S(1)} %get-tuple-element.380), channel_id=1, source_target_pairs={{0,1},{1,0},{2,3},{3,2},{4,5},{5,4},{6,7},{7,6},{8,9},{9,8},{10,11... | collective-permute-start | bytes 497672 | tf_op jit(solution)/shard_map/ppermute | solution.py:177
  378.9 14.9 %collective-permute-start.39 = (bf16[1,72,1024]{2,1,0:T(8,128)(2,1)S(1)}, bf16[1,72,1024]{2,1,0:T(8,128)(2,1)S(1)}, u32[]{:S(2)}, u32[]{:S(2)}) collective-permute-start(bf16[1,72,1024]{2,1,0:T(8,128)(2,1)S(1)} %get-tuple-element.379), channel_id=1, source_target_pairs={{0,2},{1,3},{2,0},{3,1},{4,6},{5,7},{6,4},{7,5},{8,10},{9,11},{10,... | collective-permute-start | bytes 442376 | tf_op jit(solution)/shard_map/ppermute | solution.py:177
  379.5 14.3 %collective-permute-start.41 = (f32[18,128]{1,0:T(8,128)S(1)}, f32[18,128]{1,0:T(8,128)S(1)}, u32[]{:S(2)}, u32[]{:S(2)}) collective-permute-start(f32[18,128]{1,0:T(8,128)S(1)} %add.168), channel_id=1, source_target_pairs={{0,1},{1,0},{2,3},{3,2},{4,5},{5,4},{6,7},{7,6},{8,9},{9,8},{10,11... | collective-permute-start | bytes 27656 | tf_op jit(solution)/shard_map/ppermute | solution.py:177
  398.7 36.8 %all-to-all-start.5 = ((bf16[4,72,2432]{2,1,0:T(8,128)(2,1)}), bf16[4,72,2432]{2,1,0:T(8,128)(2,1)}, u32[]{:S(2)}, u32[]{:S(2)}) async-start(bf16[4,72,2432]{2,1,0:T(8,128)(2,1)} %shard_map.189), calls=%async_computation.5 | async-start | bytes 2801664 | tf_op jit(solution)/shard_map/all_to_all | solution.py:195
  404.1 16.2 %collective-permute-start.48 = (bf16[256,1152]{1,0:T(8,128)(2,1)}, bf16[256,1152]{1,0:T(8,128)(2,1)}, u32[]{:S(2)}, u32[]{:S(2)}) collective-permute-start(bf16[256,1152]{1,0:T(8,128)(2,1)} %get-tuple-element.491), channel_id=1, source_target_pairs={{0,1},{1,0},{2,5},{3,4},{4,3},{5,2},{6,7},{7,6},{8,9},{9,8},{10,13... | collective-permute-start | bytes 1769480 | tf_op jit(solution)/shard_map/ppermute | solution.py:177
  405.0 16.2 %collective-permute-start.47 = (bf16[256,1152]{1,0:T(8,128)(2,1)S(1)}, bf16[256,1152]{1,0:T(8,128)(2,1)}, u32[]{:S(2)}, u32[]{:S(2)}) collective-permute-start(bf16[256,1152]{1,0:T(8,128)(2,1)S(1)} %get-tuple-element.404), channel_id=1, source_target_pairs={{2,4},{3,5},{4,2},{5,3},{10,12},{11,13},{12,10},{13,11},{18,20},{1... | collective-permute-start | bytes 1769480 | tf_op jit(solution)/shard_map/ppermute | solution.py:177
  406.6 28.9 %collective-permute-start.45 = (bf16[72,2176]{1,0:T(8,128)(2,1)S(1)}, bf16[72,2176]{1,0:T(8,128)(2,1)S(1)}, u32[]{:S(2)}, u32[]{:S(2)}) collective-permute-start(bf16[72,2176]{1,0:T(8,128)(2,1)S(1)} %bitcast.97), channel_id=1, source_target_pairs={{0,2},{1,3},{2,0},{3,1},{4,6},{5,7},{6,4},{7,5},{8,10},{9,11},{10,... | collective-permute-start | bytes 940040 | tf_op jit(solution)/shard_map/ppermute | solution.py:177
  409.7 25.8 %collective-permute-start.44 = (bf16[72,2176]{1,0:T(8,128)(2,1)S(1)}, bf16[72,2176]{1,0:T(8,128)(2,1)S(1)}, u32[]{:S(2)}, u32[]{:S(2)}) collective-permute-start(bf16[72,2176]{1,0:T(8,128)(2,1)S(1)} %bitcast.98), channel_id=1, source_target_pairs={{0,1},{1,0},{2,3},{3,2},{4,5},{5,4},{6,7},{7,6},{8,9},{9,8},{10,11... | collective-permute-start | bytes 940040 | tf_op jit(solution)/shard_map/ppermute | solution.py:177
  412.3 23.1 %collective-permute-start.43 = (bf16[72,2176]{1,0:T(8,128)(2,1)S(1)}, bf16[72,2176]{1,0:T(8,128)(2,1)S(1)}, u32[]{:S(2)}, u32[]{:S(2)}) collective-permute-start(bf16[72,2176]{1,0:T(8,128)(2,1)S(1)} %reduce_sum.24.refs_0_), channel_id=1, source_target_pairs={{0,2},{1,3},{2,0},{3,1},{4,6},{5,7},{6,4},{7,5},{8,10},{9,11},{10,... | collective-permute-start | bytes 940040 | tf_op jit(solution)/shard_map/ppermute | solution.py:177
  420.3 15.2 %collective-permute-start.42 = (bf16[72,2176]{1,0:T(8,128)(2,1)S(1)}, bf16[72,2176]{1,0:T(8,128)(2,1)S(1)}, u32[]{:S(2)}, u32[]{:S(2)}) collective-permute-start(bf16[72,2176]{1,0:T(8,128)(2,1)S(1)} %reduce_sum.24.refs_0_), channel_id=1, source_target_pairs={{0,1},{1,0},{2,3},{3,2},{4,5},{5,4},{6,7},{7,6},{8,9},{9,8},{10,11... | collective-permute-start | bytes 940040 | tf_op jit(solution)/shard_map/ppermute | solution.py:177
  421.2 14.3 %collective-permute-start.46 = (f32[18,128]{1,0:T(8,128)S(1)}, f32[18,128]{1,0:T(8,128)S(1)}, u32[]{:S(2)}, u32[]{:S(2)}) collective-permute-start(f32[18,128]{1,0:T(8,128)S(1)} %add.169), channel_id=1, source_target_pairs={{0,2},{1,3},{2,0},{3,1},{4,6},{5,7},{6,4},{7,5},{8,10},{9,11},{10,... | collective-permute-start | bytes 27656 | tf_op jit(solution)/shard_map/ppermute | solution.py:177
  437.1 19.8 %collective-permute-start.52 = (bf16[72,2432]{1,0:T(8,128)(2,1)S(1)}, bf16[72,2432]{1,0:T(8,128)(2,1)S(1)}, u32[]{:S(2)}, u32[]{:S(2)}) collective-permute-start(bf16[72,2432]{1,0:T(8,128)(2,1)S(1)} %reduce_sum.25.refs_0_), channel_id=1, source_target_pairs={{0,2},{1,3},{2,0},{3,1},{4,6},{5,7},{6,4},{7,5},{8,10},{9,11},{10,... | collective-permute-start | bytes 1050632 | tf_op jit(solution)/shard_map/ppermute | solution.py:177
  437.2 19.7 %collective-permute-start.51 = (bf16[72,2432]{1,0:T(8,128)(2,1)S(1)}, bf16[72,2432]{1,0:T(8,128)(2,1)S(1)}, u32[]{:S(2)}, u32[]{:S(2)}) collective-permute-start(bf16[72,2432]{1,0:T(8,128)(2,1)S(1)} %reduce_sum.25.refs_0_), channel_id=1, source_target_pairs={{0,1},{1,0},{2,3},{3,2},{4,5},{5,4},{6,7},{7,6},{8,9},{9,8},{10,11... | collective-permute-start | bytes 1050632 | tf_op jit(solution)/shard_map/ppermute | solution.py:177
  441.1 10.3 %collective-permute-start.53 = (bf16[72,1024]{1,0:T(8,128)(2,1)S(1)}, bf16[72,1024]{1,0:T(8,128)(2,1)S(1)}, u32[]{:S(2)}, u32[]{:S(2)}) collective-permute-start(bf16[72,1024]{1,0:T(8,128)(2,1)S(1)} %slice.146), channel_id=1, source_target_pairs={{0,1},{1,0},{2,3},{3,2},{4,5},{5,4},{6,7},{7,6},{8,9},{9,8},{10,11... | collective-permute-start | bytes 442376 | tf_op jit(solution)/shard_map/ppermute | solution.py:177
  442.0 14.3 %collective-permute-start.49 = (bf16[72,1024]{1,0:T(8,128)(2,1)S(1)}, bf16[72,1024]{1,0:T(8,128)(2,1)S(1)}, u32[]{:S(2)}, u32[]{:S(2)}) collective-permute-start(bf16[72,1024]{1,0:T(8,128)(2,1)S(1)} %slice.144), channel_id=1, source_target_pairs={{0,1},{1,0},{2,3},{3,2},{4,5},{5,4},{6,7},{7,6},{8,9},{9,8},{10,11... | collective-permute-start | bytes 442376 | tf_op jit(solution)/shard_map/ppermute | solution.py:177
  443.3 13.1 %collective-permute-start.54 = (bf16[72,1152]{1,0:T(8,128)(2,1)S(1)}, bf16[72,1152]{1,0:T(8,128)(2,1)S(1)}, u32[]{:S(2)}, u32[]{:S(2)}) collective-permute-start(bf16[72,1152]{1,0:T(8,128)(2,1)S(1)} %slice.147), channel_id=1, source_target_pairs={{0,2},{1,3},{2,0},{3,1},{4,6},{5,7},{6,4},{7,5},{8,10},{9,11},{10,... | collective-permute-start | bytes 497672 | tf_op jit(solution)/shard_map/ppermute | solution.py:177
  451.4 5.5 %collective-permute-start.50 = (bf16[72,1152]{1,0:T(8,128)(2,1)S(1)}, bf16[72,1152]{1,0:T(8,128)(2,1)S(1)}, u32[]{:S(2)}, u32[]{:S(2)}) collective-permute-start(bf16[72,1152]{1,0:T(8,128)(2,1)S(1)} %slice.145), channel_id=1, source_target_pairs={{0,2},{1,3},{2,0},{3,1},{4,6},{5,7},{6,4},{7,5},{8,10},{9,11},{10,... | collective-permute-start | bytes 497672 | tf_op jit(solution)/shard_map/ppermute | solution.py:177
  457.5 8.8 %collective-permute-start.59 = (bf16[2,72,2176]{2,1,0:T(8,128)(2,1)S(1)}, bf16[2,72,2176]{2,1,0:T(8,128)(2,1)S(1)}, u32[]{:S(2)}, u32[]{:S(2)}) collective-permute-start(bf16[2,72,2176]{2,1,0:T(8,128)(2,1)S(1)} %shard_map.192), channel_id=1, source_target_pairs={{0,4},{1,5},{2,6},{3,7},{4,0},{5,1},{6,2},{7,3},{8,12},{9,13},{10,... | collective-permute-start | bytes 1880072 | tf_op jit(solution)/shard_map/ppermute | solution.py:177
  458.2 8.0 %collective-permute-start.56 = (bf16[2,72,2176]{2,1,0:T(8,128)(2,1)S(1)}, bf16[2,72,2176]{2,1,0:T(8,128)(2,1)S(1)}, u32[]{:S(2)}, u32[]{:S(2)}) collective-permute-start(bf16[2,72,2176]{2,1,0:T(8,128)(2,1)S(1)} %shard_map.191), channel_id=1, source_target_pairs={{0,4},{1,5},{2,6},{3,7},{4,0},{5,1},{6,2},{7,3},{8,12},{9,13},{10,... | collective-permute-start | bytes 1880072 | tf_op jit(solution)/shard_map/ppermute | solution.py:177
  458.8 7.5 %collective-permute-start.58 = (bf16[72,1280]{1,0:T(8,128)(2,1)S(1)}, bf16[72,1280]{1,0:T(8,128)(2,1)S(1)}, u32[]{:S(2)}, u32[]{:S(2)}) collective-permute-start(bf16[72,1280]{1,0:T(8,128)(2,1)S(1)} %slice.149), channel_id=1, source_target_pairs={{0,2},{1,3},{2,0},{3,1},{4,6},{5,7},{6,4},{7,5},{8,10},{9,11},{10,... | collective-permute-start | bytes 552968 | tf_op jit(solution)/shard_map/ppermute | solution.py:177
  460.3 6.0 %collective-permute-start.57 = (bf16[72,1152]{1,0:T(8,128)(2,1)S(1)}, bf16[72,1152]{1,0:T(8,128)(2,1)S(1)}, u32[]{:S(2)}, u32[]{:S(2)}) collective-permute-start(bf16[72,1152]{1,0:T(8,128)(2,1)S(1)} %slice.148), channel_id=1, source_target_pairs={{0,1},{1,0},{2,3},{3,2},{4,5},{5,4},{6,7},{7,6},{8,9},{9,8},{10,11... | collective-permute-start | bytes 497672 | tf_op jit(solution)/shard_map/ppermute | solution.py:177
  469.3 6.6 %collective-permute-start.61 = (bf16[2,72,2432]{2,1,0:T(8,128)(2,1)}, bf16[2,72,2432]{2,1,0:T(8,128)(2,1)}, u32[]{:S(2)}, u32[]{:S(2)}) collective-permute-start(bf16[2,72,2432]{2,1,0:T(8,128)(2,1)} %shard_map.193), channel_id=1, source_target_pairs={{0,4},{1,5},{2,6},{3,7},{4,0},{5,1},{6,2},{7,3},{8,12},{9,13},{10,... | collective-permute-start | bytes 2101256 | tf_op jit(solution)/shard_map/ppermute | solution.py:177
  (109 other events, 893.7 us)

commit v2 on v1

--- a/solution.py
+++ b/solution.py
@@ -979,7 +979,7 @@
 
     upstream_in = Transfer(to_image(place, *upstream_parts))
     other_mask = place.core(key_mask)
-    close_round(qkv, tokens_in)
+    close_round(qkv, tokens_in, down)
 
     live_keys = image_order(place, pick(jnp.where(c == place.y, key_mask, other_mask), place.x))
     mask_bias = jnp.where(live_keys > 0, 0.0, NEG_FILL).astype(F32)[:, None]
@@ -996,7 +996,7 @@
     tokens, first_normed, first_inv, first_low, packed = norm_and_project(
         *tokens_in.result, full_first, qkv_shift, small_rows, 3 * half_width
     )
-    (packed,) = close_round(out_up, down, upstream_in, hold=(packed,))
+    (packed,) = close_round(out_up, upstream_in, hold=(packed,))
 
     attended_half, raised, inv_total = attention_forward(packed, mask_bias)
     (attended_half,) = close_round(out_up, down, hold=(attended_half,))

time: 491 us -> 492 us (level)
  local copies, waits for them, and re-layouts: 69.9 us -> 61.8 us
  Pallas kernels: 137 us -> 143 us
  waiting for transfers between devices: 101 us -> 107 us
    all_to_all x6, waiting for transfers between devices: 10.8 us -> 25.2 us  [over_z(): lax.all_to_all(value, 'fsdp', 0, 0, axis_index_groups=self.z_lines, tiled...]
    ppermute x62, waiting for transfers between devices: 90.5 us -> 81.6 us  [send(): return lax.ppermute(value, ('fsdp', 'seq'), pairs)]
    unnamed x212 -> x202, local copies, waits for them, and re-layouts: 43.7 us -> 35.1 us
  transfers between devices with their start and end apart: 68 -> 68, of which waited for: 25 -> 20; matrix products, arithmetic and copies ran while one was open for 17% -> 17% of each run, Pallas kernels for 26% -> 28%
where the time goes in v2:
time: 492 us; the launch traced here: 484 us
  Pallas kernels  143 us (29%)
  waiting for transfers between devices  107 us (22%)
  starting transfers between devices  97.8 us (20%)
  local copies, waits for them, and re-layouts  61.8 us (13%)
  matrix products  50.1 us (10%)
  other arithmetic  22.4 us (5%)
    ppermute x62, waiting for transfers between devices, send(): return lax.ppermute(value, ('fsdp', 'seq'), pairs)  81.6 us
    ppermute x62, starting transfers between devices, send(): return lax.ppermute(value, ('fsdp', 'seq'), pairs)  69.7 us
    unnamed x202, local copies, waits for them, and re-layouts  35.1 us
    all_to_all x6, starting transfers between devices, over_z(): lax.all_to_all(value, 'fsdp', 0, 0, axis_index_groups=self.z_lines, tiled...  28.1 us
    pallas_call x1, Pallas kernels, attention_backward(): pl.pallas_call(functools.partial(attention_backward_kernel, block, heads)...  26.3 us
    all_to_all x6, waiting for transfers between devices, over_z(): lax.all_to_all(value, 'fsdp', 0, 0, axis_index_groups=self.z_lines, tiled...  25.2 us
    pallas_call x2, Pallas kernels, weight_grad(): pl.pallas_call(functools.partial(weight_grad_kernel, cut, group, rows, le...  24.3 us
    dot_general x3, matrix products, dot_t(): lax.dot_general(a, b, (((1,), (1,)), ((), ())), preferred_element_type=F32)  22.6 us
  transfers between devices with their start and end apart: 68, of which 20 were waited for; matrix products, arithmetic and copies ran while one was open for 17% of the time, Pallas kernels for 28%

profile of v2, /device:TPU:0, one launch (start us, length us, event | category | flops | bytes accessed | tf_op | source)
XLA Modules:
  0.0 484.1 jit_solution(8898353772089028608)
XLA Ops:
  5.0 2.3 dynamic-slice_bitcast_fusion.4
  7.4 2.5 collective-permute-start.2
  9.9 1.5 collective-permute-start.1
  14.1 4.9 %all-to-all-start = ((bf16[4,72,1792]{2,1,0:T(8,128)(2,1)}), bf16[4,72,1792]{2,1,0:T(8,128)(2,1)S(1)}, u32[]{:S(2)}, u32[]{:S(2)}) async-start(bf16[4,72,1792]{2,1,0:T(8,128)(2,1)} %broadcast_in_dim.50), calls=%async_computation | async-start | bytes 2064384 | tf_op jit(solution)/shard_map/all_to_all | solution.py:195
  19.4 1.9 collective-permute-start.3
  24.5 20.4 %all-to-all-done = bf16[4,72,1792]{2,1,0:T(8,128)(2,1)S(1)} async-done(((bf16[4,72,1792]{2,1,0:T(8,128)(2,1)}), bf16[4,72,1792]{2,1,0:T(8,128)(2,1)S(1)}, u32[]{:S(2)}, u32[]{:S(2)}) %all-to-all-start) | async-done | bytes 1032224 | tf_op jit(solution)/shard_map/all_to_all | solution.py:195
  45.0 2.5 broadcast_in_dim.52
  47.5 4.4 all-to-all-start.1
  57.4 1.5 fusion.10
  65.1 10.6 %collective-permute-done.5.y_part = bf16[3,72,1792]{2,1,0:T(8,128)(2,1)} collective-permute-done((bf16[3,72,1792]{2,1,0:T(8,128)(2,1)}, bf16[3,72,1792]{2,1,0:T(8,128)(2,1)}, u32[]{:S(2)}, u32[]{:S(2)}) %collective-permute-start.5) | collective-permute-done | bytes 774176 | tf_op jit(solution)/shard_map/ppermute | solution.py:177
  75.8 1.6 collective-permute-done.4.x_part
  81.3 1.6 maximum_select_fusion.1
  84.0 6.0 %collective-permute-done.11 = bf16[256,1152]{1,0:T(8,128)(2,1)} collective-permute-done((bf16[256,1152]{1,0:T(8,128)(2,1)}, bf16[256,1152]{1,0:T(8,128)(2,1)}, u32[]{:S(2)}, u32[]{:S(2)}) %collective-permute-start.11) | collective-permute-done | bytes 589856 | tf_op jit(solution)/shard_map/ppermute | solution.py:177
  90.0 7.3 %collective-permute-done.8.refs_0_ = bf16[3,72,896]{2,1,0:T(8,128)(2,1)S(1)} collective-permute-done((bf16[3,72,896]{2,1,0:T(8,128)(2,1)S(1)}, bf16[3,72,896]{2,1,0:T(8,128)(2,1)S(1)}, u32[]{:S(2)}, u32[]{:S(2)}) %collective-permute-start.8) | collective-permute-done | bytes 387104 | tf_op jit(solution)/shard_map/ppermute | solution.py:177
  101.9 2.2 pad_maximum_fusion.2
  104.0 4.7 all-to-all-start.2
  112.0 2.8 shard_map.170
  117.0 7.9 %shard_map.172 = (bf16[1024,1152]{1,0:T(8,128)(2,1)S(1)}, bf16[1024,1152]{1,0:T(8,128)(2,1)S(1)}, f32[1024,1]{1,0:T(8,128)S(1)}, bf16[1024,1152]{1,0:T(8,128)(2,1)S(1)}, bf16[1024,1728]{1,0:T(8,128)(2,1)S(1)}) custom-call(bf16[512,1152]{1,0:T(8,128)(2,1)S(1)} %copy-done.11, bf16[512,1152]{1,0:T(8,128)(2,1)} %collective-permute-done.6.other, ...), custom_call_target="tpu_custom_call" | custom-call | flops 589824 | bytes 589824 | tf_op jit(solution)/shard_map/pallas_call | solution.py:650
  129.9 2.3 collective-permute-start.16
  132.2 19.5 %shard_map.173 = (bf16[1024,640]{1,0:T(8,128)(2,1)S(1)}, bf16[8,1024,1024]{2,1,0:T(8,128)(2,1)}, f32[8,1,1024]{2,1,0:T(1,128)S(1)}) custom-call(bf16[1024,1728]{1,0:T(8,128)(2,1)S(1)} %get-tuple-element.283.qkv_ref, f32[1024,1]{1,0:T(8,128)S(1)} %broadcast_select_fusion.2.bias_ref), custom_call_target="tpu_custom_call" | custom-call | flops 8388608 | bytes 1769472 | tf_op jit(solution)/shard_map/pallas_call | solution.py:61
  151.7 1.8 copy-done.1
  154.6 5.3 %collective-permute-done.16.refs_0_ = bf16[3,72,2816]{2,1,0:T(8,128)(2,1)} collective-permute-done((bf16[3,72,2816]{2,1,0:T(8,128)(2,1)S(1)}, bf16[3,72,2816]{2,1,0:T(8,128)(2,1)}, u32[]{:S(2)}, u32[]{:S(2)}) %collective-permute-start.16) | collective-permute-done | bytes 1216544 | tf_op jit(solution)/shard_map/ppermute | solution.py:177
  159.9 3.1 shard_map.174
  171.8 3.7 shard_map.176
  175.6 11.0 %shard_map.175 = (bf16[1024,1152]{1,0:T(8,128)(2,1)S(1)}, bf16[1152,1152]{1,0:T(8,128)(2,1)S(1)}, f32[512,1152]{1,0:T(8,128)S(1)}, bf16[1024,1152]{1,0:T(8,128)(...) custom-call(s32[5]{0:T(128)S(1)} %stack.66.where, bf16[1024,1152]{1,0:T(8,128)(2,1)S(1)} %copy-done.14, ...), custom_call_target="tpu_custom_call" | custom-call | flops 1179648 | bytes 1179648 | tf_op jit(solution)/shard_map/pallas_call | solution.py:708
  186.6 2.3 collective-permute-done.18.y_part
  194.4 11.0 %add_convert_fusion = (bf16[1024,2176]{1,0:T(8,128)(2,1)}, bf16[1024,2176]{1,0:T(8,128)(2,1)S(1)}) fusion(f32[2176]{0:T(1024)S(1)} %dynamic-slice_reduce_fusion, bf16[1024,1152]{1,0:T(8,128)(2,1)S(1)} %get-tuple-element.296.refs_0_, bf16[1152,2176]{1,0:T(8,128)(2,1)S(1)} %bitcast.93), kind=kOutput, calls=%fused_computation.2 | convolution fusion | flops 5178392576 | bytes 16294400 | tf_op jit(solution)/shard_map/dot_general | solution.py:925
  205.8 7.6 %convolution_convert_fusion = bf16[1152,2176]{1,0:T(8,128)(2,1)} fusion(bf16[1024,1152]{1,0:T(8,128)(2,1)S(1)} %constant_dynamic-update-slice_fusion.upstream, bf16[1024,2176]{1,0:T(8,128)(2,1)S(1)} %get-tuple-element.315), kind=kOutput, calls=%fused_computation | convolution fusion | flops 5136334848 | bytes 11829248 | tf_op jit(solution)/shard_map/dot_general | solution.py:933
  213.4 5.2 %all-to-all-start.3 = ((bf16[4,288,2176]{2,1,0:T(8,128)(2,1)}), bf16[4,288,2176]{2,1,0:T(8,128)(2,1)}, u32[]{:S(2)}, u32[]{:S(2)}) async-start(bf16[4,288,2176]{2,1,0:T(8,128)(2,1)} %bitcast.101), calls=%async_computation.3 | async-start | bytes 10027008 | tf_op jit(solution)/shard_map/all_to_all | solution.py:195
  218.6 3.2 shard_map.177
  221.8 8.4 %multiply_convert_fusion.refs_1_ = bf16[1024,2176]{1,0:T(8,128)(2,1)S(1)} fusion(bf16[1024,2176]{1,0:T(8,128)(2,1)} %get-tuple-element.309, bf16[1024,1152]{1,0:T(8,128)(2,1)S(1)} %copy-done.75, bf16[1152,2176]{1,0:T(8,128)(2,1)S(1)} %bitcast.91), kind=kOutput, calls=%fused_computation.1 | convolution fusion | flops 5140512768 | bytes 16285696 | tf_op jit(solution)/shard_map/dot_general | solution.py:925
  230.3 7.5 %convolution_convert_fusion.2.part = bf16[1024,1152]{1,0:T(8,128)(2,1)} fusion(bf16[1024,2176]{1,0:T(8,128)(2,1)S(1)} %multiply_convert_fusion.refs_1_, bf16[1152,2176]{1,0:T(8,128)(2,1)S(1)} %bitcast.96), kind=kOutput, calls=%fused_computation.9 | convolution fusion | flops 5135007744 | bytes 11829248 | tf_op jit(solution)/shard_map/dot_general | solution.py:929
  237.9 6.8 %convolution_convert_fusion.1 = bf16[1024,1152]{1,0:T(8,128)(2,1)S(1)} fusion(bf16[1024,2176]{1,0:T(8,128)(2,1)S(1)} %bitcast.110, bf16[1152,2176]{1,0:T(8,128)(2,1)S(1)} %bitcast.92), kind=kOutput, calls=%fused_computation.8 | convolution fusion | flops 5135007744 | bytes 11829248 | tf_op jit(solution)/shard_map/dot_general | solution.py:929
  245.9 11.3 %shard_map.178 = (bf16[2,4,72,1024]{3,2,1,0:T(8,128)(2,1)}, bf16[2,4,72,1024]{3,2,1,0:T(8,128)(2,1)}, bf16[2,4,72,1152]{3,2,1,0:T(8,128)(2,1)}, bf16[2,4,72,1152]{3,2,1,0:T(8,128)(2,1)}, f32[8,2176]{1,0:T(8,128)}) custom-call(s32[5]{0:T(128)} %copy-done.61, bf16[1024,1152]{1,0:T(8,128)(2,1)} %copy-done.17, bf16[1024,2176]{1,0:T(8,128)(2,1)} %copy-done.76), custom_call_target="tpu_custom_call" | custom-call | flops 1179648 | bytes 2506752 | tf_op jit(solution)/shard_map/pallas_call | solution.py:412
  263.1 11.7 %shard_map.179 = (bf16[1024,576]{1,0:T(8,128)(2,1)}, bf16[1024,576]{1,0:T(8,128)(2,1)}, f32[512,1152]{1,0:T(8,128)}, f32[8,1152]{1,0:T(8,128)}) custom-call(s32[5]{0:T(128)} %copy-done.61, bf16[1024,1152]{1,0:T(8,128)(2,1)} %convolution_convert_fusion.2.part, bf16[1024,1152]{1,0:T(8,128)(2,1)} %collective-permute-done.23.arrived, ...), custom_call_target="tpu_custom_call" | custom-call | tf_op jit(solution)/shard_map/pallas_call | solution.py:795
  274.8 26.3 %shard_map.180.refs_2_ = bf16[1024,1728]{1,0:T(8,128)(2,1)} custom-call(bf16[1024,1728]{1,0:T(8,128)(2,1)} %copy-done.1, bf16[1024,576]{1,0:T(8,128)(2,1)} %get-tuple-element.325.d_out_ref, bf16[1024,640]{1,0:T(8,128)(2,1)} %copy-done.4, bf16[8,1024,1024]{2,1,0:T(8,128)(2,1)} %get-tuple-element.326.probs_ref, f32[8,1,1024]{2,1,0:T(1,128)} %copy-done.72), custom_call_target="tpu_custom_call" | custom-call | flops 8388608 | bytes 1769472 | tf_op jit(solution)/shard_map/pallas_call | solution.py:132
  304.0 2.4 collective-permute-start.29
  308.5 13.1 %shard_map.183 = (bf16[2,4,72,1152]{3,2,1,0:T(8,128)(2,1)}, bf16[2,4,72,1152]{3,2,1,0:T(8,128)(2,1)}, bf16[2,4,72,1280]{3,2,1,0:T(8,128)(2,1)}, bf16[2,4,72,1280]{3,2,1,0:T(8,128)(2,1)}) custom-call(s32[5]{0:T(128)} %copy-done.61, bf16[1024,1152]{1,0:T(8,128)(2,1)} %copy-done.20, bf16[1024,1152]{1,0:T(8,128)(2,1)} %copy-done.21, ...), custom_call_target="tpu_custom_call" | custom-call | flops 1179648 | bytes 2801664 | tf_op jit(solution)/shard_map/pallas_call | solution.py:412
  323.2 4.8 all-to-all-done.3.arrived
  329.9 8.3 %fusion.2.part = bf16[1024,1152]{1,0:T(8,128)(2,1)S(1)} fusion(bf16[1024,1728]{1,0:T(8,128)(2,1)} %shard_map.180.refs_2_, bf16[1152,1792]{1,0:T(8,128)(2,1)} %bitcast.83), kind=kOutput, calls=%fused_computation.10 | convolution fusion | flops 4078043136 | bytes 10027008 | tf_op jit(solution)/shard_map/dot_general | solution.py:929
  341.4 4.5 all-to-all-start.4
  346.0 4.6 shard_map.185
  357.5 1.7 shard_map.186
  359.4 5.4 %collective-permute-done.33.from_x = bf16[2,1,72,1024]{3,2,1,0:T(8,128)(2,1)} collective-permute-done((bf16[2,1,72,1024]{3,2,1,0:T(8,128)(2,1)}, bf16[2,1,72,1024]{3,2,1,0:T(8,128)(2,1)}, u32[]{:S(2)}, u32[]{:S(2)}) %collective-permute-start.33) | collective-permute-done | bytes 294944 | tf_op jit(solution)/shard_map/ppermute | solution.py:177
  364.7 4.2 collective-permute-done.34.from_y
  371.7 4.0 shard_map.187
  383.1 12.8 %collective-permute-done.41 = f32[18,128]{1,0:T(8,128)S(1)} collective-permute-done((f32[18,128]{1,0:T(8,128)S(1)}, f32[18,128]{1,0:T(8,128)S(1)}, u32[]{:S(2)}, u32[]{:S(2)}) %collective-permute-start.41) | collective-permute-done | bytes 9248 | tf_op jit(solution)/shard_map/ppermute | solution.py:177
  397.3 3.5 shard_map.189
  400.8 4.5 all-to-all-start.5
  409.3 3.0 collective-permute-start.45
  414.5 8.1 %collective-permute-done.48 = bf16[256,1152]{1,0:T(8,128)(2,1)} collective-permute-done((bf16[256,1152]{1,0:T(8,128)(2,1)}, bf16[256,1152]{1,0:T(8,128)(2,1)}, u32[]{:S(2)}, u32[]{:S(2)}) %collective-permute-start.48) | collective-permute-done | bytes 589856 | tf_op jit(solution)/shard_map/ppermute | solution.py:177
  424.1 6.4 %collective-permute-start.46 = (f32[18,128]{1,0:T(8,128)S(1)}, f32[18,128]{1,0:T(8,128)S(1)}, u32[]{:S(2)}, u32[]{:S(2)}) collective-permute-start(f32[18,128]{1,0:T(8,128)S(1)} %add.169), channel_id=1, source_target_pairs={{0,2},{1,3},{2,0},{3,1},{4,6},{5,7},{6,4},{7,5},{8,10},{9,11},{10,... | collective-permute-start | bytes 27656 | tf_op jit(solution)/shard_map/ppermute | solution.py:177
  431.4 6.7 %collective-permute-done.46 = f32[18,128]{1,0:T(8,128)S(1)} collective-permute-done((f32[18,128]{1,0:T(8,128)S(1)}, f32[18,128]{1,0:T(8,128)S(1)}, u32[]{:S(2)}, u32[]{:S(2)}) %collective-permute-start.46) | collective-permute-done | bytes 9248 | tf_op jit(solution)/shard_map/ppermute | solution.py:177
  438.1 1.6 reduce_sum.25.refs_0_
  441.2 1.9 collective-permute-start.55
  443.1 1.6 collective-permute-start.53
  445.4 3.1 collective-permute-start.54
  448.4 5.7 %collective-permute-done.53.refs_3_ = bf16[72,1024]{1,0:T(8,128)(2,1)S(1)} collective-permute-done((bf16[72,1024]{1,0:T(8,128)(2,1)S(1)}, bf16[72,1024]{1,0:T(8,128)(2,1)S(1)}, u32[]{:S(2)}, u32[]{:S(2)}) %collective-permute-start.53) | collective-permute-done | bytes 147488 | tf_op jit(solution)/shard_map/ppermute | solution.py:177
  455.3 3.5 maximum_select_fusion.2
  463.7 2.9 collective-permute-start.60
  466.6 1.7 collective-permute-done.60
  473.7 2.3 shard_map.194
  475.9 2.3 shard_map.195
  478.3 3.0 shard_map.196
  (401 shorter events, 120.0 us)
Async XLA Ops:
  4.5 6.9 %collective-permute-start = (bf16[144,1792]{1,0:T(8,128)(2,1)S(1)}, bf16[144,1792]{1,0:T(8,128)(2,1)S(1)}, u32[]{:S(2)}, u32[]{:S(2)}) collective-permute-start(bf16[144,1792]{1,0:T(8,128)(2,1)S(1)} %get-tuple-element.234), channel_id=1, source_target_pairs={{0,4},{1,5},{2,6},{3,7},{4,0},{5,1},{6,2},{7,3},{8,12},{9,13},{10,... | collective-permute-start | bytes 1548296 | tf_op jit(solution)/shard_map/ppermute | solution.py:177
  7.4 17.1 %collective-permute-start.2 = (bf16[256,1152]{1,0:T(8,128)(2,1)}, bf16[256,1152]{1,0:T(8,128)(2,1)}, u32[]{:S(2)}, u32[]{:S(2)}) collective-permute-start(bf16[256,1152]{1,0:T(8,128)(2,1)} %get-tuple-element.497), channel_id=1, source_target_pairs={{0,1},{1,0},{2,5},{3,4},{4,3},{5,2},{6,7},{7,6},{8,9},{9,8},{10,13... | collective-permute-start | bytes 1769480 | tf_op jit(solution)/shard_map/ppermute | solution.py:177
  9.9 14.6 %collective-permute-start.1 = (bf16[256,1152]{1,0:T(8,128)(2,1)}, bf16[256,1152]{1,0:T(8,128)(2,1)}, u32[]{:S(2)}, u32[]{:S(2)}) collective-permute-start(bf16[256,1152]{1,0:T(8,128)(2,1)} %get-tuple-element.246), channel_id=1, source_target_pairs={{2,4},{3,5},{4,2},{5,3},{10,12},{11,13},{12,10},{13,11},{18,20},{1... | collective-permute-start | bytes 1769480 | tf_op jit(solution)/shard_map/ppermute | solution.py:177
  14.1 30.8 %all-to-all-start = ((bf16[4,72,1792]{2,1,0:T(8,128)(2,1)}), bf16[4,72,1792]{2,1,0:T(8,128)(2,1)S(1)}, u32[]{:S(2)}, u32[]{:S(2)}) async-start(bf16[4,72,1792]{2,1,0:T(8,128)(2,1)} %broadcast_in_dim.50), calls=%async_computation | async-start | bytes 2064384 | tf_op jit(solution)/shard_map/all_to_all | solution.py:195
  47.5 49.8 %all-to-all-start.1 = ((bf16[4,72,2816]{2,1,0:T(8,128)(2,1)}), bf16[4,72,2816]{2,1,0:T(8,128)(2,1)}, u32[]{:S(2)}, u32[]{:S(2)}) async-start(bf16[4,72,2816]{2,1,0:T(8,128)(2,1)} %broadcast_in_dim.52), calls=%async_computation.1 | async-start | bytes 3244032 | tf_op jit(solution)/shard_map/all_to_all | solution.py:195
  54.3 23.0 %collective-permute-start.6 = (bf16[512,1152]{1,0:T(8,128)(2,1)S(1)}, bf16[512,1152]{1,0:T(8,128)(2,1)}, u32[]{:S(2)}, u32[]{:S(2)}) collective-permute-start(bf16[512,1152]{1,0:T(8,128)(2,1)S(1)} %pad_maximum_fusion.1.half), channel_id=1, source_target_pairs={{0,4},{1,5},{2,6},{3,7},{4,0},{5,1},{6,2},{7,3},{8,12},{9,13},{10,... | collective-permute-start | bytes 3538952 | tf_op jit(solution)/shard_map/ppermute | solution.py:177
  56.1 19.6 %collective-permute-start.5 = (bf16[3,72,1792]{2,1,0:T(8,128)(2,1)}, bf16[3,72,1792]{2,1,0:T(8,128)(2,1)}, u32[]{:S(2)}, u32[]{:S(2)}) collective-permute-start(bf16[3,72,1792]{2,1,0:T(8,128)(2,1)} %pad_maximum_fusion.4.own), channel_id=1, source_target_pairs={{0,2},{1,3},{2,0},{3,1},{4,6},{5,7},{6,4},{7,5},{8,10},{9,11},{10,... | collective-permute-start | bytes 2322440 | tf_op jit(solution)/shard_map/ppermute | solution.py:177
  56.9 20.4 %collective-permute-start.4 = (bf16[3,72,1792]{2,1,0:T(8,128)(2,1)}, bf16[3,72,1792]{2,1,0:T(8,128)(2,1)}, u32[]{:S(2)}, u32[]{:S(2)}) collective-permute-start(bf16[3,72,1792]{2,1,0:T(8,128)(2,1)} %pad_maximum_fusion.4.own), channel_id=1, source_target_pairs={{0,1},{1,0},{2,3},{3,2},{4,5},{5,4},{6,7},{7,6},{8,9},{9,8},{10,11... | collective-permute-start | bytes 2322440 | tf_op jit(solution)/shard_map/ppermute | solution.py:177
  59.0 5.4 %collective-permute-start.7 = (bf16[144,2176]{1,0:T(8,128)(2,1)}, bf16[144,2176]{1,0:T(8,128)(2,1)}, u32[]{:S(2)}, u32[]{:S(2)}) collective-permute-start(bf16[144,2176]{1,0:T(8,128)(2,1)} %get-tuple-element.485), channel_id=1, source_target_pairs={{0,4},{1,5},{2,6},{3,7},{4,0},{5,1},{6,2},{7,3},{8,12},{9,13},{10,... | collective-permute-start | bytes 1880072 | tf_op jit(solution)/shard_map/ppermute | solution.py:177
  60.9 29.1 %collective-permute-start.11 = (bf16[256,1152]{1,0:T(8,128)(2,1)}, bf16[256,1152]{1,0:T(8,128)(2,1)}, u32[]{:S(2)}, u32[]{:S(2)}) collective-permute-start(bf16[256,1152]{1,0:T(8,128)(2,1)} %get-tuple-element.259), channel_id=1, source_target_pairs={{0,1},{1,0},{2,5},{3,4},{4,3},{5,2},{6,7},{7,6},{8,9},{9,8},{10,13... | collective-permute-start | bytes 1769480 | tf_op jit(solution)/shard_map/ppermute | solution.py:177
  64.4 25.6 %collective-permute-start.10 = (bf16[256,1152]{1,0:T(8,128)(2,1)}, bf16[256,1152]{1,0:T(8,128)(2,1)S(1)}, u32[]{:S(2)}, u32[]{:S(2)}) collective-permute-start(bf16[256,1152]{1,0:T(8,128)(2,1)} %get-tuple-element.263), channel_id=1, source_target_pairs={{2,4},{3,5},{4,2},{5,3},{10,12},{11,13},{12,10},{13,11},{18,20},{1... | collective-permute-start | bytes 1769480 | tf_op jit(solution)/shard_map/ppermute | solution.py:177
  79.4 17.9 %collective-permute-start.8 = (bf16[3,72,896]{2,1,0:T(8,128)(2,1)S(1)}, bf16[3,72,896]{2,1,0:T(8,128)(2,1)S(1)}, u32[]{:S(2)}, u32[]{:S(2)}) collective-permute-start(bf16[3,72,896]{2,1,0:T(8,128)(2,1)S(1)} %slice.126), channel_id=1, source_target_pairs={{0,1},{1,0},{2,3},{3,2},{4,5},{5,4},{6,7},{7,6},{8,9},{9,8},{10,11... | collective-permute-start | bytes 1161224 | tf_op jit(solution)/shard_map/ppermute | solution.py:177
  80.0 17.3 %collective-permute-start.9 = (bf16[3,72,896]{2,1,0:T(8,128)(2,1)S(1)}, bf16[3,72,896]{2,1,0:T(8,128)(2,1)S(1)}, u32[]{:S(2)}, u32[]{:S(2)}) collective-permute-start(bf16[3,72,896]{2,1,0:T(8,128)(2,1)S(1)} %slice.127), channel_id=1, source_target_pairs={{0,2},{1,3},{2,0},{3,1},{4,6},{5,7},{6,4},{7,5},{8,10},{9,11},{10,... | collective-permute-start | bytes 1161224 | tf_op jit(solution)/shard_map/ppermute | solution.py:177
  100.2 29.7 %collective-permute-start.14 = (bf16[3,72,2816]{2,1,0:T(8,128)(2,1)S(1)}, bf16[3,72,2816]{2,1,0:T(8,128)(2,1)}, u32[]{:S(2)}, u32[]{:S(2)}) collective-permute-start(bf16[3,72,2816]{2,1,0:T(8,128)(2,1)S(1)} %pad_maximum_fusion.own), channel_id=1, source_target_pairs={{0,2},{1,3},{2,0},{3,1},{4,6},{5,7},{6,4},{7,5},{8,10},{9,11},{10,... | collective-permute-start | bytes 3649544 | tf_op jit(solution)/shard_map/ppermute | solution.py:177
  101.2 28.7 %collective-permute-start.13 = (bf16[3,72,2816]{2,1,0:T(8,128)(2,1)S(1)}, bf16[3,72,2816]{2,1,0:T(8,128)(2,1)}, u32[]{:S(2)}, u32[]{:S(2)}) collective-permute-start(bf16[3,72,2816]{2,1,0:T(8,128)(2,1)S(1)} %pad_maximum_fusion.own), channel_id=1, source_target_pairs={{0,1},{1,0},{2,3},{3,2},{4,5},{5,4},{6,7},{7,6},{8,9},{9,8},{10,11... | collective-permute-start | bytes 3649544 | tf_op jit(solution)/shard_map/ppermute | solution.py:177
  104.0 25.9 %collective-permute-start.15 = (bf16[512,1152]{1,0:T(8,128)(2,1)}, bf16[512,1152]{1,0:T(8,128)(2,1)}, u32[]{:S(2)}, u32[]{:S(2)}) collective-permute-start(bf16[512,1152]{1,0:T(8,128)(2,1)} %pad_maximum_fusion.2), channel_id=1, source_target_pairs={{0,4},{1,5},{2,6},{3,7},{4,0},{5,1},{6,2},{7,3},{8,12},{9,13},{10,... | collective-permute-start | bytes 3538952 | tf_op jit(solution)/shard_map/ppermute | solution.py:177
  104.0 50.5 %all-to-all-start.2 = ((bf16[4,72,2176]{2,1,0:T(8,128)(2,1)}), bf16[4,72,2176]{2,1,0:T(8,128)(2,1)}, u32[]{:S(2)}, u32[]{:S(2)}) async-start(bf16[4,72,2176]{2,1,0:T(8,128)(2,1)} %broadcast_in_dim.54), calls=%async_computation.2 | async-start | bytes 2506752 | tf_op jit(solution)/shard_map/all_to_all | solution.py:195
  129.9 30.0 %collective-permute-start.16 = (bf16[3,72,2816]{2,1,0:T(8,128)(2,1)S(1)}, bf16[3,72,2816]{2,1,0:T(8,128)(2,1)}, u32[]{:S(2)}, u32[]{:S(2)}) collective-permute-start(bf16[3,72,2816]{2,1,0:T(8,128)(2,1)S(1)} %pad_maximum_fusion.own), channel_id=1, source_target_pairs={{0,3},{1,2},{2,1},{3,0},{4,7},{5,6},{6,5},{7,4},{8,11},{9,10},{10,... | collective-permute-start | bytes 3649544 | tf_op jit(solution)/shard_map/ppermute | solution.py:177
  159.9 15.7 %collective-permute-start.19 = (bf16[1024,640]{1,0:T(8,128)(2,1)}, bf16[1024,640]{1,0:T(8,128)(2,1)}, u32[]{:S(2)}, u32[]{:S(2)}) collective-permute-start(bf16[1024,640]{1,0:T(8,128)(2,1)} %copy-done.4), channel_id=1, source_target_pairs={{0,4},{1,5},{2,6},{3,7},{4,0},{5,1},{6,2},{7,3},{8,12},{9,13},{10,... | collective-permute-start | bytes 3932168 | tf_op jit(solution)/shard_map/ppermute | solution.py:177
  163.0 12.6 %collective-permute-start.20 = (bf16[1152,640]{1,0:T(8,128)(2,1)}, bf16[1152,640]{1,0:T(8,128)(2,1)}, u32[]{:S(2)}, u32[]{:S(2)}) collective-permute-start(bf16[1152,640]{1,0:T(8,128)(2,1)} %bitcast.31.w_mine), channel_id=1, source_target_pairs={{0,4},{1,5},{2,6},{3,7},{4,0},{5,1},{6,2},{7,3},{8,12},{9,13},{10,... | collective-permute-start | bytes 4423688 | tf_op jit(solution)/shard_map/ppermute | solution.py:177
  165.8 23.1 %collective-permute-start.18 = (bf16[3,72,2176]{2,1,0:T(8,128)(2,1)}, bf16[3,72,2176]{2,1,0:T(8,128)(2,1)}, u32[]{:S(2)}, u32[]{:S(2)}) collective-permute-start(bf16[3,72,2176]{2,1,0:T(8,128)(2,1)} %pad_maximum_fusion.3.own), channel_id=1, source_target_pairs={{0,2},{1,3},{2,0},{3,1},{4,6},{5,7},{6,4},{7,5},{8,10},{9,11},{10,... | collective-permute-start | bytes 2820104 | tf_op jit(solution)/shard_map/ppermute | solution.py:177
  167.1 22.8 %collective-permute-start.17 = (bf16[3,72,2176]{2,1,0:T(8,128)(2,1)}, bf16[3,72,2176]{2,1,0:T(8,128)(2,1)}, u32[]{:S(2)}, u32[]{:S(2)}) collective-permute-start(bf16[3,72,2176]{2,1,0:T(8,128)(2,1)} %pad_maximum_fusion.3.own), channel_id=1, source_target_pairs={{0,1},{1,0},{2,3},{3,2},{4,5},{5,4},{6,7},{7,6},{8,9},{9,8},{10,11... | collective-permute-start | bytes 2820104 | tf_op jit(solution)/shard_map/ppermute | solution.py:177
  191.3 14.1 %collective-permute-start.21 = (bf16[3,72,1024]{2,1,0:T(8,128)(2,1)S(1)}, bf16[3,72,1024]{2,1,0:T(8,128)(2,1)S(1)}, u32[]{:S(2)}, u32[]{:S(2)}) collective-permute-start(bf16[3,72,1024]{2,1,0:T(8,128)(2,1)S(1)} %slice.128), channel_id=1, source_target_pairs={{0,1},{1,0},{2,3},{3,2},{4,5},{5,4},{6,7},{7,6},{8,9},{9,8},{10,11... | collective-permute-start | bytes 1327112 | tf_op jit(solution)/shard_map/ppermute | solution.py:177
  193.6 12.2 %collective-permute-start.22 = (bf16[3,72,1152]{2,1,0:T(8,128)(2,1)S(1)}, bf16[3,72,1152]{2,1,0:T(8,128)(2,1)S(1)}, u32[]{:S(2)}, u32[]{:S(2)}) collective-permute-start(bf16[3,72,1152]{2,1,0:T(8,128)(2,1)S(1)} %slice.129), channel_id=1, source_target_pairs={{0,2},{1,3},{2,0},{3,1},{4,6},{5,7},{6,4},{7,5},{8,10},{9,11},{10,... | collective-permute-start | bytes 1493000 | tf_op jit(solution)/shard_map/ppermute | solution.py:177
  213.4 114.6 %all-to-all-start.3 = ((bf16[4,288,2176]{2,1,0:T(8,128)(2,1)}), bf16[4,288,2176]{2,1,0:T(8,128)(2,1)}, u32[]{:S(2)}, u32[]{:S(2)}) async-start(bf16[4,288,2176]{2,1,0:T(8,128)(2,1)} %bitcast.101), calls=%async_computation.3 | async-start | bytes 10027008 | tf_op jit(solution)/shard_map/all_to_all | solution.py:195
  237.8 19.8 %collective-permute-start.23 = (bf16[1024,1152]{1,0:T(8,128)(2,1)}, bf16[1024,1152]{1,0:T(8,128)(2,1)}, u32[]{:S(2)}, u32[]{:S(2)}) collective-permute-start(bf16[1024,1152]{1,0:T(8,128)(2,1)} %convolution_convert_fusion.2.part), channel_id=1, source_target_pairs={{0,4},{1,5},{2,6},{3,7},{4,0},{5,1},{6,2},{7,3},{8,12},{9,13},{10,... | collective-permute-start | bytes 7077896 | tf_op jit(solution)/shard_map/ppermute | solution.py:177
  244.7 12.4 %collective-permute-start.24 = (bf16[512,1152]{1,0:T(8,128)(2,1)S(1)}, bf16[512,1152]{1,0:T(8,128)(2,1)S(1)}, u32[]{:S(2)}, u32[]{:S(2)}) collective-permute-start(bf16[512,1152]{1,0:T(8,128)(2,1)S(1)} %slice.162), channel_id=1, source_target_pairs={{0,4},{1,5},{2,6},{3,7},{4,0},{5,1},{6,2},{7,3},{8,12},{9,13},{10,... | collective-permute-start | bytes 3538952 | tf_op jit(solution)/shard_map/ppermute | solution.py:177
  257.6 43.5 %collective-permute-start.26 = (bf16[2,4,72,1152]{3,2,1,0:T(8,128)(2,1)}, bf16[2,4,72,1152]{3,2,1,0:T(8,128)(2,1)S(1)}, u32[]{:S(2)}, u32[]{:S(2)}) collective-permute-start(bf16[2,4,72,1152]{3,2,1,0:T(8,128)(2,1)} %get-tuple-element.319), channel_id=1, source_target_pairs={{0,2},{1,3},{2,0},{3,1},{4,6},{5,7},{6,4},{7,5},{8,10},{9,11},{10,... | collective-permute-start | bytes 3981320 | tf_op jit(solution)/shard_map/ppermute | solution.py:177
  258.6 42.5 %collective-permute-start.25 = (bf16[2,4,72,1024]{3,2,1,0:T(8,128)(2,1)}, bf16[2,4,72,1024]{3,2,1,0:T(8,128)(2,1)S(1)}, u32[]{:S(2)}, u32[]{:S(2)}) collective-permute-start(bf16[2,4,72,1024]{3,2,1,0:T(8,128)(2,1)} %get-tuple-element.318), channel_id=1, source_target_pairs={{0,1},{1,0},{2,3},{3,2},{4,5},{5,4},{6,7},{7,6},{8,9},{9,8},{10,11... | collective-permute-start | bytes 3538952 | tf_op jit(solution)/shard_map/ppermute | solution.py:177
  260.4 40.7 %collective-permute-start.28 = (bf16[256,1152]{1,0:T(8,128)(2,1)}, bf16[256,1152]{1,0:T(8,128)(2,1)}, u32[]{:S(2)}, u32[]{:S(2)}) collective-permute-start(bf16[256,1152]{1,0:T(8,128)(2,1)} %get-tuple-element.493), channel_id=1, source_target_pairs={{0,1},{1,0},{2,5},{3,4},{4,3},{5,2},{6,7},{7,6},{8,9},{9,8},{10,13... | collective-permute-start | bytes 1769480 | tf_op jit(solution)/shard_map/ppermute | solution.py:177
  261.6 39.6 %collective-permute-start.27 = (bf16[256,1152]{1,0:T(8,128)(2,1)S(1)}, bf16[256,1152]{1,0:T(8,128)(2,1)}, u32[]{:S(2)}, u32[]{:S(2)}) collective-permute-start(bf16[256,1152]{1,0:T(8,128)(2,1)S(1)} %get-tuple-element.407), channel_id=1, source_target_pairs={{2,4},{3,5},{4,2},{5,3},{10,12},{11,13},{12,10},{13,11},{18,20},{1... | collective-permute-start | bytes 1769480 | tf_op jit(solution)/shard_map/ppermute | solution.py:177
  303.1 19.3 %collective-permute-start.30 = (bf16[4,72,1152]{2,1,0:T(8,128)(2,1)S(1)}, bf16[4,72,1152]{2,1,0:T(8,128)(2,1)S(1)}, u32[]{:S(2)}, u32[]{:S(2)}) collective-permute-start(bf16[4,72,1152]{2,1,0:T(8,128)(2,1)S(1)} %get-tuple-element.335), channel_id=1, source_target_pairs={{0,1},{1,0},{2,3},{3,2},{4,5},{5,4},{6,7},{7,6},{8,9},{9,8},{10,11... | collective-permute-start | bytes 1990664 | tf_op jit(solution)/shard_map/ppermute | solution.py:177
  304.0 17.5 %collective-permute-start.29 = (bf16[4,72,1024]{2,1,0:T(8,128)(2,1)S(1)}, bf16[4,72,1024]{2,1,0:T(8,128)(2,1)S(1)}, u32[]{:S(2)}, u32[]{:S(2)}) collective-permute-start(bf16[4,72,1024]{2,1,0:T(8,128)(2,1)S(1)} %get-tuple-element.334), channel_id=1, source_target_pairs={{0,2},{1,3},{2,0},{3,1},{4,6},{5,7},{6,4},{7,5},{8,10},{9,11},{10,... | collective-permute-start | bytes 1769480 | tf_op jit(solution)/shard_map/ppermute | solution.py:177
  328.0 40.9 %collective-permute-start.31 = (bf16[2,4,72,1152]{3,2,1,0:T(8,128)(2,1)}, bf16[2,4,72,1152]{3,2,1,0:T(8,128)(2,1)}, u32[]{:S(2)}, u32[]{:S(2)}) collective-permute-start(bf16[2,4,72,1152]{3,2,1,0:T(8,128)(2,1)} %get-tuple-element.352), channel_id=1, source_target_pairs={{0,1},{1,0},{2,3},{3,2},{4,5},{5,4},{6,7},{7,6},{8,9},{9,8},{10,11... | collective-permute-start | bytes 3981320 | tf_op jit(solution)/shard_map/ppermute | solution.py:177
  328.6 40.4 %collective-permute-start.32 = (bf16[2,4,72,1280]{3,2,1,0:T(8,128)(2,1)}, bf16[2,4,72,1280]{3,2,1,0:T(8,128)(2,1)}, u32[]{:S(2)}, u32[]{:S(2)}) collective-permute-start(bf16[2,4,72,1280]{3,2,1,0:T(8,128)(2,1)} %get-tuple-element.353), channel_id=1, source_target_pairs={{0,2},{1,3},{2,0},{3,1},{4,6},{5,7},{6,4},{7,5},{8,10},{9,11},{10,... | collective-permute-start | bytes 4423688 | tf_op jit(solution)/shard_map/ppermute | solution.py:177
  339.3 15.0 %collective-permute-start.35 = (bf16[512,1152]{1,0:T(8,128)(2,1)}, bf16[512,1152]{1,0:T(8,128)(2,1)S(1)}, u32[]{:S(2)}, u32[]{:S(2)}) collective-permute-start(bf16[512,1152]{1,0:T(8,128)(2,1)} %slice.164), channel_id=1, source_target_pairs={{0,4},{1,5},{2,6},{3,7},{4,0},{5,1},{6,2},{7,3},{8,12},{9,13},{10,... | collective-permute-start | bytes 3538952 | tf_op jit(solution)/shard_map/ppermute | solution.py:177
  341.4 55.9 %all-to-all-start.4 = ((bf16[4,72,2176]{2,1,0:T(8,128)(2,1)}), bf16[4,72,2176]{2,1,0:T(8,128)(2,1)}, u32[]{:S(2)}, u32[]{:S(2)}) async-start(bf16[4,72,2176]{2,1,0:T(8,128)(2,1)} %copy-done.8), calls=%async_computation.4 | async-start | bytes 2506752 | tf_op jit(solution)/shard_map/all_to_all | solution.py:195
  352.0 17.0 %collective-permute-start.34 = (bf16[2,1,72,1152]{3,2,1,0:T(8,128)(2,1)}, bf16[2,1,72,1152]{3,2,1,0:T(8,128)(2,1)}, u32[]{:S(2)}, u32[]{:S(2)}) collective-permute-start(bf16[2,1,72,1152]{3,2,1,0:T(8,128)(2,1)} %get-tuple-element.358), channel_id=1, source_target_pairs={{0,2},{1,3},{2,0},{3,1},{4,6},{5,7},{6,4},{7,5},{8,10},{9,11},{10,... | collective-permute-start | bytes 995336 | tf_op jit(solution)/shard_map/ppermute | solution.py:177
  352.7 12.0 %collective-permute-start.33 = (bf16[2,1,72,1024]{3,2,1,0:T(8,128)(2,1)}, bf16[2,1,72,1024]{3,2,1,0:T(8,128)(2,1)}, u32[]{:S(2)}, u32[]{:S(2)}) collective-permute-start(bf16[2,1,72,1024]{3,2,1,0:T(8,128)(2,1)} %get-tuple-element.357), channel_id=1, source_target_pairs={{0,1},{1,0},{2,3},{3,2},{4,5},{5,4},{6,7},{7,6},{8,9},{9,8},{10,11... | collective-permute-start | bytes 884744 | tf_op jit(solution)/shard_map/ppermute | solution.py:177
  359.3 9.7 %collective-permute-start.36 = (f32[18,128]{1,0:T(8,128)S(1)}, f32[18,128]{1,0:T(8,128)S(1)}, u32[]{:S(2)}, u32[]{:S(2)}) collective-permute-start(f32[18,128]{1,0:T(8,128)S(1)} %reshape.153), channel_id=1, source_target_pairs={{0,4},{1,5},{2,6},{3,7},{4,0},{5,1},{6,2},{7,3},{8,12},{9,13},{10,... | collective-permute-start | bytes 27656 | tf_op jit(solution)/shard_map/ppermute | solution.py:177
  375.7 21.6 %collective-permute-start.38 = (bf16[4,72,1280]{2,1,0:T(8,128)(2,1)}, bf16[4,72,1280]{2,1,0:T(8,128)(2,1)S(1)}, u32[]{:S(2)}, u32[]{:S(2)}) collective-permute-start(bf16[4,72,1280]{2,1,0:T(8,128)(2,1)} %get-tuple-element.372), channel_id=1, source_target_pairs={{0,1},{1,0},{2,3},{3,2},{4,5},{5,4},{6,7},{7,6},{8,9},{9,8},{10,11... | collective-permute-start | bytes 2211848 | tf_op jit(solution)/shard_map/ppermute | solution.py:177
  377.2 20.1 %collective-permute-start.37 = (bf16[4,72,1152]{2,1,0:T(8,128)(2,1)}, bf16[4,72,1152]{2,1,0:T(8,128)(2,1)}, u32[]{:S(2)}, u32[]{:S(2)}) collective-permute-start(bf16[4,72,1152]{2,1,0:T(8,128)(2,1)} %get-tuple-element.371), channel_id=1, source_target_pairs={{0,2},{1,3},{2,0},{3,1},{4,6},{5,7},{6,4},{7,5},{8,10},{9,11},{10,... | collective-permute-start | bytes 1990664 | tf_op jit(solution)/shard_map/ppermute | solution.py:177
  380.4 16.3 %collective-permute-start.40 = (bf16[1,72,1152]{2,1,0:T(8,128)(2,1)S(1)}, bf16[1,72,1152]{2,1,0:T(8,128)(2,1)S(1)}, u32[]{:S(2)}, u32[]{:S(2)}) collective-permute-start(bf16[1,72,1152]{2,1,0:T(8,128)(2,1)S(1)} %get-tuple-element.380), channel_id=1, source_target_pairs={{0,1},{1,0},{2,3},{3,2},{4,5},{5,4},{6,7},{7,6},{8,9},{9,8},{10,11... | collective-permute-start | bytes 497672 | tf_op jit(solution)/shard_map/ppermute | solution.py:177
  380.9 15.1 %collective-permute-start.39 = (bf16[1,72,1024]{2,1,0:T(8,128)(2,1)S(1)}, bf16[1,72,1024]{2,1,0:T(8,128)(2,1)S(1)}, u32[]{:S(2)}, u32[]{:S(2)}) collective-permute-start(bf16[1,72,1024]{2,1,0:T(8,128)(2,1)S(1)} %get-tuple-element.379), channel_id=1, source_target_pairs={{0,2},{1,3},{2,0},{3,1},{4,6},{5,7},{6,4},{7,5},{8,10},{9,11},{10,... | collective-permute-start | bytes 442376 | tf_op jit(solution)/shard_map/ppermute | solution.py:177
  381.6 14.3 %collective-permute-start.41 = (f32[18,128]{1,0:T(8,128)S(1)}, f32[18,128]{1,0:T(8,128)S(1)}, u32[]{:S(2)}, u32[]{:S(2)}) collective-permute-start(f32[18,128]{1,0:T(8,128)S(1)} %add.168), channel_id=1, source_target_pairs={{0,1},{1,0},{2,3},{3,2},{4,5},{5,4},{6,7},{7,6},{8,9},{9,8},{10,11... | collective-permute-start | bytes 27656 | tf_op jit(solution)/shard_map/ppermute | solution.py:177
  400.8 37.3 %all-to-all-start.5 = ((bf16[4,72,2432]{2,1,0:T(8,128)(2,1)}), bf16[4,72,2432]{2,1,0:T(8,128)(2,1)}, u32[]{:S(2)}, u32[]{:S(2)}) async-start(bf16[4,72,2432]{2,1,0:T(8,128)(2,1)} %shard_map.189), calls=%async_computation.5 | async-start | bytes 2801664 | tf_op jit(solution)/shard_map/all_to_all | solution.py:195
  406.2 16.4 %collective-permute-start.48 = (bf16[256,1152]{1,0:T(8,128)(2,1)}, bf16[256,1152]{1,0:T(8,128)(2,1)}, u32[]{:S(2)}, u32[]{:S(2)}) collective-permute-start(bf16[256,1152]{1,0:T(8,128)(2,1)} %get-tuple-element.491), channel_id=1, source_target_pairs={{0,1},{1,0},{2,5},{3,4},{4,3},{5,2},{6,7},{7,6},{8,9},{9,8},{10,13... | collective-permute-start | bytes 1769480 | tf_op jit(solution)/shard_map/ppermute | solution.py:177
  407.7 16.4 %collective-permute-start.47 = (bf16[256,1152]{1,0:T(8,128)(2,1)S(1)}, bf16[256,1152]{1,0:T(8,128)(2,1)}, u32[]{:S(2)}, u32[]{:S(2)}) collective-permute-start(bf16[256,1152]{1,0:T(8,128)(2,1)S(1)} %get-tuple-element.404), channel_id=1, source_target_pairs={{2,4},{3,5},{4,2},{5,3},{10,12},{11,13},{12,10},{13,11},{18,20},{1... | collective-permute-start | bytes 1769480 | tf_op jit(solution)/shard_map/ppermute | solution.py:177
  409.3 28.8 %collective-permute-start.45 = (bf16[72,2176]{1,0:T(8,128)(2,1)S(1)}, bf16[72,2176]{1,0:T(8,128)(2,1)S(1)}, u32[]{:S(2)}, u32[]{:S(2)}) collective-permute-start(bf16[72,2176]{1,0:T(8,128)(2,1)S(1)} %bitcast.97), channel_id=1, source_target_pairs={{0,2},{1,3},{2,0},{3,1},{4,6},{5,7},{6,4},{7,5},{8,10},{9,11},{10,... | collective-permute-start | bytes 940040 | tf_op jit(solution)/shard_map/ppermute | solution.py:177
  412.3 25.8 %collective-permute-start.44 = (bf16[72,2176]{1,0:T(8,128)(2,1)S(1)}, bf16[72,2176]{1,0:T(8,128)(2,1)S(1)}, u32[]{:S(2)}, u32[]{:S(2)}) collective-permute-start(bf16[72,2176]{1,0:T(8,128)(2,1)S(1)} %bitcast.98), channel_id=1, source_target_pairs={{0,1},{1,0},{2,3},{3,2},{4,5},{5,4},{6,7},{7,6},{8,9},{9,8},{10,11... | collective-permute-start | bytes 940040 | tf_op jit(solution)/shard_map/ppermute | solution.py:177
  414.3 23.8 %collective-permute-start.43 = (bf16[72,2176]{1,0:T(8,128)(2,1)S(1)}, bf16[72,2176]{1,0:T(8,128)(2,1)S(1)}, u32[]{:S(2)}, u32[]{:S(2)}) collective-permute-start(bf16[72,2176]{1,0:T(8,128)(2,1)S(1)} %reduce_sum.24.refs_0_), channel_id=1, source_target_pairs={{0,2},{1,3},{2,0},{3,1},{4,6},{5,7},{6,4},{7,5},{8,10},{9,11},{10,... | collective-permute-start | bytes 940040 | tf_op jit(solution)/shard_map/ppermute | solution.py:177
  422.6 15.5 %collective-permute-start.42 = (bf16[72,2176]{1,0:T(8,128)(2,1)S(1)}, bf16[72,2176]{1,0:T(8,128)(2,1)S(1)}, u32[]{:S(2)}, u32[]{:S(2)}) collective-permute-start(bf16[72,2176]{1,0:T(8,128)(2,1)S(1)} %reduce_sum.24.refs_0_), channel_id=1, source_target_pairs={{0,1},{1,0},{2,3},{3,2},{4,5},{5,4},{6,7},{7,6},{8,9},{9,8},{10,11... | collective-permute-start | bytes 940040 | tf_op jit(solution)/shard_map/ppermute | solution.py:177
  424.1 14.0 %collective-permute-start.46 = (f32[18,128]{1,0:T(8,128)S(1)}, f32[18,128]{1,0:T(8,128)S(1)}, u32[]{:S(2)}, u32[]{:S(2)}) collective-permute-start(f32[18,128]{1,0:T(8,128)S(1)} %add.169), channel_id=1, source_target_pairs={{0,2},{1,3},{2,0},{3,1},{4,6},{5,7},{6,4},{7,5},{8,10},{9,11},{10,... | collective-permute-start | bytes 27656 | tf_op jit(solution)/shard_map/ppermute | solution.py:177
  439.7 19.7 %collective-permute-start.52 = (bf16[72,2432]{1,0:T(8,128)(2,1)S(1)}, bf16[72,2432]{1,0:T(8,128)(2,1)S(1)}, u32[]{:S(2)}, u32[]{:S(2)}) collective-permute-start(bf16[72,2432]{1,0:T(8,128)(2,1)S(1)} %reduce_sum.25.refs_0_), channel_id=1, source_target_pairs={{0,2},{1,3},{2,0},{3,1},{4,6},{5,7},{6,4},{7,5},{8,10},{9,11},{10,... | collective-permute-start | bytes 1050632 | tf_op jit(solution)/shard_map/ppermute | solution.py:177
  439.8 19.6 %collective-permute-start.51 = (bf16[72,2432]{1,0:T(8,128)(2,1)S(1)}, bf16[72,2432]{1,0:T(8,128)(2,1)S(1)}, u32[]{:S(2)}, u32[]{:S(2)}) collective-permute-start(bf16[72,2432]{1,0:T(8,128)(2,1)S(1)} %reduce_sum.25.refs_0_), channel_id=1, source_target_pairs={{0,1},{1,0},{2,3},{3,2},{4,5},{5,4},{6,7},{7,6},{8,9},{9,8},{10,11... | collective-permute-start | bytes 1050632 | tf_op jit(solution)/shard_map/ppermute | solution.py:177
  443.1 10.9 %collective-permute-start.53 = (bf16[72,1024]{1,0:T(8,128)(2,1)S(1)}, bf16[72,1024]{1,0:T(8,128)(2,1)S(1)}, u32[]{:S(2)}, u32[]{:S(2)}) collective-permute-start(bf16[72,1024]{1,0:T(8,128)(2,1)S(1)} %slice.146), channel_id=1, source_target_pairs={{0,1},{1,0},{2,3},{3,2},{4,5},{5,4},{6,7},{7,6},{8,9},{9,8},{10,11... | collective-permute-start | bytes 442376 | tf_op jit(solution)/shard_map/ppermute | solution.py:177
  444.7 14.0 %collective-permute-start.49 = (bf16[72,1024]{1,0:T(8,128)(2,1)S(1)}, bf16[72,1024]{1,0:T(8,128)(2,1)S(1)}, u32[]{:S(2)}, u32[]{:S(2)}) collective-permute-start(bf16[72,1024]{1,0:T(8,128)(2,1)S(1)} %slice.144), channel_id=1, source_target_pairs={{0,1},{1,0},{2,3},{3,2},{4,5},{5,4},{6,7},{7,6},{8,9},{9,8},{10,11... | collective-permute-start | bytes 442376 | tf_op jit(solution)/shard_map/ppermute | solution.py:177
  445.4 13.4 %collective-permute-start.54 = (bf16[72,1152]{1,0:T(8,128)(2,1)S(1)}, bf16[72,1152]{1,0:T(8,128)(2,1)S(1)}, u32[]{:S(2)}, u32[]{:S(2)}) collective-permute-start(bf16[72,1152]{1,0:T(8,128)(2,1)S(1)} %slice.147), channel_id=1, source_target_pairs={{0,2},{1,3},{2,0},{3,1},{4,6},{5,7},{6,4},{7,5},{8,10},{9,11},{10,... | collective-permute-start | bytes 497672 | tf_op jit(solution)/shard_map/ppermute | solution.py:177
  454.1 5.3 %collective-permute-start.50 = (bf16[72,1152]{1,0:T(8,128)(2,1)S(1)}, bf16[72,1152]{1,0:T(8,128)(2,1)S(1)}, u32[]{:S(2)}, u32[]{:S(2)}) collective-permute-start(bf16[72,1152]{1,0:T(8,128)(2,1)S(1)} %slice.145), channel_id=1, source_target_pairs={{0,2},{1,3},{2,0},{3,1},{4,6},{5,7},{6,4},{7,5},{8,10},{9,11},{10,... | collective-permute-start | bytes 497672 | tf_op jit(solution)/shard_map/ppermute | solution.py:177
  460.1 8.5 %collective-permute-start.59 = (bf16[2,72,2176]{2,1,0:T(8,128)(2,1)S(1)}, bf16[2,72,2176]{2,1,0:T(8,128)(2,1)S(1)}, u32[]{:S(2)}, u32[]{:S(2)}) collective-permute-start(bf16[2,72,2176]{2,1,0:T(8,128)(2,1)S(1)} %shard_map.192), channel_id=1, source_target_pairs={{0,4},{1,5},{2,6},{3,7},{4,0},{5,1},{6,2},{7,3},{8,12},{9,13},{10,... | collective-permute-start | bytes 1880072 | tf_op jit(solution)/shard_map/ppermute | solution.py:177
  460.8 7.8 %collective-permute-start.56 = (bf16[2,72,2176]{2,1,0:T(8,128)(2,1)S(1)}, bf16[2,72,2176]{2,1,0:T(8,128)(2,1)S(1)}, u32[]{:S(2)}, u32[]{:S(2)}) collective-permute-start(bf16[2,72,2176]{2,1,0:T(8,128)(2,1)S(1)} %shard_map.191), channel_id=1, source_target_pairs={{0,4},{1,5},{2,6},{3,7},{4,0},{5,1},{6,2},{7,3},{8,12},{9,13},{10,... | collective-permute-start | bytes 1880072 | tf_op jit(solution)/shard_map/ppermute | solution.py:177
  461.4 7.2 %collective-permute-start.58 = (bf16[72,1280]{1,0:T(8,128)(2,1)S(1)}, bf16[72,1280]{1,0:T(8,128)(2,1)S(1)}, u32[]{:S(2)}, u32[]{:S(2)}) collective-permute-start(bf16[72,1280]{1,0:T(8,128)(2,1)S(1)} %slice.149), channel_id=1, source_target_pairs={{0,2},{1,3},{2,0},{3,1},{4,6},{5,7},{6,4},{7,5},{8,10},{9,11},{10,... | collective-permute-start | bytes 552968 | tf_op jit(solution)/shard_map/ppermute | solution.py:177
  462.6 6.0 %collective-permute-start.57 = (bf16[72,1152]{1,0:T(8,128)(2,1)S(1)}, bf16[72,1152]{1,0:T(8,128)(2,1)S(1)}, u32[]{:S(2)}, u32[]{:S(2)}) collective-permute-start(bf16[72,1152]{1,0:T(8,128)(2,1)S(1)} %slice.148), channel_id=1, source_target_pairs={{0,1},{1,0},{2,3},{3,2},{4,5},{5,4},{6,7},{7,6},{8,9},{9,8},{10,11... | collective-permute-start | bytes 497672 | tf_op jit(solution)/shard_map/ppermute | solution.py:177
  471.6 6.6 %collective-permute-start.61 = (bf16[2,72,2432]{2,1,0:T(8,128)(2,1)}, bf16[2,72,2432]{2,1,0:T(8,128)(2,1)}, u32[]{:S(2)}, u32[]{:S(2)}) collective-permute-start(bf16[2,72,2432]{2,1,0:T(8,128)(2,1)} %shard_map.193), channel_id=1, source_target_pairs={{0,4},{1,5},{2,6},{3,7},{4,0},{5,1},{6,2},{7,3},{8,12},{9,13},{10,... | collective-permute-start | bytes 2101256 | tf_op jit(solution)/shard_map/ppermute | solution.py:177
  (104 other events, 895.6 us)
